TPU v7x, 512 devices: a whole 4x8x8 slice. The times are simulated.
512 devices in a mesh: dp: 32 (over y, x), pipe: 16 (over z, core).
Axes of the slice: x: 4, y: 8, z: 8, core: 2. Of those that a mesh axis runs over, the one named last changes fastest.
Arguments:
- base_ids: int32 [32, 3, 64, 32], P('dp'), may hold values from 0 to 3
- embed_table: bfloat16 [128, 768], replicated, may hold values from -1 to 1
- segment_weights: bfloat16 [16, 768, 768], P('pipe'), may hold values from -0.21875 to 0.21875
- conv_taps: float32 [16, 3, 768], P('pipe'), may hold values from -3 to 3
- norm_gains: float32 [16, 768], P('pipe'), may hold values from 0.1 to 1.9
- cotangent: bfloat16 [32, 3, 64, 768], P('dp'), may hold values from -6 to 6
Outputs:
- weight_grads: float32 [16, 768, 768], P('pipe')
All inputs are finite; a program needn't handle non-finite values.
Results may differ from a plain program's by a relative error of at most 0.023.
Values may be sent and summed in bfloat16 or wider, within the bound.
No kernel may reach another device: no remote copies, remote signals or barrier semaphores. Data moves between devices by JAX's collectives and lax.ppermute only.
A program may use at most 64 MiB of HBM per device.

v0:
```python
import math

import jax
import jax.numpy as jnp
from jax import lax
from jax.sharding import PartitionSpec as P


def passed_along(block, axis, distance):
    devices = range(lax.axis_size(axis))
    route = [(i - distance, i) for i in devices if i - distance in devices]
    return lax.ppermute(block, axis, route)


def encode_bases(base_rows, embed_table):
    one_hot = (base_rows[:, :, None] == jnp.arange(4, dtype=jnp.int32)).astype(jnp.bfloat16)
    one_hot = one_hot.reshape(base_rows.shape[0], -1)
    return jnp.dot(one_hot, embed_table, preferred_element_type=jnp.float32).astype(jnp.bfloat16)


def section_parts(segment_input, skip_input, tap_rows, gain_row):
    inner_sum = segment_input.astype(jnp.float32) + skip_input.astype(jnp.float32)
    inv_rms = lax.rsqrt(jnp.mean(inner_sum * inner_sum, axis=-1, keepdims=True) + 1e-06)
    normed = inner_sum * inv_rms * gain_row
    padded = jnp.pad(normed, ((1, 1), (0, 0)))
    mixed = tap_rows[0] * padded[:-2] + tap_rows[1] * padded[1:-1] + tap_rows[2] * padded[2:]
    return (inner_sum, jax.nn.gelu(mixed))


def section_forward(segment_input, skip_input, weight, tap_rows, gain_row):
    inner_sum, act_full = section_parts(segment_input, skip_input, tap_rows, gain_row)
    product = jnp.dot(act_full.astype(jnp.bfloat16), weight, preferred_element_type=jnp.float32)
    return (inner_sum + product).astype(jnp.bfloat16)


def section_back(segment_input, skip_input, weight, tap_rows, gain_row, upstream):
    upstream_bf = upstream.astype(jnp.bfloat16)
    primal, pullback = jax.vjp(
        lambda first_in, second_in: section_parts(first_in, second_in, tap_rows, gain_row),
        segment_input,
        skip_input,
    )
    act_bf = primal[1].astype(jnp.bfloat16)
    weight_term = lax.dot_general(
        act_bf, upstream_bf, (((0,), (0,)), ((), ())), preferred_element_type=jnp.float32
    )
    act_grad = lax.dot_general(
        upstream_bf, weight, (((1,), (1,)), ((), ())), preferred_element_type=jnp.float32
    )
    input_grad, skip_grad = pullback((upstream, act_grad))
    return (input_grad, skip_grad, weight_term)


def store_slot(buffer, value, slot_index, is_valid):
    kept = jnp.where(is_valid, value, buffer[slot_index])
    return lax.dynamic_update_index_in_dim(buffer, kept, slot_index, 0)


def shards(base_ids, embed_table, segment_weights, conv_taps, norm_gains, cotangent):
    segments = lax.axis_size("pipe")
    quarter = segments // 4
    position = lax.axis_index("pipe")
    weight = segment_weights[0]
    tap_rows = conv_taps[0]
    gain_row = norm_gains[0]
    micro_count = base_ids.shape[1]
    row_count = base_ids.shape[2]
    channels = weight.shape[1]
    steps_total = segments + micro_count - 1
    split_step = quarter + micro_count - 1
    zero_rows = jnp.zeros((row_count, channels), jnp.bfloat16)
    zero_buffer = jnp.zeros((micro_count, row_count, channels), jnp.bfloat16)

    def forward_step(time_step, loop_state):
        arrived, stored_inputs, towers, skip_maps = loop_state
        micro_index = time_step - position
        active = (micro_index >= 0) & (micro_index < micro_count)
        slot_index = jnp.clip(micro_index, 0, micro_count - 1)

        def forward_compute(operands):
            arrived_in, skips_in = operands
            encoded = encode_bases(base_ids[0, slot_index], embed_table)
            segment_input = jnp.where(position == 0, encoded, arrived_in)
            output = section_forward(
                segment_input, skips_in[slot_index], weight, tap_rows, gain_row
            )
            return (segment_input, output)

        def forward_passthrough(operands):
            return (zero_rows, zero_rows)

        segment_input, output = lax.cond(
            active, forward_compute, forward_passthrough, (arrived, skip_maps)
        )
        stored_inputs = store_slot(stored_inputs, segment_input, slot_index, active)
        towers = store_slot(towers, output, slot_index, active)
        landed = passed_along(output, "pipe", 3 * quarter)
        source = time_step - (position - 3 * quarter)
        is_valid = (position >= 3 * quarter) & (source >= 0) & (source < micro_count)
        skip_maps = store_slot(skip_maps, landed, jnp.clip(source, 0, micro_count - 1), is_valid)
        arrived = passed_along(output, "pipe", 1)
        return (arrived, stored_inputs, towers, skip_maps)

    loop_state = (zero_rows, zero_buffer, zero_buffer, zero_buffer)
    loop_state = lax.fori_loop(0, split_step, forward_step, loop_state)
    loop_state = lax.fori_loop(split_step, steps_total, forward_step, loop_state)
    stored_inputs = loop_state[1]
    skip_maps = loop_state[3]

    def backward_step(time_step, loop_state):
        arrived, returned, skip_grads, accumulated = loop_state
        micro_index = time_step - (segments - 1 - position)
        active = (micro_index >= 0) & (micro_index < micro_count)
        slot_index = jnp.clip(micro_index, 0, micro_count - 1)

        def backward_compute(operands):
            arrived_in, returned_in, accum_in = operands
            from_next = jnp.where(
                position == segments - 1,
                cotangent[0, slot_index].astype(jnp.float32),
                arrived_in.astype(jnp.float32),
            )
            upstream = from_next + returned_in[slot_index].astype(jnp.float32)
            input_grad, skip_grad, weight_term = section_back(
                stored_inputs[slot_index],
                skip_maps[slot_index],
                weight,
                tap_rows,
                gain_row,
                upstream,
            )
            return (input_grad, skip_grad, accum_in + weight_term)

        def backward_passthrough(operands):
            return (zero_rows, zero_rows, operands[2])

        input_grad, skip_grad, accumulated = lax.cond(
            active, backward_compute, backward_passthrough, (arrived, returned, accumulated)
        )
        skip_grads = store_slot(skip_grads, skip_grad, slot_index, active)
        landed = passed_along(skip_grad, "pipe", -3 * quarter)
        source = time_step - (segments - 1 - (position + 3 * quarter))
        is_valid = (position < quarter) & (source >= 0) & (source < micro_count)
        returned = store_slot(returned, landed, jnp.clip(source, 0, micro_count - 1), is_valid)
        arrived = passed_along(input_grad, "pipe", -1)
        return (arrived, returned, skip_grads, accumulated)

    back_state = (zero_rows, zero_buffer, zero_buffer, jnp.zeros((channels, channels), jnp.float32))
    back_state = lax.fori_loop(0, split_step, backward_step, back_state)
    back_state = lax.fori_loop(split_step, steps_total, backward_step, back_state)
    total = lax.psum(back_state[3], "dp")
    factor = 1.0 / math.sqrt(lax.axis_size("dp") * micro_count * row_count)
    return (total * factor)[None]


def solution(mesh):
    return jax.shard_map(
        shards,
        mesh=mesh,
        in_specs=(
            P("dp", None, None, None),
            P(),
            P("pipe", None, None),
            P("pipe", None, None),
            P("pipe", None),
            P("dp", None, None, None),
        ),
        out_specs=P("pipe", None, None),
        check_vma=False,
    )
```

profile of v0, /device:TPU:64, one launch (start us, length us, event | category | flops | bytes accessed | tf_op | source)
XLA Modules:
  0.0 635.2 jit_solution(8572554592605807592)
XLA Ops:
  7.3 76.5 %while.84 = (s32[]{:T(128)}, bf16[64,768]{1,0:T(8,128)(2,1)S(1)}, bf16[3,64,768]{2,1,0:T(8,128)(2,1)S(1)}, bf16[3,64,768]{2,1,0:T(8,128)(2,1)S(1)}, s32[]{:T(128...) while((s32[]{:T(128)}, bf16[64,768]{1,0:T(8,128)(2,1)S(1)}, ...), condition=%wide.region_4.5_spmd, body=%wide.region_0.4_spmd.sunk | while | flops 89710664 | bytes 4455945 | solution.py:105
  9.9 10.0 %collective-permute-start.1 = (bf16[64,768]{1,0:T(8,128)(2,1)S(1)}, bf16[64,768]{1,0:T(8,128)(2,1)S(1)}, u32[]{:S(2)}, u32[]{:S(2)}) collective-permute-start(bf16[64,768]{1,0:T(8,128)(2,1)S(1)} %get-tuple-element.1675), channel_id=1, source_target_pairs={{0,12},{1,13},{2,14},{3,15},{16,28},{17,29},{18,30},{19,31},{32,44... | collective-permute-start | bytes 294920 | tf_op jit(solution)/shard_map/while/body/eval_jaxpr/ppermute | solution.py:12
  24.9 6.5 %collective-permute-start.1 = (bf16[64,768]{1,0:T(8,128)(2,1)S(1)}, bf16[64,768]{1,0:T(8,128)(2,1)S(1)}, u32[]{:S(2)}, u32[]{:S(2)}) collective-permute-start(bf16[64,768]{1,0:T(8,128)(2,1)S(1)} %get-tuple-element.1675), channel_id=1, source_target_pairs={{0,12},{1,13},{2,14},{3,15},{16,28},{17,29},{18,30},{19,31},{32,44... | collective-permute-start | bytes 294920 | tf_op jit(solution)/shard_map/while/body/eval_jaxpr/ppermute | solution.py:12
  83.9 154.5 %while.85 = (s32[]{:T(128)}, bf16[64,768]{1,0:T(8,128)(2,1)S(1)}, bf16[3,64,768]{2,1,0:T(8,128)(2,1)S(1)}, bf16[3,64,768]{2,1,0:T(8,128)(2,1)S(1)}, s32[]{:T(128...) while((s32[]{:T(128)}, bf16[64,768]{1,0:T(8,128)(2,1)S(1)}, ...), condition=%wide.region_9.10_spmd, body=%wide.region_5.9_spmd.sunk | while | flops 89710664 | bytes 4455965 | solution.py:106
  132.0 6.5 %collective-permute-start.3 = (bf16[64,768]{1,0:T(8,128)(2,1)S(1)}, bf16[64,768]{1,0:T(8,128)(2,1)S(1)}, u32[]{:S(2)}, u32[]{:S(2)}) collective-permute-start(bf16[64,768]{1,0:T(8,128)(2,1)S(1)} %get-tuple-element.1691), channel_id=1, source_target_pairs={{0,12},{1,13},{2,14},{3,15},{16,28},{17,29},{18,30},{19,31},{32,44... | collective-permute-start | bytes 294920 | tf_op jit(solution)/shard_map/while/body/eval_jaxpr/ppermute | solution.py:12
  143.4 6.5 %collective-permute-start.3 = (bf16[64,768]{1,0:T(8,128)(2,1)S(1)}, bf16[64,768]{1,0:T(8,128)(2,1)S(1)}, u32[]{:S(2)}, u32[]{:S(2)}) collective-permute-start(bf16[64,768]{1,0:T(8,128)(2,1)S(1)} %get-tuple-element.1691), channel_id=1, source_target_pairs={{0,12},{1,13},{2,14},{3,15},{16,28},{17,29},{18,30},{19,31},{32,44... | collective-permute-start | bytes 294920 | tf_op jit(solution)/shard_map/while/body/eval_jaxpr/ppermute | solution.py:12
  154.8 6.5 %collective-permute-start.3 = (bf16[64,768]{1,0:T(8,128)(2,1)S(1)}, bf16[64,768]{1,0:T(8,128)(2,1)S(1)}, u32[]{:S(2)}, u32[]{:S(2)}) collective-permute-start(bf16[64,768]{1,0:T(8,128)(2,1)S(1)} %get-tuple-element.1691), channel_id=1, source_target_pairs={{0,12},{1,13},{2,14},{3,15},{16,28},{17,29},{18,30},{19,31},{32,44... | collective-permute-start | bytes 294920 | tf_op jit(solution)/shard_map/while/body/eval_jaxpr/ppermute | solution.py:12
  166.2 6.5 %collective-permute-start.3 = (bf16[64,768]{1,0:T(8,128)(2,1)S(1)}, bf16[64,768]{1,0:T(8,128)(2,1)S(1)}, u32[]{:S(2)}, u32[]{:S(2)}) collective-permute-start(bf16[64,768]{1,0:T(8,128)(2,1)S(1)} %get-tuple-element.1691), channel_id=1, source_target_pairs={{0,12},{1,13},{2,14},{3,15},{16,28},{17,29},{18,30},{19,31},{32,44... | collective-permute-start | bytes 294920 | tf_op jit(solution)/shard_map/while/body/eval_jaxpr/ppermute | solution.py:12
  177.6 13.4 %collective-permute-start.3 = (bf16[64,768]{1,0:T(8,128)(2,1)S(1)}, bf16[64,768]{1,0:T(8,128)(2,1)S(1)}, u32[]{:S(2)}, u32[]{:S(2)}) collective-permute-start(bf16[64,768]{1,0:T(8,128)(2,1)S(1)} %get-tuple-element.1691), channel_id=1, source_target_pairs={{0,12},{1,13},{2,14},{3,15},{16,28},{17,29},{18,30},{19,31},{32,44... | collective-permute-start | bytes 294920 | tf_op jit(solution)/shard_map/while/body/eval_jaxpr/ppermute | solution.py:12
  195.9 12.0 %collective-permute-start.3 = (bf16[64,768]{1,0:T(8,128)(2,1)S(1)}, bf16[64,768]{1,0:T(8,128)(2,1)S(1)}, u32[]{:S(2)}, u32[]{:S(2)}) collective-permute-start(bf16[64,768]{1,0:T(8,128)(2,1)S(1)} %get-tuple-element.1691), channel_id=1, source_target_pairs={{0,12},{1,13},{2,14},{3,15},{16,28},{17,29},{18,30},{19,31},{32,44... | collective-permute-start | bytes 294920 | tf_op jit(solution)/shard_map/while/body/eval_jaxpr/ppermute | solution.py:12
  212.8 12.0 %collective-permute-start.3 = (bf16[64,768]{1,0:T(8,128)(2,1)S(1)}, bf16[64,768]{1,0:T(8,128)(2,1)S(1)}, u32[]{:S(2)}, u32[]{:S(2)}) collective-permute-start(bf16[64,768]{1,0:T(8,128)(2,1)S(1)} %get-tuple-element.1691), channel_id=1, source_target_pairs={{0,12},{1,13},{2,14},{3,15},{16,28},{17,29},{18,30},{19,31},{32,44... | collective-permute-start | bytes 294920 | tf_op jit(solution)/shard_map/while/body/eval_jaxpr/ppermute | solution.py:12
  239.1 73.2 %while.86 = (s32[]{:T(128)}, bf16[64,768]{1,0:T(8,128)(2,1)S(1)}, bf16[3,64,768]{2,1,0:T(8,128)(2,1)S(1)}, f32[768,768]{1,0:T(8,128)S(1)}, s32[]{:T(128)}, /*ind...) while((s32[]{:T(128)}, bf16[64,768]{1,0:T(8,128)(2,1)S(1)}, ...), condition=%wide.region_15.16_spmd, body=%wide.region_10.15_spmd.sunk | while | flops 155271552 | bytes 11747327 | solution.py:149
  244.2 7.3 %collective-permute-done.5 = bf16[64,768]{1,0:T(8,128)(2,1)S(1)} collective-permute-done((bf16[64,768]{1,0:T(8,128)(2,1)S(1)}, bf16[64,768]{1,0:T(8,128)(2,1)S(1)}, u32[]{:S(2)}, u32[]{:S(2)}) %collective-permute-start.5) | collective-permute-done | bytes 98336 | tf_op jit(solution)/shard_map/while/body/eval_jaxpr/ppermute | solution.py:12
  257.3 8.7 %collective-permute-done.5 = bf16[64,768]{1,0:T(8,128)(2,1)S(1)} collective-permute-done((bf16[64,768]{1,0:T(8,128)(2,1)S(1)}, bf16[64,768]{1,0:T(8,128)(2,1)S(1)}, u32[]{:S(2)}, u32[]{:S(2)}) %collective-permute-start.5) | collective-permute-done | bytes 98336 | tf_op jit(solution)/shard_map/while/body/eval_jaxpr/ppermute | solution.py:12
  269.3 8.7 %collective-permute-done.5 = bf16[64,768]{1,0:T(8,128)(2,1)S(1)} collective-permute-done((bf16[64,768]{1,0:T(8,128)(2,1)S(1)}, bf16[64,768]{1,0:T(8,128)(2,1)S(1)}, u32[]{:S(2)}, u32[]{:S(2)}) %collective-permute-start.5) | collective-permute-done | bytes 98336 | tf_op jit(solution)/shard_map/while/body/eval_jaxpr/ppermute | solution.py:12
  281.4 8.1 %collective-permute-done.5 = bf16[64,768]{1,0:T(8,128)(2,1)S(1)} collective-permute-done((bf16[64,768]{1,0:T(8,128)(2,1)S(1)}, bf16[64,768]{1,0:T(8,128)(2,1)S(1)}, u32[]{:S(2)}, u32[]{:S(2)}) %collective-permute-start.5) | collective-permute-done | bytes 98336 | tf_op jit(solution)/shard_map/while/body/eval_jaxpr/ppermute | solution.py:12
  292.9 8.1 %collective-permute-done.5 = bf16[64,768]{1,0:T(8,128)(2,1)S(1)} collective-permute-done((bf16[64,768]{1,0:T(8,128)(2,1)S(1)}, bf16[64,768]{1,0:T(8,128)(2,1)S(1)}, u32[]{:S(2)}, u32[]{:S(2)}) %collective-permute-start.5) | collective-permute-done | bytes 98336 | tf_op jit(solution)/shard_map/while/body/eval_jaxpr/ppermute | solution.py:12
  304.4 7.9 %collective-permute-done.5 = bf16[64,768]{1,0:T(8,128)(2,1)S(1)} collective-permute-done((bf16[64,768]{1,0:T(8,128)(2,1)S(1)}, bf16[64,768]{1,0:T(8,128)(2,1)S(1)}, u32[]{:S(2)}, u32[]{:S(2)}) %collective-permute-start.5) | collective-permute-done | bytes 98336 | tf_op jit(solution)/shard_map/while/body/eval_jaxpr/ppermute | solution.py:12
  312.3 148.8 %while.87 = (s32[]{:T(128)}, bf16[64,768]{1,0:T(8,128)(2,1)S(1)}, bf16[3,64,768]{2,1,0:T(8,128)(2,1)S(1)}, f32[768,768]{1,0:T(8,128)S(1)}, s32[]{:T(128)}, /*ind...) while((s32[]{:T(128)}, bf16[64,768]{1,0:T(8,128)(2,1)S(1)}, ...), condition=%wide.region_21.22_spmd, body=%wide.region_16.21_spmd.sunk | while | flops 155271552 | bytes 11747347 | solution.py:150
  315.6 7.9 %collective-permute-done.7 = bf16[64,768]{1,0:T(8,128)(2,1)S(1)} collective-permute-done((bf16[64,768]{1,0:T(8,128)(2,1)S(1)}, bf16[64,768]{1,0:T(8,128)(2,1)S(1)}, u32[]{:S(2)}, u32[]{:S(2)}) %collective-permute-start.7) | collective-permute-done | bytes 98336 | tf_op jit(solution)/shard_map/while/body/eval_jaxpr/ppermute | solution.py:12
  326.9 7.9 %collective-permute-done.7 = bf16[64,768]{1,0:T(8,128)(2,1)S(1)} collective-permute-done((bf16[64,768]{1,0:T(8,128)(2,1)S(1)}, bf16[64,768]{1,0:T(8,128)(2,1)S(1)}, u32[]{:S(2)}, u32[]{:S(2)}) %collective-permute-start.7) | collective-permute-done | bytes 98336 | tf_op jit(solution)/shard_map/while/body/eval_jaxpr/ppermute | solution.py:12
  338.1 7.9 %collective-permute-done.7 = bf16[64,768]{1,0:T(8,128)(2,1)S(1)} collective-permute-done((bf16[64,768]{1,0:T(8,128)(2,1)S(1)}, bf16[64,768]{1,0:T(8,128)(2,1)S(1)}, u32[]{:S(2)}, u32[]{:S(2)}) %collective-permute-start.7) | collective-permute-done | bytes 98336 | tf_op jit(solution)/shard_map/while/body/eval_jaxpr/ppermute | solution.py:12
  349.3 7.9 %collective-permute-done.7 = bf16[64,768]{1,0:T(8,128)(2,1)S(1)} collective-permute-done((bf16[64,768]{1,0:T(8,128)(2,1)S(1)}, bf16[64,768]{1,0:T(8,128)(2,1)S(1)}, u32[]{:S(2)}, u32[]{:S(2)}) %collective-permute-start.7) | collective-permute-done | bytes 98336 | tf_op jit(solution)/shard_map/while/body/eval_jaxpr/ppermute | solution.py:12
  360.6 7.9 %collective-permute-done.7 = bf16[64,768]{1,0:T(8,128)(2,1)S(1)} collective-permute-done((bf16[64,768]{1,0:T(8,128)(2,1)S(1)}, bf16[64,768]{1,0:T(8,128)(2,1)S(1)}, u32[]{:S(2)}, u32[]{:S(2)}) %collective-permute-start.7) | collective-permute-done | bytes 98336 | tf_op jit(solution)/shard_map/while/body/eval_jaxpr/ppermute | solution.py:12
  371.8 7.9 %collective-permute-done.7 = bf16[64,768]{1,0:T(8,128)(2,1)S(1)} collective-permute-done((bf16[64,768]{1,0:T(8,128)(2,1)S(1)}, bf16[64,768]{1,0:T(8,128)(2,1)S(1)}, u32[]{:S(2)}, u32[]{:S(2)}) %collective-permute-start.7) | collective-permute-done | bytes 98336 | tf_op jit(solution)/shard_map/while/body/eval_jaxpr/ppermute | solution.py:12
  383.1 7.3 %collective-permute-done.7 = bf16[64,768]{1,0:T(8,128)(2,1)S(1)} collective-permute-done((bf16[64,768]{1,0:T(8,128)(2,1)S(1)}, bf16[64,768]{1,0:T(8,128)(2,1)S(1)}, u32[]{:S(2)}, u32[]{:S(2)}) %collective-permute-start.7) | collective-permute-done | bytes 98336 | tf_op jit(solution)/shard_map/while/body/eval_jaxpr/ppermute | solution.py:12
  398.9 7.3 %collective-permute-done.7 = bf16[64,768]{1,0:T(8,128)(2,1)S(1)} collective-permute-done((bf16[64,768]{1,0:T(8,128)(2,1)S(1)}, bf16[64,768]{1,0:T(8,128)(2,1)S(1)}, u32[]{:S(2)}, u32[]{:S(2)}) %collective-permute-start.7) | collective-permute-done | bytes 98336 | tf_op jit(solution)/shard_map/while/body/eval_jaxpr/ppermute | solution.py:12
  414.7 7.3 %collective-permute-done.7 = bf16[64,768]{1,0:T(8,128)(2,1)S(1)} collective-permute-done((bf16[64,768]{1,0:T(8,128)(2,1)S(1)}, bf16[64,768]{1,0:T(8,128)(2,1)S(1)}, u32[]{:S(2)}, u32[]{:S(2)}) %collective-permute-start.7) | collective-permute-done | bytes 98336 | tf_op jit(solution)/shard_map/while/body/eval_jaxpr/ppermute | solution.py:12
  430.5 7.9 %collective-permute-done.7 = bf16[64,768]{1,0:T(8,128)(2,1)S(1)} collective-permute-done((bf16[64,768]{1,0:T(8,128)(2,1)S(1)}, bf16[64,768]{1,0:T(8,128)(2,1)S(1)}, u32[]{:S(2)}, u32[]{:S(2)}) %collective-permute-start.7) | collective-permute-done | bytes 98336 | tf_op jit(solution)/shard_map/while/body/eval_jaxpr/ppermute | solution.py:12
  441.7 8.1 %collective-permute-done.7 = bf16[64,768]{1,0:T(8,128)(2,1)S(1)} collective-permute-done((bf16[64,768]{1,0:T(8,128)(2,1)S(1)}, bf16[64,768]{1,0:T(8,128)(2,1)S(1)}, u32[]{:S(2)}, u32[]{:S(2)}) %collective-permute-start.7) | collective-permute-done | bytes 98336 | tf_op jit(solution)/shard_map/while/body/eval_jaxpr/ppermute | solution.py:12
  453.2 7.9 %collective-permute-done.7 = bf16[64,768]{1,0:T(8,128)(2,1)S(1)} collective-permute-done((bf16[64,768]{1,0:T(8,128)(2,1)S(1)}, bf16[64,768]{1,0:T(8,128)(2,1)S(1)}, u32[]{:S(2)}, u32[]{:S(2)}) %collective-permute-start.7) | collective-permute-done | bytes 98336 | tf_op jit(solution)/shard_map/while/body/eval_jaxpr/ppermute | solution.py:12
  462.6 162.6 %all-reduce.12.cloned.1.call-done = f32[768,768]{1,0:T(8,128)} async-done(((f32[768,768]{1,0:T(8,128)}), f32[768,768]{1,0:T(8,128)}) %all-reduce.12.cloned.1.call-update) | async-done | bytes 2359312 | tf_op jit(solution)/shard_map/psum | solution.py:151
  (365 shorter events, 278.2 us)
Async XLA Ops:
  6.5 618.6 %all-reduce.12.cloned.1.call-start = ((), (), s32[]{:S(2)}) async-start(), calls=%async_computation | async-start | bytes 4718592 | tf_op jit(solution)/shard_map/psum | solution.py:151
  8.0 14.2 %collective-permute-start = (bf16[64,768]{1,0:T(8,128)(2,1)S(1)}, bf16[64,768]{1,0:T(8,128)(2,1)S(1)}, u32[]{:S(2)}, u32[]{:S(2)}) collective-permute-start(bf16[64,768]{1,0:T(8,128)(2,1)S(1)} %get-tuple-element.1675), channel_id=1, source_target_pairs={{0,1},{1,2},{2,3},{3,4},{4,5},{5,6},{6,7},{7,8},{8,9},{9,10},{10,1... | collective-permute-start | bytes 294920 | tf_op jit(solution)/shard_map/while/body/eval_jaxpr/ppermute | solution.py:12
  9.9 12.2 %collective-permute-start.1 = (bf16[64,768]{1,0:T(8,128)(2,1)S(1)}, bf16[64,768]{1,0:T(8,128)(2,1)S(1)}, u32[]{:S(2)}, u32[]{:S(2)}) collective-permute-start(bf16[64,768]{1,0:T(8,128)(2,1)S(1)} %get-tuple-element.1675), channel_id=1, source_target_pairs={{0,12},{1,13},{2,14},{3,15},{16,28},{17,29},{18,30},{19,31},{32,44... | collective-permute-start | bytes 294920 | tf_op jit(solution)/shard_map/while/body/eval_jaxpr/ppermute | solution.py:12
  22.9 12.6 %collective-permute-start = (bf16[64,768]{1,0:T(8,128)(2,1)S(1)}, bf16[64,768]{1,0:T(8,128)(2,1)S(1)}, u32[]{:S(2)}, u32[]{:S(2)}) collective-permute-start(bf16[64,768]{1,0:T(8,128)(2,1)S(1)} %get-tuple-element.1675), channel_id=1, source_target_pairs={{0,1},{1,2},{2,3},{3,4},{4,5},{5,6},{6,7},{7,8},{8,9},{9,10},{10,1... | collective-permute-start | bytes 294920 | tf_op jit(solution)/shard_map/while/body/eval_jaxpr/ppermute | solution.py:12
  107.2 10.7 %collective-permute-start.2 = (bf16[64,768]{1,0:T(8,128)(2,1)S(1)}, bf16[64,768]{1,0:T(8,128)(2,1)S(1)}, u32[]{:S(2)}, u32[]{:S(2)}) collective-permute-start(bf16[64,768]{1,0:T(8,128)(2,1)S(1)} %get-tuple-element.1691), channel_id=1, source_target_pairs={{0,1},{1,2},{2,3},{3,4},{4,5},{5,6},{6,7},{7,8},{8,9},{9,10},{10,1... | collective-permute-start | bytes 294920 | tf_op jit(solution)/shard_map/while/body/eval_jaxpr/ppermute | solution.py:12
  118.6 10.7 %collective-permute-start.2 = (bf16[64,768]{1,0:T(8,128)(2,1)S(1)}, bf16[64,768]{1,0:T(8,128)(2,1)S(1)}, u32[]{:S(2)}, u32[]{:S(2)}) collective-permute-start(bf16[64,768]{1,0:T(8,128)(2,1)S(1)} %get-tuple-element.1691), channel_id=1, source_target_pairs={{0,1},{1,2},{2,3},{3,4},{4,5},{5,6},{6,7},{7,8},{8,9},{9,10},{10,1... | collective-permute-start | bytes 294920 | tf_op jit(solution)/shard_map/while/body/eval_jaxpr/ppermute | solution.py:12
  130.0 10.7 %collective-permute-start.2 = (bf16[64,768]{1,0:T(8,128)(2,1)S(1)}, bf16[64,768]{1,0:T(8,128)(2,1)S(1)}, u32[]{:S(2)}, u32[]{:S(2)}) collective-permute-start(bf16[64,768]{1,0:T(8,128)(2,1)S(1)} %get-tuple-element.1691), channel_id=1, source_target_pairs={{0,1},{1,2},{2,3},{3,4},{4,5},{5,6},{6,7},{7,8},{8,9},{9,10},{10,1... | collective-permute-start | bytes 294920 | tf_op jit(solution)/shard_map/while/body/eval_jaxpr/ppermute | solution.py:12
  141.4 10.7 %collective-permute-start.2 = (bf16[64,768]{1,0:T(8,128)(2,1)S(1)}, bf16[64,768]{1,0:T(8,128)(2,1)S(1)}, u32[]{:S(2)}, u32[]{:S(2)}) collective-permute-start(bf16[64,768]{1,0:T(8,128)(2,1)S(1)} %get-tuple-element.1691), channel_id=1, source_target_pairs={{0,1},{1,2},{2,3},{3,4},{4,5},{5,6},{6,7},{7,8},{8,9},{9,10},{10,1... | collective-permute-start | bytes 294920 | tf_op jit(solution)/shard_map/while/body/eval_jaxpr/ppermute | solution.py:12
  152.8 10.7 %collective-permute-start.2 = (bf16[64,768]{1,0:T(8,128)(2,1)S(1)}, bf16[64,768]{1,0:T(8,128)(2,1)S(1)}, u32[]{:S(2)}, u32[]{:S(2)}) collective-permute-start(bf16[64,768]{1,0:T(8,128)(2,1)S(1)} %get-tuple-element.1691), channel_id=1, source_target_pairs={{0,1},{1,2},{2,3},{3,4},{4,5},{5,6},{6,7},{7,8},{8,9},{9,10},{10,1... | collective-permute-start | bytes 294920 | tf_op jit(solution)/shard_map/while/body/eval_jaxpr/ppermute | solution.py:12
  164.2 10.7 %collective-permute-start.2 = (bf16[64,768]{1,0:T(8,128)(2,1)S(1)}, bf16[64,768]{1,0:T(8,128)(2,1)S(1)}, u32[]{:S(2)}, u32[]{:S(2)}) collective-permute-start(bf16[64,768]{1,0:T(8,128)(2,1)S(1)} %get-tuple-element.1691), channel_id=1, source_target_pairs={{0,1},{1,2},{2,3},{3,4},{4,5},{5,6},{6,7},{7,8},{8,9},{9,10},{10,1... | collective-permute-start | bytes 294920 | tf_op jit(solution)/shard_map/while/body/eval_jaxpr/ppermute | solution.py:12
  175.6 17.6 %collective-permute-start.2 = (bf16[64,768]{1,0:T(8,128)(2,1)S(1)}, bf16[64,768]{1,0:T(8,128)(2,1)S(1)}, u32[]{:S(2)}, u32[]{:S(2)}) collective-permute-start(bf16[64,768]{1,0:T(8,128)(2,1)S(1)} %get-tuple-element.1691), channel_id=1, source_target_pairs={{0,1},{1,2},{2,3},{3,4},{4,5},{5,6},{6,7},{7,8},{8,9},{9,10},{10,1... | collective-permute-start | bytes 294920 | tf_op jit(solution)/shard_map/while/body/eval_jaxpr/ppermute | solution.py:12
  177.6 15.6 %collective-permute-start.3 = (bf16[64,768]{1,0:T(8,128)(2,1)S(1)}, bf16[64,768]{1,0:T(8,128)(2,1)S(1)}, u32[]{:S(2)}, u32[]{:S(2)}) collective-permute-start(bf16[64,768]{1,0:T(8,128)(2,1)S(1)} %get-tuple-element.1691), channel_id=1, source_target_pairs={{0,12},{1,13},{2,14},{3,15},{16,28},{17,29},{18,30},{19,31},{32,44... | collective-permute-start | bytes 294920 | tf_op jit(solution)/shard_map/while/body/eval_jaxpr/ppermute | solution.py:12
  194.0 16.1 %collective-permute-start.2 = (bf16[64,768]{1,0:T(8,128)(2,1)S(1)}, bf16[64,768]{1,0:T(8,128)(2,1)S(1)}, u32[]{:S(2)}, u32[]{:S(2)}) collective-permute-start(bf16[64,768]{1,0:T(8,128)(2,1)S(1)} %get-tuple-element.1691), channel_id=1, source_target_pairs={{0,1},{1,2},{2,3},{3,4},{4,5},{5,6},{6,7},{7,8},{8,9},{9,10},{10,1... | collective-permute-start | bytes 294920 | tf_op jit(solution)/shard_map/while/body/eval_jaxpr/ppermute | solution.py:12
  195.9 14.2 %collective-permute-start.3 = (bf16[64,768]{1,0:T(8,128)(2,1)S(1)}, bf16[64,768]{1,0:T(8,128)(2,1)S(1)}, u32[]{:S(2)}, u32[]{:S(2)}) collective-permute-start(bf16[64,768]{1,0:T(8,128)(2,1)S(1)} %get-tuple-element.1691), channel_id=1, source_target_pairs={{0,12},{1,13},{2,14},{3,15},{16,28},{17,29},{18,30},{19,31},{32,44... | collective-permute-start | bytes 294920 | tf_op jit(solution)/shard_map/while/body/eval_jaxpr/ppermute | solution.py:12
  210.8 16.1 %collective-permute-start.2 = (bf16[64,768]{1,0:T(8,128)(2,1)S(1)}, bf16[64,768]{1,0:T(8,128)(2,1)S(1)}, u32[]{:S(2)}, u32[]{:S(2)}) collective-permute-start(bf16[64,768]{1,0:T(8,128)(2,1)S(1)} %get-tuple-element.1691), channel_id=1, source_target_pairs={{0,1},{1,2},{2,3},{3,4},{4,5},{5,6},{6,7},{7,8},{8,9},{9,10},{10,1... | collective-permute-start | bytes 294920 | tf_op jit(solution)/shard_map/while/body/eval_jaxpr/ppermute | solution.py:12
  212.8 14.2 %collective-permute-start.3 = (bf16[64,768]{1,0:T(8,128)(2,1)S(1)}, bf16[64,768]{1,0:T(8,128)(2,1)S(1)}, u32[]{:S(2)}, u32[]{:S(2)}) collective-permute-start(bf16[64,768]{1,0:T(8,128)(2,1)S(1)} %get-tuple-element.1691), channel_id=1, source_target_pairs={{0,12},{1,13},{2,14},{3,15},{16,28},{17,29},{18,30},{19,31},{32,44... | collective-permute-start | bytes 294920 | tf_op jit(solution)/shard_map/while/body/eval_jaxpr/ppermute | solution.py:12
  227.7 10.7 %collective-permute-start.2 = (bf16[64,768]{1,0:T(8,128)(2,1)S(1)}, bf16[64,768]{1,0:T(8,128)(2,1)S(1)}, u32[]{:S(2)}, u32[]{:S(2)}) collective-permute-start(bf16[64,768]{1,0:T(8,128)(2,1)S(1)} %get-tuple-element.1691), channel_id=1, source_target_pairs={{0,1},{1,2},{2,3},{3,4},{4,5},{5,6},{6,7},{7,8},{8,9},{9,10},{10,1... | collective-permute-start | bytes 294920 | tf_op jit(solution)/shard_map/while/body/eval_jaxpr/ppermute | solution.py:12
  239.1 12.4 %collective-permute-start.4 = (bf16[64,768]{1,0:T(8,128)(2,1)S(1)}, bf16[64,768]{1,0:T(8,128)(2,1)S(1)}, u32[]{:S(2)}, u32[]{:S(2)}) collective-permute-start(bf16[64,768]{1,0:T(8,128)(2,1)S(1)} %get-tuple-element.1709), channel_id=1, source_target_pairs={{1,0},{2,1},{3,2},{4,3},{5,4},{6,5},{7,6},{8,7},{9,8},{10,9},{11,1... | collective-permute-start | bytes 294920 | tf_op jit(solution)/shard_map/while/body/eval_jaxpr/ppermute | solution.py:12
  251.6 14.4 %collective-permute-start.4 = (bf16[64,768]{1,0:T(8,128)(2,1)S(1)}, bf16[64,768]{1,0:T(8,128)(2,1)S(1)}, u32[]{:S(2)}, u32[]{:S(2)}) collective-permute-start(bf16[64,768]{1,0:T(8,128)(2,1)S(1)} %get-tuple-element.1709), channel_id=1, source_target_pairs={{1,0},{2,1},{3,2},{4,3},{5,4},{6,5},{7,6},{8,7},{9,8},{10,9},{11,1... | collective-permute-start | bytes 294920 | tf_op jit(solution)/shard_map/while/body/eval_jaxpr/ppermute | solution.py:12
  266.1 12.0 %collective-permute-start.4 = (bf16[64,768]{1,0:T(8,128)(2,1)S(1)}, bf16[64,768]{1,0:T(8,128)(2,1)S(1)}, u32[]{:S(2)}, u32[]{:S(2)}) collective-permute-start(bf16[64,768]{1,0:T(8,128)(2,1)S(1)} %get-tuple-element.1709), channel_id=1, source_target_pairs={{1,0},{2,1},{3,2},{4,3},{5,4},{6,5},{7,6},{8,7},{9,8},{10,9},{11,1... | collective-permute-start | bytes 294920 | tf_op jit(solution)/shard_map/while/body/eval_jaxpr/ppermute | solution.py:12
  278.1 11.4 %collective-permute-start.4 = (bf16[64,768]{1,0:T(8,128)(2,1)S(1)}, bf16[64,768]{1,0:T(8,128)(2,1)S(1)}, u32[]{:S(2)}, u32[]{:S(2)}) collective-permute-start(bf16[64,768]{1,0:T(8,128)(2,1)S(1)} %get-tuple-element.1709), channel_id=1, source_target_pairs={{1,0},{2,1},{3,2},{4,3},{5,4},{6,5},{7,6},{8,7},{9,8},{10,9},{11,1... | collective-permute-start | bytes 294920 | tf_op jit(solution)/shard_map/while/body/eval_jaxpr/ppermute | solution.py:12
  289.6 11.4 %collective-permute-start.4 = (bf16[64,768]{1,0:T(8,128)(2,1)S(1)}, bf16[64,768]{1,0:T(8,128)(2,1)S(1)}, u32[]{:S(2)}, u32[]{:S(2)}) collective-permute-start(bf16[64,768]{1,0:T(8,128)(2,1)S(1)} %get-tuple-element.1709), channel_id=1, source_target_pairs={{1,0},{2,1},{3,2},{4,3},{5,4},{6,5},{7,6},{8,7},{9,8},{10,9},{11,1... | collective-permute-start | bytes 294920 | tf_op jit(solution)/shard_map/while/body/eval_jaxpr/ppermute | solution.py:12
  301.1 11.2 %collective-permute-start.4 = (bf16[64,768]{1,0:T(8,128)(2,1)S(1)}, bf16[64,768]{1,0:T(8,128)(2,1)S(1)}, u32[]{:S(2)}, u32[]{:S(2)}) collective-permute-start(bf16[64,768]{1,0:T(8,128)(2,1)S(1)} %get-tuple-element.1709), channel_id=1, source_target_pairs={{1,0},{2,1},{3,2},{4,3},{5,4},{6,5},{7,6},{8,7},{9,8},{10,9},{11,1... | collective-permute-start | bytes 294920 | tf_op jit(solution)/shard_map/while/body/eval_jaxpr/ppermute | solution.py:12
  312.3 11.2 %collective-permute-start.6 = (bf16[64,768]{1,0:T(8,128)(2,1)S(1)}, bf16[64,768]{1,0:T(8,128)(2,1)S(1)}, u32[]{:S(2)}, u32[]{:S(2)}) collective-permute-start(bf16[64,768]{1,0:T(8,128)(2,1)S(1)} %get-tuple-element.1725), channel_id=1, source_target_pairs={{1,0},{2,1},{3,2},{4,3},{5,4},{6,5},{7,6},{8,7},{9,8},{10,9},{11,1... | collective-permute-start | bytes 294920 | tf_op jit(solution)/shard_map/while/body/eval_jaxpr/ppermute | solution.py:12
  323.6 11.2 %collective-permute-start.6 = (bf16[64,768]{1,0:T(8,128)(2,1)S(1)}, bf16[64,768]{1,0:T(8,128)(2,1)S(1)}, u32[]{:S(2)}, u32[]{:S(2)}) collective-permute-start(bf16[64,768]{1,0:T(8,128)(2,1)S(1)} %get-tuple-element.1725), channel_id=1, source_target_pairs={{1,0},{2,1},{3,2},{4,3},{5,4},{6,5},{7,6},{8,7},{9,8},{10,9},{11,1... | collective-permute-start | bytes 294920 | tf_op jit(solution)/shard_map/while/body/eval_jaxpr/ppermute | solution.py:12
  334.8 11.2 %collective-permute-start.6 = (bf16[64,768]{1,0:T(8,128)(2,1)S(1)}, bf16[64,768]{1,0:T(8,128)(2,1)S(1)}, u32[]{:S(2)}, u32[]{:S(2)}) collective-permute-start(bf16[64,768]{1,0:T(8,128)(2,1)S(1)} %get-tuple-element.1725), channel_id=1, source_target_pairs={{1,0},{2,1},{3,2},{4,3},{5,4},{6,5},{7,6},{8,7},{9,8},{10,9},{11,1... | collective-permute-start | bytes 294920 | tf_op jit(solution)/shard_map/while/body/eval_jaxpr/ppermute | solution.py:12
  346.1 11.2 %collective-permute-start.6 = (bf16[64,768]{1,0:T(8,128)(2,1)S(1)}, bf16[64,768]{1,0:T(8,128)(2,1)S(1)}, u32[]{:S(2)}, u32[]{:S(2)}) collective-permute-start(bf16[64,768]{1,0:T(8,128)(2,1)S(1)} %get-tuple-element.1725), channel_id=1, source_target_pairs={{1,0},{2,1},{3,2},{4,3},{5,4},{6,5},{7,6},{8,7},{9,8},{10,9},{11,1... | collective-permute-start | bytes 294920 | tf_op jit(solution)/shard_map/while/body/eval_jaxpr/ppermute | solution.py:12
  357.3 11.2 %collective-permute-start.6 = (bf16[64,768]{1,0:T(8,128)(2,1)S(1)}, bf16[64,768]{1,0:T(8,128)(2,1)S(1)}, u32[]{:S(2)}, u32[]{:S(2)}) collective-permute-start(bf16[64,768]{1,0:T(8,128)(2,1)S(1)} %get-tuple-element.1725), channel_id=1, source_target_pairs={{1,0},{2,1},{3,2},{4,3},{5,4},{6,5},{7,6},{8,7},{9,8},{10,9},{11,1... | collective-permute-start | bytes 294920 | tf_op jit(solution)/shard_map/while/body/eval_jaxpr/ppermute | solution.py:12
  368.5 11.2 %collective-permute-start.6 = (bf16[64,768]{1,0:T(8,128)(2,1)S(1)}, bf16[64,768]{1,0:T(8,128)(2,1)S(1)}, u32[]{:S(2)}, u32[]{:S(2)}) collective-permute-start(bf16[64,768]{1,0:T(8,128)(2,1)S(1)} %get-tuple-element.1725), channel_id=1, source_target_pairs={{1,0},{2,1},{3,2},{4,3},{5,4},{6,5},{7,6},{8,7},{9,8},{10,9},{11,1... | collective-permute-start | bytes 294920 | tf_op jit(solution)/shard_map/while/body/eval_jaxpr/ppermute | solution.py:12
  427.2 11.2 %collective-permute-start.6 = (bf16[64,768]{1,0:T(8,128)(2,1)S(1)}, bf16[64,768]{1,0:T(8,128)(2,1)S(1)}, u32[]{:S(2)}, u32[]{:S(2)}) collective-permute-start(bf16[64,768]{1,0:T(8,128)(2,1)S(1)} %get-tuple-element.1725), channel_id=1, source_target_pairs={{1,0},{2,1},{3,2},{4,3},{5,4},{6,5},{7,6},{8,7},{9,8},{10,9},{11,1... | collective-permute-start | bytes 294920 | tf_op jit(solution)/shard_map/while/body/eval_jaxpr/ppermute | solution.py:12
  438.4 11.4 %collective-permute-start.6 = (bf16[64,768]{1,0:T(8,128)(2,1)S(1)}, bf16[64,768]{1,0:T(8,128)(2,1)S(1)}, u32[]{:S(2)}, u32[]{:S(2)}) collective-permute-start(bf16[64,768]{1,0:T(8,128)(2,1)S(1)} %get-tuple-element.1725), channel_id=1, source_target_pairs={{1,0},{2,1},{3,2},{4,3},{5,4},{6,5},{7,6},{8,7},{9,8},{10,9},{11,1... | collective-permute-start | bytes 294920 | tf_op jit(solution)/shard_map/while/body/eval_jaxpr/ppermute | solution.py:12
  449.9 11.2 %collective-permute-start.6 = (bf16[64,768]{1,0:T(8,128)(2,1)S(1)}, bf16[64,768]{1,0:T(8,128)(2,1)S(1)}, u32[]{:S(2)}, u32[]{:S(2)}) collective-permute-start(bf16[64,768]{1,0:T(8,128)(2,1)S(1)} %get-tuple-element.1725), channel_id=1, source_target_pairs={{1,0},{2,1},{3,2},{4,3},{5,4},{6,5},{7,6},{8,7},{9,8},{10,9},{11,1... | collective-permute-start | bytes 294920 | tf_op jit(solution)/shard_map/while/body/eval_jaxpr/ppermute | solution.py:12
  (43 other events, 352.8 us)
Sparse Core Ops, SparseCore 0:
  462.7 162.4 all-reduce.11
where the time goes:
time: 638 us; the launch traced here: 635 us
  waiting for transfers between devices  344 us (54%)
  starting transfers between devices  219 us (34%)
  other arithmetic  20.1 us (3%)
  matrix products  18.7 us (3%)
  local copies, waits for them, and re-layouts  16.1 us (3%)
  between operations  13.5 us (2%)
    ppermute x72, starting transfers between devices, passed_along(): return lax.ppermute(block, axis, route)  219 us
    ppermute x72, waiting for transfers between devices, passed_along(): return lax.ppermute(block, axis, route)  181 us
    psum x1, waiting for transfers between devices, shards(): total = lax.psum(back_state[3], 'dp')  163 us
  transfers between devices with their start and end apart: 73, of which 41 were waited for; matrix products, arithmetic and copies ran while one was open for 1% of the time, Pallas kernels for 0%

commit v1 on v0

v1 whole, which is shorter than its diff:
```python
import functools
import math

import jax
import jax.numpy as jnp
from jax import lax
from jax.experimental import pallas as pl
from jax.experimental.pallas import tpu as pltpu
from jax.sharding import PartitionSpec as P

GROUP = 4
MICROS = 3
CHUNK = 256
ANY = pl.BlockSpec(memory_space=pl.ANY)
VM = pl.BlockSpec(memory_space=pltpu.VMEM)
SM = pl.BlockSpec(memory_space=pltpu.SMEM)
PARAMS = pltpu.CompilerParams(vmem_limit_bytes=40 * 1024 * 1024)
CUBIC = 0.044715
SCALE = math.sqrt(2.0 / math.pi)


def row_before(block):
    rows = lax.broadcasted_iota(jnp.int32, block.shape, 0)
    return jnp.where(rows == 0, 0.0, pltpu.roll(block, 1, 0))


def row_after(block):
    size = block.shape[0]
    rows = lax.broadcasted_iota(jnp.int32, block.shape, 0)
    return jnp.where(rows == size - 1, 0.0, pltpu.roll(block, size - 1, 0))


def chunks_of(channels):
    return [slice(c, c + CHUNK) for c in range(0, channels, CHUNK)]


def start_weights(member, order, sources, wbuf, wsem):
    for j in order:
        for d in range(GROUP):

            @pl.when(jnp.bitwise_xor(member, j) == d)
            def _():
                pltpu.make_async_copy(sources[d], wbuf.at[d], wsem.at[d]).start()


def forward_kernel(stage, skip, towers, flags, x_ref, w0, w1, w2, w3, par_ref, *rest):
    rest = list(rest)
    k_ref = rest.pop(0) if skip else None
    rest.pop(0)
    y_ref, uh_hbm, gp_hbm, inv_hbm, h_hbm = rest[:5]
    rest = rest[5:]
    ys_hbm = rest.pop(0) if towers else None
    wbuf, ub, uh, gp, inv_b, hb, yb, wsem, osem = rest
    channels = x_ref.shape[1]
    member = flags[1]

    @pl.when((flags[0] == stage) & (member < MICROS))
    def _():
        start_weights(member, range(GROUP), (w0, w1, w2, w3), wbuf, wsem)
        copies = []
        for j in range(GROUP):
            d = jnp.bitwise_xor(member, j)
            squares = None
            for cs in chunks_of(channels):
                if j == 0:
                    u = x_ref[:, cs].astype(jnp.float32)
                else:
                    u = yb[j - 1, :, cs].astype(jnp.float32)
                if skip:
                    u = u + k_ref[j, :, cs].astype(jnp.float32)
                ub[:, cs] = u
                part = jnp.sum(u * u, axis=-1, keepdims=True)
                squares = part if squares is None else squares + part
            inv = lax.rsqrt(squares * (1.0 / channels) + 1e-06)
            inv_b[j] = jnp.broadcast_to(inv, inv_b.shape[1:])
            pltpu.make_async_copy(w0, wbuf.at[d], wsem.at[d]).wait()
            total = None
            for cs in chunks_of(channels):
                unit = ub[:, cs] * inv
                uh[j, :, cs] = unit
                n = unit * par_ref[d, 3:4, cs]
                v = (
                    par_ref[d, 0:1, cs] * row_before(n)
                    + par_ref[d, 1:2, cs] * n
                    + par_ref[d, 2:3, cs] * row_after(n)
                )
                v2 = v * v
                th = jnp.tanh(v * (SCALE + (SCALE * CUBIC) * v2))
                half = 0.5 * (1.0 + th)
                gp[j, :, cs] = half + (0.5 * v) * (1.0 - th * th) * (
                    SCALE + (3.0 * SCALE * CUBIC) * v2
                )
                act = (v * half).astype(jnp.bfloat16)
                hb[d, :, cs] = act
                part = jnp.dot(act, wbuf[d, cs, :], preferred_element_type=jnp.float32)
                total = part if total is None else total + part
            y = (ub[...] + total).astype(jnp.bfloat16)
            yb[j] = y
            for buf, hbm, at in ((uh, uh_hbm, j), (gp, gp_hbm, j), (inv_b, inv_hbm, j), (hb, h_hbm, d)):
                copies.append(pltpu.make_async_copy(buf.at[at], hbm.at[at], osem.at[len(copies)]))
                copies[-1].start()
        y_ref[...] = yb[GROUP - 1]
        if towers:
            copies.append(pltpu.make_async_copy(yb, ys_hbm, osem.at[len(copies)]))
            copies[-1].start()
        for copy in copies:
            copy.wait()


def forward_stage(stage, skip, towers, flags, x, weights, par, k, h):
    rows, channels = x.shape
    f32, bf = jnp.float32, jnp.bfloat16
    wide = (GROUP, rows, channels)
    thin = (GROUP, rows, 128)
    out_shape = [
        jax.ShapeDtypeStruct((rows, channels), bf),
        jax.ShapeDtypeStruct(wide, f32),
        jax.ShapeDtypeStruct(wide, f32),
        jax.ShapeDtypeStruct(thin, f32),
        jax.ShapeDtypeStruct(wide, bf),
    ]
    out_specs = [VM, ANY, ANY, ANY, ANY]
    if towers:
        out_shape.append(jax.ShapeDtypeStruct(wide, bf))
        out_specs.append(ANY)
    args = [flags, x, *weights, par]
    in_specs = [SM, VM, ANY, ANY, ANY, ANY, VM]
    if skip:
        args.append(k)
        in_specs.append(VM)
    args.append(h)
    in_specs.append(ANY)
    return pl.pallas_call(
        functools.partial(forward_kernel, stage, skip, towers),
        out_shape=out_shape,
        in_specs=in_specs,
        out_specs=out_specs,
        scratch_shapes=[
            pltpu.VMEM((GROUP, channels, channels), bf),
            pltpu.VMEM((rows, channels), f32),
            pltpu.VMEM(wide, f32),
            pltpu.VMEM(wide, f32),
            pltpu.VMEM(thin, f32),
            pltpu.VMEM(wide, bf),
            pltpu.VMEM(wide, bf),
            pltpu.SemaphoreType.DMA((GROUP,)),
            pltpu.SemaphoreType.DMA((4 * GROUP + 1,)),
        ],
        input_output_aliases={len(args) - 1: 4},
        compiler_params=PARAMS,
        name=f"ahead{stage}",
    )(*args)


def backward_kernel(stage, last, first, flags, g_ref, w0, w1, w2, w3, par_ref, uh_hbm, gp_hbm, inv_hbm, *rest):
    rest = list(rest)
    k_ref = rest.pop(0) if first else None
    rest.pop(0)
    e_hbm = rest.pop(0)
    dx_ref = None if first else rest.pop(0)
    gk_hbm = rest.pop(0) if last else None
    wbuf, gb, mb, uh, gp, inv_b, eb, db, wsem, ssem, osem = rest
    channels = g_ref.shape[1]
    member = flags[1]

    @pl.when((flags[0] == stage) & (member < MICROS))
    def _():
        order = list(reversed(range(GROUP)))
        reads = {}
        for j in order:
            start_weights(member, [j], (w0, w1, w2, w3), wbuf, wsem)
            reads[j] = [
                pltpu.make_async_copy(hbm.at[j], buf.at[j], ssem.at[3 * j + i])
                for i, (hbm, buf) in enumerate(((uh_hbm, uh), (gp_hbm, gp), (inv_hbm, inv_b)))
            ]
            for read in reads[j]:
                read.start()
        copies = []
        for j in order:
            d = jnp.bitwise_xor(member, j)
            source = g_ref if j == GROUP - 1 else db.at[j + 1]
            for cs in chunks_of(channels):
                g = source[:, cs].astype(jnp.float32)
                if first:
                    g = g + k_ref[j, :, cs].astype(jnp.float32)
                gb[:, cs] = g
                eb[d, :, cs] = g.astype(jnp.bfloat16)
            copies.append(pltpu.make_async_copy(eb.at[d], e_hbm.at[d], osem.at[len(copies)]))
            copies[-1].start()
            pltpu.make_async_copy(w0, wbuf.at[d], wsem.at[d]).wait()
            for read in reads[j]:
                read.wait()
            if first and j == 0:
                continue
            e = eb[d]
            dots = None
            for cs in chunks_of(channels):
                da = lax.dot_general(
                    e, wbuf[d, cs, :], (((1,), (1,)), ((), ())), preferred_element_type=jnp.float32
                )
                dv = da * gp[j, :, cs]
                dn = (
                    par_ref[d, 0:1, cs] * row_after(dv)
                    + par_ref[d, 1:2, cs] * dv
                    + par_ref[d, 2:3, cs] * row_before(dv)
                )
                m = dn * par_ref[d, 3:4, cs]
                mb[:, cs] = m
                part = jnp.sum(m * uh[j, :, cs], axis=-1, keepdims=True)
                dots = part if dots is None else dots + part
            mean = dots * (1.0 / channels)
            inv = inv_b[j, :, 0:1]
            for cs in chunks_of(channels):
                du = inv * (mb[:, cs] - uh[j, :, cs] * mean)
                db[j, :, cs] = (gb[:, cs] + du).astype(jnp.bfloat16)
        if not first:
            dx_ref[...] = db[0]
        if last:
            copies.append(pltpu.make_async_copy(db, gk_hbm, osem.at[len(copies)]))
            copies[-1].start()
        for copy in copies:
            copy.wait()


def backward_stage(stage, last, first, flags, g, weights, par, state, k, e):
    rows, channels = g.shape
    f32, bf = jnp.float32, jnp.bfloat16
    wide = (GROUP, rows, channels)
    thin = (GROUP, rows, 128)
    args = [flags, g, *weights, par, *state]
    in_specs = [SM, VM, ANY, ANY, ANY, ANY, VM, ANY, ANY, ANY]
    if first:
        args.append(k)
        in_specs.append(VM)
    args.append(e)
    in_specs.append(ANY)
    out_shape = [jax.ShapeDtypeStruct(wide, bf)]
    out_specs = [ANY]
    if not first:
        out_shape.append(jax.ShapeDtypeStruct((rows, channels), bf))
        out_specs.append(VM)
    if last:
        out_shape.append(jax.ShapeDtypeStruct(wide, bf))
        out_specs.append(ANY)
    return pl.pallas_call(
        functools.partial(backward_kernel, stage, last, first),
        out_shape=out_shape,
        in_specs=in_specs,
        out_specs=out_specs,
        scratch_shapes=[
            pltpu.VMEM((GROUP, channels, channels), bf),
            pltpu.VMEM((rows, channels), f32),
            pltpu.VMEM((rows, channels), f32),
            pltpu.VMEM(wide, f32),
            pltpu.VMEM(wide, f32),
            pltpu.VMEM(thin, f32),
            pltpu.VMEM(wide, bf),
            pltpu.VMEM(wide, bf),
            pltpu.SemaphoreType.DMA((GROUP,)),
            pltpu.SemaphoreType.DMA((3 * GROUP,)),
            pltpu.SemaphoreType.DMA((GROUP + 1,)),
        ],
        input_output_aliases={len(args) - 1: 0},
        compiler_params=PARAMS,
        name=f"behind{stage}",
    )(*args)


def encode_bases(base_rows, embed_table):
    one_hot = (base_rows[:, :, None] == jnp.arange(4, dtype=jnp.int32)).astype(jnp.bfloat16)
    one_hot = one_hot.reshape(base_rows.shape[0], -1)
    return jnp.dot(one_hot, embed_table, preferred_element_type=jnp.float32).astype(jnp.bfloat16)


def swapped(block, distance, count):
    return lax.ppermute(block, "pipe", [(i, i ^ distance) for i in range(count)])


def shifted(block, stage, to_stage):
    pairs = [(GROUP * stage + i, GROUP * to_stage + i) for i in range(MICROS)]
    return lax.ppermute(block, "pipe", pairs)


def traded(block, distance, count):
    pairs = [(i, i ^ distance) for i in range(count) if i % GROUP < MICROS]
    return lax.ppermute(block[distance], "pipe", pairs)


def shards(base_ids, embed_table, segment_weights, conv_taps, norm_gains, cotangent):
    count = lax.axis_size("pipe")
    replicas = lax.axis_size("dp")
    stages = count // GROUP
    position = lax.axis_index("pipe")
    member = position % GROUP
    flags = jnp.stack([position // GROUP, member]).astype(jnp.int32)
    micro = jnp.minimum(member, MICROS - 1)
    weight = segment_weights[0]
    channels = weight.shape[1]
    row_count = base_ids.shape[2]
    half = channels // 2

    own = jnp.concatenate([conv_taps[0], norm_gains, jnp.zeros((4, channels), jnp.float32)])
    across = [swapped(weight[:half], 2, count), swapped(weight[half:], 2, count)]
    beside = swapped(weight, 1, count)
    par = jnp.stack([own] + [swapped(own, d, count) for d in range(1, GROUP)])
    corner = [swapped(part, 1, count) for part in across]
    weights = (weight, beside, jnp.concatenate(across), jnp.concatenate(corner))

    x = encode_bases(base_ids[0, micro], embed_table)
    wide = (GROUP, row_count, channels)
    h = jnp.zeros(wide, jnp.bfloat16)
    e = jnp.zeros(wide, jnp.bfloat16)
    states, k = [], None
    for stage in range(stages):
        skip, towers = stage == stages - 1, stage == 0
        outs = forward_stage(stage, skip, towers, flags, x, weights, par, k, h)
        states.append(outs[1:4])
        h = outs[4]
        if towers:
            k = shifted(outs[5], 0, stages - 1)
        if stage < stages - 1:
            x = shifted(outs[0], stage, stage + 1)

    g = cotangent[0, micro]
    returned = None
    for stage in reversed(range(stages)):
        last, first = stage == stages - 1, stage == 0
        outs = backward_stage(stage, last, first, flags, g, weights, par, states[stage], returned, e)
        e = outs[0]
        if last:
            returned = shifted(outs[2], stages - 1, 0)
            h, e = lax.optimization_barrier((h, e))
            acts = jnp.concatenate([h[0]] + [traded(h, d, count) for d in range(1, GROUP)])
        if stage > 0:
            g = shifted(outs[1], stage, stage - 1)
    errors = jnp.concatenate([e[0]] + [traded(e, d, count) for d in range(1, GROUP)])

    terms = lax.dot_general(acts, errors, (((0,), (0,)), ((), ())), preferred_element_type=jnp.float32)
    pieces = terms.astype(jnp.bfloat16).reshape(replicas, channels // replicas, channels)
    pieces = lax.all_to_all(pieces, "dp", 0, 0)
    factor = 1.0 / math.sqrt(replicas * MICROS * row_count)
    piece = jnp.sum(pieces.astype(jnp.float32), axis=0) * factor
    piece = jnp.broadcast_to(piece.astype(jnp.bfloat16)[None], pieces.shape)
    whole = lax.all_to_all(piece, "dp", 0, 0)
    return whole.reshape(1, channels, channels).astype(jnp.float32)


def solution(mesh):
    return jax.shard_map(
        shards,
        mesh=mesh,
        in_specs=(
            P("dp", None, None, None),
            P(),
            P("pipe", None, None),
            P("pipe", None, None),
            P("pipe", None),
            P("dp", None, None, None),
        ),
        out_specs=P("pipe", None, None),
        check_vma=False,
    )
```

time: 638 us -> 227 us (0.36)
  the two profiles are of different devices: /device:TPU:64 before, /device:TPU:8 now
where the time goes in v1:
time: 227 us; the launch traced here: 226 us
  blocking collectives  78 us (34%)
  waiting for transfers between devices  72.1 us (32%)
  starting transfers between devices  46.4 us (20%)
  Pallas kernels  18.9 us (8%)
  local copies, waits for them, and re-layouts  5.92 us (3%)
  other arithmetic  3.3 us (1%)
    ppermute x8, waiting for transfers between devices, shifted(): return lax.ppermute(block, 'pipe', pairs)  58.4 us
    all_to_all x1, blocking collectives, shards(): pieces = lax.all_to_all(pieces, 'dp', 0, 0)  42.2 us
    all_to_all x1, blocking collectives, shards(): whole = lax.all_to_all(piece, 'dp', 0, 0)  35.8 us
    ppermute x8, starting transfers between devices, swapped(): lax.ppermute(block, 'pipe', [(i, i ^ distance) for i in range(count)])  20.4 us
    ppermute x6, starting transfers between devices, traded(): return lax.ppermute(block[distance], 'pipe', pairs)  15.3 us
    ppermute x8, waiting for transfers between devices, swapped(): lax.ppermute(block, 'pipe', [(i, i ^ distance) for i in range(count)])  12.5 us
    ppermute x8, starting transfers between devices, shifted(): return lax.ppermute(block, 'pipe', pairs)  10.6 us
    pallas_call x4, Pallas kernels, forward_stage(): pl.pallas_call(functools.partial(forward_kernel, stage, skip, towers), ou...  9.85 us
  transfers between devices with their start and end apart: 22, of which 7 were waited for; matrix products, arithmetic and copies ran while one was open for 2% of the time, Pallas kernels for 4%

profile of v1, /device:TPU:8, one launch (start us, length us, event | category | flops | bytes accessed | tf_op | source)
XLA Modules:
  0.0 226.0 jit_solution(12528890899432516480)
XLA Ops:
  0.0 2.5 %slice_bitcast_fusion = (bf16[384,768]{1,0:T(8,128)(2,1)}, bf16[384,768]{1,0:T(8,128)(2,1)}) fusion(bf16[1,768,768]{2,1,0:T(8,128)(2,1)} %param.8), kind=kLoop, calls=%fused_computation.4 | loop fusion | bytes 2359296 | tf_op jit(solution)/shard_map/slice | solution.py:303
  2.5 4.3 %collective-permute-start.1 = (bf16[384,768]{1,0:T(8,128)(2,1)}, bf16[384,768]{1,0:T(8,128)(2,1)}, u32[]{:S(2)}, u32[]{:S(2)}) collective-permute-start(bf16[384,768]{1,0:T(8,128)(2,1)} %get-tuple-element.64), channel_id=1, source_target_pairs={{0,2},{1,3},{2,0},{3,1},{4,6},{5,7},{6,4},{7,5},{8,10},{9,11},{10,... | collective-permute-start | bytes 1769480 | tf_op jit(solution)/shard_map/ppermute | solution.py:276
  6.8 1.9 collective-permute-start.2
  8.7 1.9 collective-permute-start
  11.5 4.0 %collective-permute-start.7 = (f32[8,768]{1,0:T(8,128)}, f32[8,768]{1,0:T(8,128)}, u32[]{:S(2)}, u32[]{:S(2)}) collective-permute-start(f32[8,768]{1,0:T(8,128)} %get-tuple-element.74), channel_id=1, source_target_pairs={{0,3},{1,2},{2,1},{3,0},{4,7},{5,6},{6,5},{7,4},{8,11},{9,10},{10,... | collective-permute-start | bytes 73736 | tf_op jit(solution)/shard_map/ppermute | solution.py:276
  15.5 1.9 collective-permute-start.6
  18.3 3.0 %collective-permute-done.1 = bf16[384,768]{1,0:T(8,128)(2,1)} collective-permute-done((bf16[384,768]{1,0:T(8,128)(2,1)}, bf16[384,768]{1,0:T(8,128)(2,1)}, u32[]{:S(2)}, u32[]{:S(2)}) %collective-permute-start.1) | collective-permute-done | bytes 589856 | tf_op jit(solution)/shard_map/ppermute | solution.py:276
  21.2 1.9 collective-permute-start.3
  23.5 9.5 %collective-permute-done.7 = f32[8,768]{1,0:T(8,128)} collective-permute-done((f32[8,768]{1,0:T(8,128)}, f32[8,768]{1,0:T(8,128)}, u32[]{:S(2)}, u32[]{:S(2)}) %collective-permute-start.7) | collective-permute-done | bytes 24608 | tf_op jit(solution)/shard_map/ppermute | solution.py:276
  33.0 2.6 %collective-permute-start.5 = (f32[8,768]{1,0:T(8,128)}, f32[8,768]{1,0:T(8,128)S(1)}, u32[]{:S(2)}, u32[]{:S(2)}) collective-permute-start(f32[8,768]{1,0:T(8,128)} %get-tuple-element.74), channel_id=1, source_target_pairs={{0,1},{1,0},{2,3},{3,2},{4,5},{5,4},{6,7},{7,6},{8,9},{9,8},{10,11... | collective-permute-start | bytes 73736 | tf_op jit(solution)/shard_map/ppermute | solution.py:276
  35.6 1.9 collective-permute-start.4
  38.4 1.1 constant_dynamic-update-slice_fusion.1
  39.5 1.1 constant_dynamic-update-slice_fusion.3
  40.8 7.0 %ahead0.1 = (bf16[64,768]{1,0:T(8,128)(2,1)S(1)}, f32[4,64,768]{2,1,0:T(8,128)S(1)}, f32[4,64,768]{2,1,0:T(8,128)S(1)}, f32[4,64,128]{2,1,0:T(8,128)S(1)}, bf16[...) custom-call(s32[2]{0:T(128)S(1)} %pad_add_fusion.flags, ...), custom_call_target="tpu_custom_call", output_to_operand_aliasing={{4}: (7, {})} | custom-call | tf_op jit(solution)/shard_map/ahead0/pallas_call | solution.py:133
  47.8 4.1 %collective-permute-start.11 = (bf16[4,64,768]{2,1,0:T(8,128)(2,1)S(1)}, bf16[4,64,768]{2,1,0:T(8,128)(2,1)S(1)}, u32[]{:S(2)}, u32[]{:S(2)}) collective-permute-start(bf16[4,64,768]{2,1,0:T(8,128)(2,1)S(1)} %get-tuple-element.39), channel_id=1, source_target_pairs={{0,12},{1,13},{2,14},{16,28},{17,29},{18,30},{32,44},{33,45},{34,4... | collective-permute-start | bytes 1179656 | tf_op jit(solution)/shard_map/ppermute | solution.py:281
  51.8 1.3 collective-permute-start.8
  53.1 2.7 %collective-permute-done.8.x_ref = bf16[64,768]{1,0:T(8,128)(2,1)S(1)} collective-permute-done((bf16[64,768]{1,0:T(8,128)(2,1)S(1)}, bf16[64,768]{1,0:T(8,128)(2,1)S(1)}, u32[]{:S(2)}, u32[]{:S(2)}) %collective-permute-start.8) | collective-permute-done | bytes 98336 | tf_op jit(solution)/shard_map/ppermute | solution.py:281
  58.7 6.3 %collective-permute-done.11.rest_0_ = bf16[4,64,768]{2,1,0:T(8,128)(2,1)S(1)} collective-permute-done((bf16[4,64,768]{2,1,0:T(8,128)(2,1)S(1)}, bf16[4,64,768]{2,1,0:T(8,128)(2,1)S(1)}, u32[]{:S(2)}, u32[]{:S(2)}) %collective-permute-start.11) | collective-permute-done | bytes 393248 | tf_op jit(solution)/shard_map/ppermute | solution.py:281
  65.0 1.4 ahead3.1
  68.1 1.3 collective-permute-start.18
  71.6 1.3 collective-permute-start.17
  72.9 1.3 collective-permute-start.14
  74.2 3.9 %collective-permute-start.13 = (bf16[64,768]{1,0:T(8,128)(2,1)S(1)}, bf16[64,768]{1,0:T(8,128)(2,1)S(1)}, u32[]{:S(2)}, u32[]{:S(2)}) collective-permute-start(bf16[64,768]{1,0:T(8,128)(2,1)S(1)} %get-tuple-element.71), channel_id=1, source_target_pairs={{0,2},{1,3},{2,0},{4,6},{5,7},{6,4},{8,10},{9,11},{10,8},{12,14},{... | collective-permute-start | bytes 294920 | tf_op jit(solution)/shard_map/ppermute | solution.py:286
  78.1 1.9 collective-permute-start.12
  80.0 49.3 %collective-permute-done.17.g_ref = bf16[64,768]{1,0:T(8,128)(2,1)S(1)} collective-permute-done((bf16[64,768]{1,0:T(8,128)(2,1)S(1)}, bf16[64,768]{1,0:T(8,128)(2,1)S(1)}, u32[]{:S(2)}, u32[]{:S(2)}) %collective-permute-start.17) | collective-permute-done | bytes 98336 | tf_op jit(solution)/shard_map/ppermute | solution.py:281
  129.4 6.6 %behind0.1 = bf16[4,64,768]{2,1,0:T(8,128)(2,1)S(1)} custom-call(s32[2]{0:T(128)S(1)} %pad_add_fusion.flags, bf16[64,768]{1,0:T(8,128)(2,1)S(1)} %collective-permute-done.17.g_ref, bf16[768,768]{1,0:T(8,128)(2,1)S(1)} %bitcast.50, bf16[768,768]{1,0:T(8,128)(2,1)S(1)} %collective-permute-done.w1, ...), custom_call_target="tpu_custom_call", output_to_operand_aliasing={{}: (11, {})} | custom-call | tf_op jit(solution)/shard_map/behind0/pallas_call | solution.py:245
  136.0 1.3 collective-permute-start.21
  137.3 5.0 %collective-permute-start.20 = (bf16[64,768]{1,0:T(8,128)(2,1)S(1)}, bf16[64,768]{1,0:T(8,128)(2,1)S(1)}, u32[]{:S(2)}, u32[]{:S(2)}) collective-permute-start(bf16[64,768]{1,0:T(8,128)(2,1)S(1)} %get-tuple-element.67), channel_id=1, source_target_pairs={{0,2},{1,3},{2,0},{4,6},{5,7},{6,4},{8,10},{9,11},{10,8},{12,14},{... | collective-permute-start | bytes 294920 | tf_op jit(solution)/shard_map/ppermute | solution.py:286
  142.4 1.9 collective-permute-start.19
  146.1 42.2 %all_to_all.10 = bf16[32,24,768]{2,1,0:T(8,128)(2,1)S(1)} all-to-all(bf16[32,24,768]{2,1,0:T(8,128)(2,1)S(1)} %bitcast.52), channel_id=1, replica_groups=mesh['dp'=32,'pipe'=16] {'dp'}, dimensions={0} | all-to-all | bytes 2359296 | tf_op jit(solution)/shard_map/all_to_all | solution.py:340
  188.6 35.8 %all_to_all.11 = bf16[32,24,768]{2,1,0:T(8,128)(2,1)S(1)} all-to-all(bf16[32,24,768]{2,1,0:T(8,128)(2,1)S(1)} %broadcast_in_dim.5), channel_id=1, replica_groups=mesh['dp'=32,'pipe'=16] {'dp'}, dimensions={0} | all-to-all | bytes 2359296 | tf_op jit(solution)/shard_map/all_to_all | solution.py:344
  224.4 1.6 bitcast_convert_fusion
  (58 shorter events, 11.6 us)
Async XLA Ops:
  0.0 58.7 %copy-start = (bf16[1,3,64,768]{3,2,1,0:T(8,128)(2,1)S(1)}, bf16[1,3,64,768]{3,2,1,0:T(8,128)(2,1)}, u32[]{:S(2)}) copy-start(bf16[1,3,64,768]{3,2,1,0:T(8,128)(2,1)} %param.11) | copy-start | bytes 884740
  0.0 8.7 %copy-start.1 = (bf16[1,768,768]{2,1,0:T(8,128)(2,1)S(1)}, bf16[1,768,768]{2,1,0:T(8,128)(2,1)}, u32[]{:S(2)}) copy-start(bf16[1,768,768]{2,1,0:T(8,128)(2,1)} %param.8) | copy-start | bytes 3538948
  0.0 10.7 %copy-start.3 = (f32[1,3,768]{2,0,1:T(1,128)S(1)}, f32[1,3,768]{2,0,1:T(1,128)}, u32[]{:S(2)}) copy-start(f32[1,3,768]{2,0,1:T(1,128)} %param.9) | copy-start | bytes 27652
  0.0 10.8 %copy-start.4 = (f32[1,768]{1,0:T(1,128)S(1)}, f32[1,768]{1,0:T(1,128)}, u32[]{:S(2)}) copy-start(f32[1,768]{1,0:T(1,128)} %param.10) | copy-start | bytes 9220
  0.0 23.2 %copy-start.2 = (bf16[128,768]{1,0:T(8,128)(2,1)S(1)}, bf16[128,768]{1,0:T(8,128)(2,1)}, u32[]{:S(2)}) copy-start(bf16[128,768]{1,0:T(8,128)(2,1)} %param.7) | copy-start | bytes 589828
  2.5 18.7 %collective-permute-start.1 = (bf16[384,768]{1,0:T(8,128)(2,1)}, bf16[384,768]{1,0:T(8,128)(2,1)}, u32[]{:S(2)}, u32[]{:S(2)}) collective-permute-start(bf16[384,768]{1,0:T(8,128)(2,1)} %get-tuple-element.64), channel_id=1, source_target_pairs={{0,2},{1,3},{2,0},{3,1},{4,6},{5,7},{6,4},{7,5},{8,10},{9,11},{10,... | collective-permute-start | bytes 1769480 | tf_op jit(solution)/shard_map/ppermute | solution.py:276
  6.8 28.8 %collective-permute-start.2 = (bf16[384,768]{1,0:T(8,128)(2,1)}, bf16[384,768]{1,0:T(8,128)(2,1)S(1)}, u32[]{:S(2)}, u32[]{:S(2)}) collective-permute-start(bf16[384,768]{1,0:T(8,128)(2,1)} %get-tuple-element.63), channel_id=1, source_target_pairs={{0,2},{1,3},{2,0},{3,1},{4,6},{5,7},{6,4},{7,5},{8,10},{9,11},{10,... | collective-permute-start | bytes 1769480 | tf_op jit(solution)/shard_map/ppermute | solution.py:276
  8.7 32.0 %collective-permute-start = (bf16[768,768]{1,0:T(8,128)(2,1)S(1)}, bf16[768,768]{1,0:T(8,128)(2,1)S(1)}, u32[]{:S(2)}, u32[]{:S(2)}) collective-permute-start(bf16[768,768]{1,0:T(8,128)(2,1)S(1)} %bitcast.42), channel_id=1, source_target_pairs={{0,1},{1,0},{2,3},{3,2},{4,5},{5,4},{6,7},{7,6},{8,9},{9,8},{10,11... | collective-permute-start | bytes 3538952 | tf_op jit(solution)/shard_map/ppermute | solution.py:276
  11.5 21.5 %collective-permute-start.7 = (f32[8,768]{1,0:T(8,128)}, f32[8,768]{1,0:T(8,128)}, u32[]{:S(2)}, u32[]{:S(2)}) collective-permute-start(f32[8,768]{1,0:T(8,128)} %get-tuple-element.74), channel_id=1, source_target_pairs={{0,3},{1,2},{2,1},{3,0},{4,7},{5,6},{6,5},{7,4},{8,11},{9,10},{10,... | collective-permute-start | bytes 73736 | tf_op jit(solution)/shard_map/ppermute | solution.py:276
  15.5 22.1 %collective-permute-start.6 = (f32[8,768]{1,0:T(8,128)}, f32[8,768]{1,0:T(8,128)}, u32[]{:S(2)}, u32[]{:S(2)}) collective-permute-start(f32[8,768]{1,0:T(8,128)} %get-tuple-element.74), channel_id=1, source_target_pairs={{0,2},{1,3},{2,0},{3,1},{4,6},{5,7},{6,4},{7,5},{8,10},{9,11},{10,... | collective-permute-start | bytes 73736 | tf_op jit(solution)/shard_map/ppermute | solution.py:276
  21.2 18.3 %collective-permute-start.3 = (bf16[384,768]{1,0:T(8,128)(2,1)}, bf16[384,768]{1,0:T(8,128)(2,1)}, u32[]{:S(2)}, u32[]{:S(2)}) collective-permute-start(bf16[384,768]{1,0:T(8,128)(2,1)} %collective-permute-done.1), channel_id=1, source_target_pairs={{0,1},{1,0},{2,3},{3,2},{4,5},{5,4},{6,7},{7,6},{8,9},{9,8},{10,11... | collective-permute-start | bytes 1769480 | tf_op jit(solution)/shard_map/ppermute | solution.py:276
  33.0 4.6 %collective-permute-start.5 = (f32[8,768]{1,0:T(8,128)}, f32[8,768]{1,0:T(8,128)S(1)}, u32[]{:S(2)}, u32[]{:S(2)}) collective-permute-start(f32[8,768]{1,0:T(8,128)} %get-tuple-element.74), channel_id=1, source_target_pairs={{0,1},{1,0},{2,3},{3,2},{4,5},{5,4},{6,7},{7,6},{8,9},{9,8},{10,11... | collective-permute-start | bytes 73736 | tf_op jit(solution)/shard_map/ppermute | solution.py:276
  35.6 5.1 %collective-permute-start.4 = (bf16[384,768]{1,0:T(8,128)(2,1)S(1)}, bf16[384,768]{1,0:T(8,128)(2,1)S(1)}, u32[]{:S(2)}, u32[]{:S(2)}) collective-permute-start(bf16[384,768]{1,0:T(8,128)(2,1)S(1)} %collective-permute-done.2), channel_id=1, source_target_pairs={{0,1},{1,0},{2,3},{3,2},{4,5},{5,4},{6,7},{7,6},{8,9},{9,8},{10,11... | collective-permute-start | bytes 1769480 | tf_op jit(solution)/shard_map/ppermute | solution.py:276
  47.8 17.3 %collective-permute-start.11 = (bf16[4,64,768]{2,1,0:T(8,128)(2,1)S(1)}, bf16[4,64,768]{2,1,0:T(8,128)(2,1)S(1)}, u32[]{:S(2)}, u32[]{:S(2)}) collective-permute-start(bf16[4,64,768]{2,1,0:T(8,128)(2,1)S(1)} %get-tuple-element.39), channel_id=1, source_target_pairs={{0,12},{1,13},{2,14},{16,28},{17,29},{18,30},{32,44},{33,45},{34,4... | collective-permute-start | bytes 1179656 | tf_op jit(solution)/shard_map/ppermute | solution.py:281
  51.8 4.0 %collective-permute-start.8 = (bf16[64,768]{1,0:T(8,128)(2,1)S(1)}, bf16[64,768]{1,0:T(8,128)(2,1)S(1)}, u32[]{:S(2)}, u32[]{:S(2)}) collective-permute-start(bf16[64,768]{1,0:T(8,128)(2,1)S(1)} %get-tuple-element.34), channel_id=1, source_target_pairs={{0,4},{1,5},{2,6},{16,20},{17,21},{18,22},{32,36},{33,37},{34,38},... | collective-permute-start | bytes 294920 | tf_op jit(solution)/shard_map/ppermute | solution.py:281
  56.6 0.7 collective-permute-start.9
  58.0 0.7 collective-permute-start.10
  67.4 2.0 collective-permute-start.15
  68.1 61.3 %collective-permute-start.18 = (bf16[4,64,768]{2,1,0:T(8,128)(2,1)S(1)}, bf16[4,64,768]{2,1,0:T(8,128)(2,1)S(1)}, u32[]{:S(2)}, u32[]{:S(2)}) collective-permute-start(bf16[4,64,768]{2,1,0:T(8,128)(2,1)S(1)} %get-tuple-element.61), channel_id=1, source_target_pairs={{12,0},{13,1},{14,2},{28,16},{29,17},{30,18},{44,32},{45,33},{46,3... | collective-permute-start | bytes 1179656 | tf_op jit(solution)/shard_map/ppermute | solution.py:281
  70.1 0.7 collective-permute-start.16
  71.6 57.8 %collective-permute-start.17 = (bf16[64,768]{1,0:T(8,128)(2,1)S(1)}, bf16[64,768]{1,0:T(8,128)(2,1)S(1)}, u32[]{:S(2)}, u32[]{:S(2)}) collective-permute-start(bf16[64,768]{1,0:T(8,128)(2,1)S(1)} %get-tuple-element.57), channel_id=1, source_target_pairs={{4,0},{5,1},{6,2},{20,16},{21,17},{22,18},{36,32},{37,33},{38,34},... | collective-permute-start | bytes 294920 | tf_op jit(solution)/shard_map/ppermute | solution.py:281
  72.9 69.5 %collective-permute-start.14 = (bf16[64,768]{1,0:T(8,128)(2,1)S(1)}, bf16[64,768]{1,0:T(8,128)(2,1)S(1)}, u32[]{:S(2)}, u32[]{:S(2)}) collective-permute-start(bf16[64,768]{1,0:T(8,128)(2,1)S(1)} %get-tuple-element.70), channel_id=1, source_target_pairs={{0,3},{1,2},{2,1},{4,7},{5,6},{6,5},{8,11},{9,10},{10,9},{12,15},{... | collective-permute-start | bytes 294920 | tf_op jit(solution)/shard_map/ppermute | solution.py:286
  74.2 70.1 %collective-permute-start.13 = (bf16[64,768]{1,0:T(8,128)(2,1)S(1)}, bf16[64,768]{1,0:T(8,128)(2,1)S(1)}, u32[]{:S(2)}, u32[]{:S(2)}) collective-permute-start(bf16[64,768]{1,0:T(8,128)(2,1)S(1)} %get-tuple-element.71), channel_id=1, source_target_pairs={{0,2},{1,3},{2,0},{4,6},{5,7},{6,4},{8,10},{9,11},{10,8},{12,14},{... | collective-permute-start | bytes 294920 | tf_op jit(solution)/shard_map/ppermute | solution.py:286
  78.1 66.3 %collective-permute-start.12 = (bf16[64,768]{1,0:T(8,128)(2,1)S(1)}, bf16[64,768]{1,0:T(8,128)(2,1)S(1)}, u32[]{:S(2)}, u32[]{:S(2)}) collective-permute-start(bf16[64,768]{1,0:T(8,128)(2,1)S(1)} %get-tuple-element.72), channel_id=1, source_target_pairs={{0,1},{1,0},{2,3},{4,5},{5,4},{6,7},{8,9},{9,8},{10,11},{12,13},{1... | collective-permute-start | bytes 294920 | tf_op jit(solution)/shard_map/ppermute | solution.py:286
  136.0 8.3 %collective-permute-start.21 = (bf16[64,768]{1,0:T(8,128)(2,1)S(1)}, bf16[64,768]{1,0:T(8,128)(2,1)S(1)}, u32[]{:S(2)}, u32[]{:S(2)}) collective-permute-start(bf16[64,768]{1,0:T(8,128)(2,1)S(1)} %get-tuple-element.66), channel_id=1, source_target_pairs={{0,3},{1,2},{2,1},{4,7},{5,6},{6,5},{8,11},{9,10},{10,9},{12,15},{... | collective-permute-start | bytes 294920 | tf_op jit(solution)/shard_map/ppermute | solution.py:286
  137.3 7.6 %collective-permute-start.20 = (bf16[64,768]{1,0:T(8,128)(2,1)S(1)}, bf16[64,768]{1,0:T(8,128)(2,1)S(1)}, u32[]{:S(2)}, u32[]{:S(2)}) collective-permute-start(bf16[64,768]{1,0:T(8,128)(2,1)S(1)} %get-tuple-element.67), channel_id=1, source_target_pairs={{0,2},{1,3},{2,0},{4,6},{5,7},{6,4},{8,10},{9,11},{10,8},{12,14},{... | collective-permute-start | bytes 294920 | tf_op jit(solution)/shard_map/ppermute | solution.py:286
  142.4 3.2 %collective-permute-start.19 = (bf16[64,768]{1,0:T(8,128)(2,1)S(1)}, bf16[64,768]{1,0:T(8,128)(2,1)S(1)}, u32[]{:S(2)}, u32[]{:S(2)}) collective-permute-start(bf16[64,768]{1,0:T(8,128)(2,1)S(1)} %get-tuple-element.68), channel_id=1, source_target_pairs={{0,1},{1,0},{2,3},{4,5},{5,4},{6,7},{8,9},{9,8},{10,11},{12,13},{1... | collective-permute-start | bytes 294920 | tf_op jit(solution)/shard_map/ppermute | solution.py:286

commit v2 on v1

v2 whole, which is shorter than its diff:
```python
import functools
import math

import jax
import jax.numpy as jnp
from jax import lax
from jax.experimental import pallas as pl
from jax.experimental.pallas import tpu as pltpu
from jax.sharding import PartitionSpec as P

GROUP = 4
MICROS = 3
CHUNK = 256
ANY = pl.BlockSpec(memory_space=pl.ANY)
VM = pl.BlockSpec(memory_space=pltpu.VMEM)
SM = pl.BlockSpec(memory_space=pltpu.SMEM)
PARAMS = pltpu.CompilerParams(vmem_limit_bytes=24 * 1024 * 1024)
CUBIC = 0.044715
SCALE = math.sqrt(2.0 / math.pi)


def row_before(block):
    rows = lax.broadcasted_iota(jnp.int32, block.shape, 0)
    return jnp.where(rows == 0, 0.0, pltpu.roll(block, 1, 0))


def row_after(block):
    size = block.shape[0]
    rows = lax.broadcasted_iota(jnp.int32, block.shape, 0)
    return jnp.where(rows == size - 1, 0.0, pltpu.roll(block, size - 1, 0))


def chunks_of(channels):
    return [slice(c, c + CHUNK) for c in range(0, channels, CHUNK)]


def forward_kernel(stage, skip, towers, flags, x_ref, w_ref, par_ref, *rest):
    rest = list(rest)
    k_ref = rest.pop(0) if skip else None
    h_ref = rest.pop(0)
    y_ref, uh, gp, inv_b, hb = rest[:5]
    rest = rest[5:]
    ys = rest.pop(0) if towers else None
    (ub,) = rest
    channels = x_ref.shape[1]
    member = flags[1]
    active = (flags[0] == stage) & (member < MICROS)

    @pl.when(jnp.logical_not(active))
    def _():
        hb[...] = h_ref[...]

    @pl.when(active)
    def _():
        y = x_ref[...]
        for j in range(GROUP):
            d = jnp.bitwise_xor(member, j)
            squares = None
            for cs in chunks_of(channels):
                u = y[:, cs].astype(jnp.float32)
                if skip:
                    u = u + k_ref[j, :, cs].astype(jnp.float32)
                ub[:, cs] = u
                part = jnp.sum(u * u, axis=-1, keepdims=True)
                squares = part if squares is None else squares + part
            inv = lax.rsqrt(squares * (1.0 / channels) + 1e-06)
            inv_b[j] = jnp.broadcast_to(inv, inv_b.shape[1:])
            total = None
            for cs in chunks_of(channels):
                unit = ub[:, cs] * inv
                uh[j, :, cs] = unit
                n = unit * par_ref[j, 3:4, cs]
                v = (
                    par_ref[j, 0:1, cs] * row_before(n)
                    + par_ref[j, 1:2, cs] * n
                    + par_ref[j, 2:3, cs] * row_after(n)
                )
                v2 = v * v
                th = jnp.tanh(v * (SCALE + (SCALE * CUBIC) * v2))
                half = 0.5 * (1.0 + th)
                gp[j, :, cs] = half + (0.5 * v) * (1.0 - th * th) * (
                    SCALE + (3.0 * SCALE * CUBIC) * v2
                )
                act = (v * half).astype(jnp.bfloat16)
                hb[d, :, cs] = act
                part = jnp.dot(act, w_ref[j, cs, :], preferred_element_type=jnp.float32)
                total = part if total is None else total + part
            y = (ub[...] + total).astype(jnp.bfloat16)
            if towers:
                ys[j] = y
        y_ref[...] = y


def kept(shape, kind):
    return pltpu.VMEM(shape, kind)


def held(*arrays):
    return [pltpu.with_memory_space_constraint(a, pltpu.VMEM) for a in arrays]


def forward_stage(stage, skip, towers, flags, x, weights, par, k, h):
    rows, channels = x.shape
    f32, bf = jnp.float32, jnp.bfloat16
    wide = (GROUP, rows, channels)
    thin = (GROUP, rows, 128)
    out_shape = [
        kept((rows, channels), bf),
        kept(wide, f32),
        kept(wide, f32),
        kept(thin, f32),
        kept(wide, bf),
    ]
    if towers:
        out_shape.append(kept(wide, bf))
    args = [x, weights, par]
    if skip:
        args.append(k)
    args.append(h)
    args = [flags] + held(*args)
    return pl.pallas_call(
        functools.partial(forward_kernel, stage, skip, towers),
        out_shape=out_shape,
        in_specs=[SM] + [VM] * (len(args) - 1),
        out_specs=[VM] * len(out_shape),
        scratch_shapes=[pltpu.VMEM((rows, channels), f32)],
        input_output_aliases={len(args) - 1: 4},
        compiler_params=PARAMS,
        name=f"ahead{stage}",
    )(*args)


def backward_kernel(stage, last, first, flags, g_ref, w_ref, par_ref, uh, gp, inv_b, *rest):
    rest = list(rest)
    k_ref = rest.pop(0) if first else None
    e_ref = rest.pop(0)
    eb = rest.pop(0)
    dx_ref = None if first else rest.pop(0)
    gk_ref = rest.pop(0) if last else None
    gb, mb = rest
    channels = g_ref.shape[1]
    member = flags[1]
    active = (flags[0] == stage) & (member < MICROS)

    @pl.when(jnp.logical_not(active))
    def _():
        eb[...] = e_ref[...]

    @pl.when(active)
    def _():
        dx = g_ref[...]
        for j in reversed(range(GROUP)):
            d = jnp.bitwise_xor(member, j)
            for cs in chunks_of(channels):
                g = dx[:, cs].astype(jnp.float32)
                if first:
                    g = g + k_ref[j, :, cs].astype(jnp.float32)
                gb[:, cs] = g
            e = gb[...].astype(jnp.bfloat16)
            eb[d] = e
            if first and j == 0:
                continue
            dots = None
            for cs in chunks_of(channels):
                da = lax.dot_general(
                    e, w_ref[j, cs, :], (((1,), (1,)), ((), ())), preferred_element_type=jnp.float32
                )
                dv = da * gp[j, :, cs]
                dn = (
                    par_ref[j, 0:1, cs] * row_after(dv)
                    + par_ref[j, 1:2, cs] * dv
                    + par_ref[j, 2:3, cs] * row_before(dv)
                )
                m = dn * par_ref[j, 3:4, cs]
                mb[:, cs] = m
                part = jnp.sum(m * uh[j, :, cs], axis=-1, keepdims=True)
                dots = part if dots is None else dots + part
            mean = dots * (1.0 / channels)
            inv = inv_b[j, :, 0:1]
            dx = (gb[...] + inv * (mb[...] - uh[j] * mean)).astype(jnp.bfloat16)
            if last:
                gk_ref[j] = dx
        if not first:
            dx_ref[...] = dx


def backward_stage(stage, last, first, flags, g, weights, par, state, k, e):
    rows, channels = g.shape
    f32, bf = jnp.float32, jnp.bfloat16
    wide = (GROUP, rows, channels)
    args = [g, weights, par, *state]
    if first:
        args.append(k)
    args.append(e)
    args = [flags] + held(*args)
    out_shape = [kept(wide, bf)]
    if not first:
        out_shape.append(kept((rows, channels), bf))
    if last:
        out_shape.append(kept(wide, bf))
    return pl.pallas_call(
        functools.partial(backward_kernel, stage, last, first),
        out_shape=out_shape,
        in_specs=[SM] + [VM] * (len(args) - 1),
        out_specs=[VM] * len(out_shape),
        scratch_shapes=[pltpu.VMEM((rows, channels), f32)] * 2,
        input_output_aliases={len(args) - 1: 0},
        compiler_params=PARAMS,
        name=f"behind{stage}",
    )(*args)


def encode_bases(base_rows, embed_table):
    one_hot = (base_rows[:, :, None] == jnp.arange(4, dtype=jnp.int32)).astype(jnp.bfloat16)
    one_hot = one_hot.reshape(base_rows.shape[0], -1)
    return jnp.dot(one_hot, embed_table, preferred_element_type=jnp.float32).astype(jnp.bfloat16)


def swapped(block, distance, count):
    return lax.ppermute(block, "pipe", [(i, i ^ distance) for i in range(count)])


def pack_kernel(places, flags, *rest):
    parts, out, sems = rest[: len(places)], rest[-2], rest[-1]
    copies = []
    for i, ((d, row), part) in enumerate(zip(places, parts)):
        slot = jnp.bitwise_xor(flags[1], d)
        target = out.at[slot, pl.ds(row, part.shape[0]), :]
        copies.append(pltpu.make_async_copy(part, target, sems.at[i]))
        copies[-1].start()
    for copy in copies:
        copy.wait()


def packed(stack, flags, items):
    places = [(d, row) for d, row, _ in items]
    parts = [part for _, _, part in items]
    channels = parts[0].shape[1]
    args, specs, aliases = [flags] + parts, [SM] + [ANY] * len(parts), {}
    if stack is not None:
        aliases = {len(args): 0}
        args += held(stack)
        specs.append(ANY)
    return pl.pallas_call(
        functools.partial(pack_kernel, places),
        out_shape=kept((GROUP, channels, channels), jnp.bfloat16),
        in_specs=specs,
        out_specs=ANY,
        scratch_shapes=[pltpu.SemaphoreType.DMA((len(parts),))],
        input_output_aliases=aliases,
        compiler_params=PARAMS,
        name="packed",
    )(*args)


def placed(stack, parts, member, row=0):
    for d, part in enumerate(parts):
        if part is not None:
            slot = jnp.bitwise_xor(member, d)
            stack = lax.dynamic_update_slice(stack, part[None], (slot, row, 0))
    return stack


def shifted(block, stage, to_stage):
    pairs = [(GROUP * stage + i, GROUP * to_stage + i) for i in range(MICROS)]
    return lax.ppermute(block, "pipe", pairs)


def traded(block, distance, count):
    pairs = [(i, i ^ distance) for i in range(count) if i % GROUP < MICROS]
    return lax.ppermute(block[distance], "pipe", pairs)


def shards(base_ids, embed_table, segment_weights, conv_taps, norm_gains, cotangent):
    count = lax.axis_size("pipe")
    replicas = lax.axis_size("dp")
    stages = count // GROUP
    position = lax.axis_index("pipe")
    member = position % GROUP
    flags = jnp.stack([position // GROUP, member]).astype(jnp.int32)
    micro = jnp.minimum(member, MICROS - 1)
    weight = segment_weights[0]
    channels = weight.shape[1]
    row_count = base_ids.shape[2]
    half = channels // 2

    own = jnp.concatenate([conv_taps[0], norm_gains, jnp.zeros((4, channels), jnp.float32)])
    across = [swapped(weight[:half], 2, count), swapped(weight[half:], 2, count)]
    beside = swapped(weight, 1, count)
    par = placed(
        jnp.zeros((GROUP,) + own.shape, jnp.float32),
        [own] + [swapped(own, d, count) for d in range(1, GROUP)],
        member,
    )
    corner = [swapped(part, 1, count) for part in across]
    weights = packed(None, flags, [(0, 0, weight), (1, 0, beside)])
    weights = packed(weights, flags, [(2, 0, across[0]), (3, 0, corner[0]), (2, half, across[1])])
    weights = packed(weights, flags, [(3, half, corner[1])])

    x = encode_bases(base_ids[0, micro], embed_table)
    wide = (GROUP, row_count, channels)
    h = jnp.zeros(wide, jnp.bfloat16)
    e = jnp.zeros(wide, jnp.bfloat16)
    states, k = [], None
    for stage in range(stages):
        skip, towers = stage == stages - 1, stage == 0
        outs = forward_stage(stage, skip, towers, flags, x, weights, par, k, h)
        states.append(outs[1:4])
        h = outs[4]
        if stage < stages - 1:
            x = shifted(outs[0], stage, stage + 1)
        if towers:
            x, tower = lax.optimization_barrier((x, outs[5]))
            k = shifted(tower, 0, stages - 1)

    g = cotangent[0, micro]
    returned = None
    for stage in reversed(range(stages)):
        last, first = stage == stages - 1, stage == 0
        outs = backward_stage(stage, last, first, flags, g, weights, par, states[stage], returned, e)
        e = outs[0]
        if stage > 0:
            g = shifted(outs[1], stage, stage - 1)
        if last:
            g, skip_grad = lax.optimization_barrier((g, outs[2]))
            returned = shifted(skip_grad, stages - 1, 0)
        if stage == stages - 2:
            h, e = lax.optimization_barrier((h, e))
            acts = jnp.concatenate([h[0]] + [traded(h, d, count) for d in range(1, GROUP)])
    errors = jnp.concatenate([e[0]] + [traded(e, d, count) for d in range(1, GROUP)])

    terms = lax.dot_general(acts, errors, (((0,), (0,)), ((), ())), preferred_element_type=jnp.float32)
    pieces = terms.astype(jnp.bfloat16).reshape(replicas, channels // replicas, channels)
    pieces = lax.all_to_all(pieces, "dp", 0, 0)
    factor = 1.0 / math.sqrt(replicas * MICROS * row_count)
    piece = jnp.sum(pieces.astype(jnp.float32), axis=0) * factor
    piece = jnp.broadcast_to(piece.astype(jnp.bfloat16)[None], pieces.shape)
    whole = lax.all_to_all(piece, "dp", 0, 0)
    return whole.reshape(1, channels, channels).astype(jnp.float32)


def solution(mesh):
    return jax.shard_map(
        shards,
        mesh=mesh,
        in_specs=(
            P("dp", None, None, None),
            P(),
            P("pipe", None, None),
            P("pipe", None, None),
            P("pipe", None),
            P("dp", None, None, None),
        ),
        out_specs=P("pipe", None, None),
        check_vma=False,
    )
```

time: 227 us -> 199 us (0.88)
  the two profiles are of different devices: /device:TPU:8 before, /device:TPU:128 now
where the time goes in v2:
time: 199 us
  blocking collectives  77.9 us (39%)
  waiting for transfers between devices  53.9 us (27%)
  starting transfers between devices  43.9 us (22%)
  Pallas kernels  13.6 us (7%)
  local copies, waits for them, and re-layouts  4.27 us (2%)
  other arithmetic  2.66 us (1%)
    all_to_all x1, blocking collectives, shards(): pieces = lax.all_to_all(pieces, 'dp', 0, 0)  42.1 us
    all_to_all x1, blocking collectives, shards(): whole = lax.all_to_all(piece, 'dp', 0, 0)  35.8 us
    ppermute x8, waiting for transfers between devices, shifted(): return lax.ppermute(block, 'pipe', pairs)  35.1 us
    ppermute x8, starting transfers between devices, swapped(): lax.ppermute(block, 'pipe', [(i, i ^ distance) for i in range(count)])  19.9 us
    ppermute x8, waiting for transfers between devices, swapped(): lax.ppermute(block, 'pipe', [(i, i ^ distance) for i in range(count)])  17.6 us
    ppermute x6, starting transfers between devices, traded(): return lax.ppermute(block[distance], 'pipe', pairs)  16.1 us
    ppermute x8, starting transfers between devices, shifted(): return lax.ppermute(block, 'pipe', pairs)  7.87 us
    pallas_call x4, Pallas kernels, forward_stage(): pl.pallas_call(functools.partial(forward_kernel, stage, skip, towers), ou...  5.2 us
  transfers between devices with their start and end apart: 22, of which 8 were waited for; matrix products, arithmetic and copies ran while one was open for 2% of the time, Pallas kernels for 5%

profile of v2, /device:TPU:128, one launch (start us, length us, event | category | flops | bytes accessed | tf_op | source)
XLA Modules:
  0.0 198.6 jit_solution(15079110152363040293)
XLA Ops:
  1.6 2.0 %collective-permute-start.5 = (f32[8,768]{1,0:T(8,128)S(1)}, f32[8,768]{1,0:T(8,128)S(1)}, u32[]{:S(2)}, u32[]{:S(2)}) collective-permute-start(f32[8,768]{1,0:T(8,128)S(1)} %maximum_maximum_fusion), channel_id=1, source_target_pairs={{0,1},{1,0},{2,3},{3,2},{4,5},{5,4},{6,7},{7,6},{8,9},{9,8},{10,11... | collective-permute-start | bytes 73736 | tf_op jit(solution)/shard_map/ppermute | solution.py:220
  3.6 4.3 %collective-permute-start.6 = (f32[8,768]{1,0:T(8,128)S(1)}, f32[8,768]{1,0:T(8,128)S(1)}, u32[]{:S(2)}, u32[]{:S(2)}) collective-permute-start(f32[8,768]{1,0:T(8,128)S(1)} %maximum_maximum_fusion), channel_id=1, source_target_pairs={{0,2},{1,3},{2,0},{3,1},{4,6},{5,7},{6,4},{7,5},{8,10},{9,11},{10,... | collective-permute-start | bytes 73736 | tf_op jit(solution)/shard_map/ppermute | solution.py:220
  7.9 2.3 %slice_bitcast_fusion = (bf16[384,768]{1,0:T(8,128)(2,1)}, bf16[384,768]{1,0:T(8,128)(2,1)}) fusion(bf16[1,768,768]{2,1,0:T(8,128)(2,1)} %param.8), kind=kLoop, calls=%fused_computation.4 | loop fusion | bytes 2359296 | tf_op jit(solution)/shard_map/slice | solution.py:288
  10.3 1.9 collective-permute-start
  12.2 3.9 %collective-permute-start.2 = (bf16[384,768]{1,0:T(8,128)(2,1)}, bf16[384,768]{1,0:T(8,128)(2,1)}, u32[]{:S(2)}, u32[]{:S(2)}) collective-permute-start(bf16[384,768]{1,0:T(8,128)(2,1)} %get-tuple-element.71), channel_id=1, source_target_pairs={{0,2},{1,3},{2,0},{3,1},{4,6},{5,7},{6,4},{7,5},{8,10},{9,11},{10,... | collective-permute-start | bytes 1769480 | tf_op jit(solution)/shard_map/ppermute | solution.py:220
  16.1 1.9 collective-permute-start.4
  19.0 1.2 convolution_convert_fusion.1.x_ref
  20.3 2.0 %collective-permute-start.7 = (f32[8,768]{1,0:T(8,128)S(1)}, f32[8,768]{1,0:T(8,128)S(1)}, u32[]{:S(2)}, u32[]{:S(2)}) collective-permute-start(f32[8,768]{1,0:T(8,128)S(1)} %maximum_maximum_fusion), channel_id=1, source_target_pairs={{0,3},{1,2},{2,1},{3,0},{4,7},{5,6},{6,5},{7,4},{8,11},{9,10},{10,... | collective-permute-start | bytes 73736 | tf_op jit(solution)/shard_map/ppermute | solution.py:220
  22.4 6.2 %collective-permute-done.rest_2_ = bf16[384,768]{1,0:T(8,128)(2,1)S(1)} collective-permute-done((bf16[384,768]{1,0:T(8,128)(2,1)}, bf16[384,768]{1,0:T(8,128)(2,1)S(1)}, u32[]{:S(2)}, u32[]{:S(2)}) %collective-permute-start) | collective-permute-done | bytes 589856 | tf_op jit(solution)/shard_map/ppermute | solution.py:220
  28.5 1.9 collective-permute-start.1
  30.4 10.4 %collective-permute-done.2.rest_0_ = bf16[384,768]{1,0:T(8,128)(2,1)} collective-permute-done((bf16[384,768]{1,0:T(8,128)(2,1)}, bf16[384,768]{1,0:T(8,128)(2,1)}, u32[]{:S(2)}, u32[]{:S(2)}) %collective-permute-start.2) | collective-permute-done | bytes 589856 | tf_op jit(solution)/shard_map/ppermute | solution.py:220
  40.8 1.9 collective-permute-start.3
  44.9 1.6 packed.4.rest_1_
  47.9 1.3 collective-permute-start.8
  49.2 7.4 %collective-permute-done.8.x_ref = bf16[64,768]{1,0:T(8,128)(2,1)S(1)} collective-permute-done((bf16[64,768]{1,0:T(8,128)(2,1)S(1)}, bf16[64,768]{1,0:T(8,128)(2,1)S(1)}, u32[]{:S(2)}, u32[]{:S(2)}) %collective-permute-start.8) | collective-permute-done | bytes 98336 | tf_op jit(solution)/shard_map/ppermute | solution.py:266
  57.2 2.7 %ahead1.1 = (bf16[64,768]{1,0:T(8,128)(2,1)S(1)}, f32[4,64,768]{2,1,0:T(8,128)S(1)}, f32[4,64,768]{2,1,0:T(8,128)S(1)}, f32[4,64,128]{2,1,0:T(8,128)S(1)}, bf16[4,64,768]{2,1,0:T(8,128)(2,1)S(1)}) custom-call(s32[2]{0:T(128)S(1)} %pad_add_fusion.flags, bf16[64,768]{1,0:T(8,128)(2,1)S(1)} %collective-permute-done.8.x_ref, ...), custom_call_target="tpu_custom_call", output_to_operand_aliasing={{4}: (4, {})} | custom-call | tf_op jit(solution)/shard_map/ahead1/pallas_call | solution.py:121
  60.0 1.3 collective-permute-start.9
  61.3 2.2 %collective-permute-done.9.x_ref = bf16[64,768]{1,0:T(8,128)(2,1)S(1)} collective-permute-done((bf16[64,768]{1,0:T(8,128)(2,1)S(1)}, bf16[64,768]{1,0:T(8,128)(2,1)S(1)}, u32[]{:S(2)}, u32[]{:S(2)}) %collective-permute-start.9) | collective-permute-done | bytes 98336 | tf_op jit(solution)/shard_map/ppermute | solution.py:266
  64.8 1.2 ahead3.1
  68.7 1.3 collective-permute-start.16
  70.0 25.6 %collective-permute-done.16.g_ref = bf16[64,768]{1,0:T(8,128)(2,1)S(1)} collective-permute-done((bf16[64,768]{1,0:T(8,128)(2,1)S(1)}, bf16[64,768]{1,0:T(8,128)(2,1)S(1)}, u32[]{:S(2)}, u32[]{:S(2)}) %collective-permute-start.16) | collective-permute-done | bytes 98336 | tf_op jit(solution)/shard_map/ppermute | solution.py:266
  95.6 3.2 %behind1.1 = (bf16[4,64,768]{2,1,0:T(8,128)(2,1)S(1)}, bf16[64,768]{1,0:T(8,128)(2,1)S(1)}) custom-call(s32[2]{0:T(128)S(1)} %pad_add_fusion.flags, bf16[64,768]{1,0:T(8,128)(2,1)S(1)} %collective-permute-done.16.g_ref, bf16[4,768,768]{2,1,0:T(8,128)(2,1)S(1)} %packed.5.w_ref, ...), custom_call_target="tpu_custom_call", output_to_operand_aliasing={{0}: (7, {})} | custom-call | tf_op jit(solution)/shard_map/behind1/pallas_call | solution.py:201
  98.8 1.3 collective-permute-start.17
  100.2 1.3 collective-permute-start.15
  101.5 5.1 %collective-permute-start.14 = (bf16[64,768]{1,0:T(8,128)(2,1)S(1)}, bf16[64,768]{1,0:T(8,128)(2,1)S(1)}, u32[]{:S(2)}, u32[]{:S(2)}) collective-permute-start(bf16[64,768]{1,0:T(8,128)(2,1)S(1)} %get-tuple-element.79), channel_id=1, source_target_pairs={{0,2},{1,3},{2,0},{4,6},{5,7},{6,4},{8,10},{9,11},{10,8},{12,14},{... | collective-permute-start | bytes 294920 | tf_op jit(solution)/shard_map/ppermute | solution.py:271
  106.5 1.9 collective-permute-start.13
  109.1 1.3 collective-permute-start.21
  110.4 4.7 %collective-permute-start.20 = (bf16[64,768]{1,0:T(8,128)(2,1)S(1)}, bf16[64,768]{1,0:T(8,128)(2,1)S(1)}, u32[]{:S(2)}, u32[]{:S(2)}) collective-permute-start(bf16[64,768]{1,0:T(8,128)(2,1)S(1)} %get-tuple-element.75), channel_id=1, source_target_pairs={{0,2},{1,3},{2,0},{4,6},{5,7},{6,4},{8,10},{9,11},{10,8},{12,14},{... | collective-permute-start | bytes 294920 | tf_op jit(solution)/shard_map/ppermute | solution.py:271
  115.1 1.9 collective-permute-start.19
  118.8 42.1 %all_to_all.10 = bf16[32,24,768]{2,1,0:T(8,128)(2,1)S(1)} all-to-all(bf16[32,24,768]{2,1,0:T(8,128)(2,1)S(1)} %bitcast.48), channel_id=1, replica_groups=mesh['dp'=32,'pipe'=16] {'dp'}, dimensions={0} | all-to-all | bytes 2359296 | tf_op jit(solution)/shard_map/all_to_all | solution.py:334
  161.2 35.8 %all_to_all.11 = bf16[32,24,768]{2,1,0:T(8,128)(2,1)S(1)} all-to-all(bf16[32,24,768]{2,1,0:T(8,128)(2,1)S(1)} %broadcast_in_dim.31), channel_id=1, replica_groups=mesh['dp'=32,'pipe'=16] {'dp'}, dimensions={0} | all-to-all | bytes 2359296 | tf_op jit(solution)/shard_map/all_to_all | solution.py:338
  197.0 1.6 bitcast_convert_fusion
  (57 shorter events, 13.3 us)
Async XLA Ops:
  0.0 64.8 %copy-start = (bf16[1,3,64,768]{3,2,1,0:T(8,128)(2,1)S(1)}, bf16[1,3,64,768]{3,2,1,0:T(8,128)(2,1)}, u32[]{:S(2)}) copy-start(bf16[1,3,64,768]{3,2,1,0:T(8,128)(2,1)} %param.11) | copy-start | bytes 884740
  1.6 14.5 %copy-start.1 = (bf16[1,768,768]{2,1,0:T(8,128)(2,1)S(1)}, bf16[1,768,768]{2,1,0:T(8,128)(2,1)}, u32[]{:S(2)}) copy-start(bf16[1,768,768]{2,1,0:T(8,128)(2,1)} %param.8) | copy-start | bytes 3538948
  1.6 16.5 %copy-start.2 = (f32[1,768]{1,0:T(1,128)S(1)}, f32[1,768]{1,0:T(1,128)}, u32[]{:S(2)}) copy-start(f32[1,768]{1,0:T(1,128)} %param.10) | copy-start | bytes 9220
  1.6 18.7 %collective-permute-start.5 = (f32[8,768]{1,0:T(8,128)S(1)}, f32[8,768]{1,0:T(8,128)S(1)}, u32[]{:S(2)}, u32[]{:S(2)}) collective-permute-start(f32[8,768]{1,0:T(8,128)S(1)} %maximum_maximum_fusion), channel_id=1, source_target_pairs={{0,1},{1,0},{2,3},{3,2},{4,5},{5,4},{6,7},{7,6},{8,9},{9,8},{10,11... | collective-permute-start | bytes 73736 | tf_op jit(solution)/shard_map/ppermute | solution.py:220
  3.6 39.1 %collective-permute-start.6 = (f32[8,768]{1,0:T(8,128)S(1)}, f32[8,768]{1,0:T(8,128)S(1)}, u32[]{:S(2)}, u32[]{:S(2)}) collective-permute-start(f32[8,768]{1,0:T(8,128)S(1)} %maximum_maximum_fusion), channel_id=1, source_target_pairs={{0,2},{1,3},{2,0},{3,1},{4,6},{5,7},{6,4},{7,5},{8,10},{9,11},{10,... | collective-permute-start | bytes 73736 | tf_op jit(solution)/shard_map/ppermute | solution.py:220
  10.3 18.3 %collective-permute-start = (bf16[384,768]{1,0:T(8,128)(2,1)}, bf16[384,768]{1,0:T(8,128)(2,1)S(1)}, u32[]{:S(2)}, u32[]{:S(2)}) collective-permute-start(bf16[384,768]{1,0:T(8,128)(2,1)} %get-tuple-element.72), channel_id=1, source_target_pairs={{0,2},{1,3},{2,0},{3,1},{4,6},{5,7},{6,4},{7,5},{8,10},{9,11},{10,... | collective-permute-start | bytes 1769480 | tf_op jit(solution)/shard_map/ppermute | solution.py:220
  12.2 28.6 %collective-permute-start.2 = (bf16[384,768]{1,0:T(8,128)(2,1)}, bf16[384,768]{1,0:T(8,128)(2,1)}, u32[]{:S(2)}, u32[]{:S(2)}) collective-permute-start(bf16[384,768]{1,0:T(8,128)(2,1)} %get-tuple-element.71), channel_id=1, source_target_pairs={{0,2},{1,3},{2,0},{3,1},{4,6},{5,7},{6,4},{7,5},{8,10},{9,11},{10,... | collective-permute-start | bytes 1769480 | tf_op jit(solution)/shard_map/ppermute | solution.py:220
  16.1 26.7 %collective-permute-start.4 = (bf16[768,768]{1,0:T(8,128)(2,1)S(1)}, bf16[768,768]{1,0:T(8,128)(2,1)S(1)}, u32[]{:S(2)}, u32[]{:S(2)}) collective-permute-start(bf16[768,768]{1,0:T(8,128)(2,1)S(1)} %bitcast.45), channel_id=1, source_target_pairs={{0,1},{1,0},{2,3},{3,2},{4,5},{5,4},{6,7},{7,6},{8,9},{9,8},{10,11... | collective-permute-start | bytes 3538952 | tf_op jit(solution)/shard_map/ppermute | solution.py:220
  20.3 22.4 %collective-permute-start.7 = (f32[8,768]{1,0:T(8,128)S(1)}, f32[8,768]{1,0:T(8,128)S(1)}, u32[]{:S(2)}, u32[]{:S(2)}) collective-permute-start(f32[8,768]{1,0:T(8,128)S(1)} %maximum_maximum_fusion), channel_id=1, source_target_pairs={{0,3},{1,2},{2,1},{3,0},{4,7},{5,6},{6,5},{7,4},{8,11},{9,10},{10,... | collective-permute-start | bytes 73736 | tf_op jit(solution)/shard_map/ppermute | solution.py:220
  28.5 18.0 %collective-permute-start.1 = (bf16[384,768]{1,0:T(8,128)(2,1)S(1)}, bf16[384,768]{1,0:T(8,128)(2,1)S(1)}, u32[]{:S(2)}, u32[]{:S(2)}) collective-permute-start(bf16[384,768]{1,0:T(8,128)(2,1)S(1)} %collective-permute-done.rest_2_), channel_id=1, source_target_pairs={{0,1},{1,0},{2,3},{3,2},{4,5},{5,4},{6,7},{7,6},{8,9},{9,8},{10,11... | collective-permute-start | bytes 1769480 | tf_op jit(solution)/shard_map/ppermute | solution.py:220
  40.8 4.1 %collective-permute-start.3 = (bf16[384,768]{1,0:T(8,128)(2,1)}, bf16[384,768]{1,0:T(8,128)(2,1)S(1)}, u32[]{:S(2)}, u32[]{:S(2)}) collective-permute-start(bf16[384,768]{1,0:T(8,128)(2,1)} %collective-permute-done.2.rest_0_), channel_id=1, source_target_pairs={{0,1},{1,0},{2,3},{3,2},{4,5},{5,4},{6,7},{7,6},{8,9},{9,8},{10,11... | collective-permute-start | bytes 1769480 | tf_op jit(solution)/shard_map/ppermute | solution.py:220
  47.9 8.7 %collective-permute-start.8 = (bf16[64,768]{1,0:T(8,128)(2,1)S(1)}, bf16[64,768]{1,0:T(8,128)(2,1)S(1)}, u32[]{:S(2)}, u32[]{:S(2)}) collective-permute-start(bf16[64,768]{1,0:T(8,128)(2,1)S(1)} %get-tuple-element.38), channel_id=1, source_target_pairs={{0,4},{1,5},{2,6},{16,20},{17,21},{18,22},{32,36},{33,37},{34,38},... | collective-permute-start | bytes 294920 | tf_op jit(solution)/shard_map/ppermute | solution.py:266
  56.6 8.3 %collective-permute-start.11 = (bf16[4,64,768]{2,1,0:T(8,128)(2,1)S(1)}, bf16[4,64,768]{2,1,0:T(8,128)(2,1)S(1)}, u32[]{:S(2)}, u32[]{:S(2)}) collective-permute-start(bf16[4,64,768]{2,1,0:T(8,128)(2,1)S(1)} %get-tuple-element.45), channel_id=1, source_target_pairs={{0,12},{1,13},{2,14},{16,28},{17,29},{18,30},{32,44},{33,45},{34,4... | collective-permute-start | bytes 1179656 | tf_op jit(solution)/shard_map/ppermute | solution.py:266
  60.0 3.5 %collective-permute-start.9 = (bf16[64,768]{1,0:T(8,128)(2,1)S(1)}, bf16[64,768]{1,0:T(8,128)(2,1)S(1)}, u32[]{:S(2)}, u32[]{:S(2)}) collective-permute-start(bf16[64,768]{1,0:T(8,128)(2,1)S(1)} %get-tuple-element.42), channel_id=1, source_target_pairs={{4,8},{5,9},{6,10},{20,24},{21,25},{22,26},{36,40},{37,41},{38,42}... | collective-permute-start | bytes 294920 | tf_op jit(solution)/shard_map/ppermute | solution.py:266
  64.1 0.7 collective-permute-start.10
  66.7 0.7 collective-permute-start.12
  67.4 41.1 %collective-permute-start.18 = (bf16[4,64,768]{2,1,0:T(8,128)(2,1)S(1)}, bf16[4,64,768]{2,1,0:T(8,128)(2,1)S(1)}, u32[]{:S(2)}, u32[]{:S(2)}) collective-permute-start(bf16[4,64,768]{2,1,0:T(8,128)(2,1)S(1)} %get-tuple-element.69), channel_id=1, source_target_pairs={{12,0},{13,1},{14,2},{28,16},{29,17},{30,18},{44,32},{45,33},{46,3... | collective-permute-start | bytes 1179656 | tf_op jit(solution)/shard_map/ppermute | solution.py:266
  68.7 26.9 %collective-permute-start.16 = (bf16[64,768]{1,0:T(8,128)(2,1)S(1)}, bf16[64,768]{1,0:T(8,128)(2,1)S(1)}, u32[]{:S(2)}, u32[]{:S(2)}) collective-permute-start(bf16[64,768]{1,0:T(8,128)(2,1)S(1)} %get-tuple-element.60), channel_id=1, source_target_pairs={{8,4},{9,5},{10,6},{24,20},{25,21},{26,22},{40,36},{41,37},{42,38}... | collective-permute-start | bytes 294920 | tf_op jit(solution)/shard_map/ppermute | solution.py:266
  98.8 9.6 %collective-permute-start.17 = (bf16[64,768]{1,0:T(8,128)(2,1)S(1)}, bf16[64,768]{1,0:T(8,128)(2,1)S(1)}, u32[]{:S(2)}, u32[]{:S(2)}) collective-permute-start(bf16[64,768]{1,0:T(8,128)(2,1)S(1)} %get-tuple-element.65), channel_id=1, source_target_pairs={{4,0},{5,1},{6,2},{20,16},{21,17},{22,18},{36,32},{37,33},{38,34},... | collective-permute-start | bytes 294920 | tf_op jit(solution)/shard_map/ppermute | solution.py:266
  100.2 14.9 %collective-permute-start.15 = (bf16[64,768]{1,0:T(8,128)(2,1)S(1)}, bf16[64,768]{1,0:T(8,128)(2,1)S(1)}, u32[]{:S(2)}, u32[]{:S(2)}) collective-permute-start(bf16[64,768]{1,0:T(8,128)(2,1)S(1)} %get-tuple-element.78), channel_id=1, source_target_pairs={{0,3},{1,2},{2,1},{4,7},{5,6},{6,5},{8,11},{9,10},{10,9},{12,15},{... | collective-permute-start | bytes 294920 | tf_op jit(solution)/shard_map/ppermute | solution.py:271
  101.5 15.6 %collective-permute-start.14 = (bf16[64,768]{1,0:T(8,128)(2,1)S(1)}, bf16[64,768]{1,0:T(8,128)(2,1)S(1)}, u32[]{:S(2)}, u32[]{:S(2)}) collective-permute-start(bf16[64,768]{1,0:T(8,128)(2,1)S(1)} %get-tuple-element.79), channel_id=1, source_target_pairs={{0,2},{1,3},{2,0},{4,6},{5,7},{6,4},{8,10},{9,11},{10,8},{12,14},{... | collective-permute-start | bytes 294920 | tf_op jit(solution)/shard_map/ppermute | solution.py:271
  106.5 10.5 %collective-permute-start.13 = (bf16[64,768]{1,0:T(8,128)(2,1)S(1)}, bf16[64,768]{1,0:T(8,128)(2,1)S(1)}, u32[]{:S(2)}, u32[]{:S(2)}) collective-permute-start(bf16[64,768]{1,0:T(8,128)(2,1)S(1)} %get-tuple-element.80), channel_id=1, source_target_pairs={{0,1},{1,0},{2,3},{4,5},{5,4},{6,7},{8,9},{9,8},{10,11},{12,13},{1... | collective-permute-start | bytes 294920 | tf_op jit(solution)/shard_map/ppermute | solution.py:271
  109.1 7.9 %collective-permute-start.21 = (bf16[64,768]{1,0:T(8,128)(2,1)S(1)}, bf16[64,768]{1,0:T(8,128)(2,1)S(1)}, u32[]{:S(2)}, u32[]{:S(2)}) collective-permute-start(bf16[64,768]{1,0:T(8,128)(2,1)S(1)} %get-tuple-element.74), channel_id=1, source_target_pairs={{0,3},{1,2},{2,1},{4,7},{5,6},{6,5},{8,11},{9,10},{10,9},{12,15},{... | collective-permute-start | bytes 294920 | tf_op jit(solution)/shard_map/ppermute | solution.py:271
  110.4 7.2 %collective-permute-start.20 = (bf16[64,768]{1,0:T(8,128)(2,1)S(1)}, bf16[64,768]{1,0:T(8,128)(2,1)S(1)}, u32[]{:S(2)}, u32[]{:S(2)}) collective-permute-start(bf16[64,768]{1,0:T(8,128)(2,1)S(1)} %get-tuple-element.75), channel_id=1, source_target_pairs={{0,2},{1,3},{2,0},{4,6},{5,7},{6,4},{8,10},{9,11},{10,8},{12,14},{... | collective-permute-start | bytes 294920 | tf_op jit(solution)/shard_map/ppermute | solution.py:271
  115.1 3.2 %collective-permute-start.19 = (bf16[64,768]{1,0:T(8,128)(2,1)S(1)}, bf16[64,768]{1,0:T(8,128)(2,1)S(1)}, u32[]{:S(2)}, u32[]{:S(2)}) collective-permute-start(bf16[64,768]{1,0:T(8,128)(2,1)S(1)} %get-tuple-element.76), channel_id=1, source_target_pairs={{0,1},{1,0},{2,3},{4,5},{5,4},{6,7},{8,9},{9,8},{10,11},{12,13},{1... | collective-permute-start | bytes 294920 | tf_op jit(solution)/shard_map/ppermute | solution.py:271

commit v3 on v2

--- a/solution.py
+++ b/solution.py
@@ -6,15 +6,17 @@
 from jax import lax
 from jax.experimental import pallas as pl
 from jax.experimental.pallas import tpu as pltpu
+from jax.sharding import Mesh
 from jax.sharding import PartitionSpec as P
 
 GROUP = 4
 MICROS = 3
 CHUNK = 256
+PIPE = ("g", "q")
 ANY = pl.BlockSpec(memory_space=pl.ANY)
 VM = pl.BlockSpec(memory_space=pltpu.VMEM)
 SM = pl.BlockSpec(memory_space=pltpu.SMEM)
-PARAMS = pltpu.CompilerParams(vmem_limit_bytes=24 * 1024 * 1024)
+PARAMS = pltpu.CompilerParams(vmem_limit_bytes=4 * 1024 * 1024)
 CUBIC = 0.044715
 SCALE = math.sqrt(2.0 / math.pi)
 
@@ -54,7 +56,6 @@
     def _():
         y = x_ref[...]
         for j in range(GROUP):
-            d = jnp.bitwise_xor(member, j)
             squares = None
             for cs in chunks_of(channels):
                 u = y[:, cs].astype(jnp.float32)
@@ -82,7 +83,7 @@
                     SCALE + (3.0 * SCALE * CUBIC) * v2
                 )
                 act = (v * half).astype(jnp.bfloat16)
-                hb[d, :, cs] = act
+                hb[j, :, cs] = act
                 part = jnp.dot(act, w_ref[j, cs, :], preferred_element_type=jnp.float32)
                 total = part if total is None else total + part
             y = (ub[...] + total).astype(jnp.bfloat16)
@@ -150,14 +151,14 @@
     def _():
         dx = g_ref[...]
         for j in reversed(range(GROUP)):
-            d = jnp.bitwise_xor(member, j)
             for cs in chunks_of(channels):
                 g = dx[:, cs].astype(jnp.float32)
                 if first:
                     g = g + k_ref[j, :, cs].astype(jnp.float32)
                 gb[:, cs] = g
             e = gb[...].astype(jnp.bfloat16)
-            eb[d] = e
+            for i in range(eb.shape[0]):
+                eb[i, j] = e[:, i * eb.shape[3] : (i + 1) * eb.shape[3]]
             if first and j == 0:
                 continue
             dots = None
@@ -193,7 +194,7 @@
         args.append(k)
     args.append(e)
     args = [flags] + held(*args)
-    out_shape = [kept(wide, bf)]
+    out_shape = [kept(e.shape, bf)]
     if not first:
         out_shape.append(kept((rows, channels), bf))
     if last:
@@ -216,8 +217,9 @@
     return jnp.dot(one_hot, embed_table, preferred_element_type=jnp.float32).astype(jnp.bfloat16)
 
 
-def swapped(block, distance, count):
-    return lax.ppermute(block, "pipe", [(i, i ^ distance) for i in range(count)])
+def swapped(block, distance):
+    pairs = [(i, i ^ distance) for i in range(lax.axis_size(PIPE))]
+    return lax.ppermute(block, PIPE, pairs)
 
 
 def pack_kernel(places, flags, *rest):
@@ -263,44 +265,59 @@
 
 def shifted(block, stage, to_stage):
     pairs = [(GROUP * stage + i, GROUP * to_stage + i) for i in range(MICROS)]
-    return lax.ppermute(block, "pipe", pairs)
-
-
-def traded(block, distance, count):
-    pairs = [(i, i ^ distance) for i in range(count) if i % GROUP < MICROS]
-    return lax.ppermute(block[distance], "pipe", pairs)
+    return lax.ppermute(block, PIPE, pairs)
+
+
+def gathered(h, member, across_count):
+    group = jnp.zeros(h.shape, h.dtype)
+    own = lax.dynamic_index_in_dim(h, member, 0, keepdims=True)
+    group = lax.dynamic_update_slice(group, own, (member, 0, 0))
+    for d in range(1, GROUP):
+        slot = jnp.bitwise_xor(member, d)
+        pairs = [(i, i ^ d) for i in range(lax.axis_size(PIPE)) if i % GROUP < MICROS]
+        sent = lax.dynamic_index_in_dim(h, slot, 0, keepdims=True)
+        group = lax.dynamic_update_slice(group, lax.ppermute(sent, PIPE, pairs), (slot, 0, 0))
+    group = group.reshape(1, -1, h.shape[2])
+    here = lax.axis_index("x")
+    acts = jnp.zeros((across_count,) + group.shape[1:], h.dtype)
+    acts = lax.dynamic_update_slice(acts, group, (here, 0, 0))
+    for shift in range(1, across_count):
+        pairs = [(i, (i + shift) % across_count) for i in range(across_count)]
+        slot = (here - shift) % across_count
+        acts = lax.dynamic_update_slice(acts, lax.ppermute(group, "x", pairs), (slot, 0, 0))
+    return acts.reshape(-1, h.shape[2])
 
 
 def shards(base_ids, embed_table, segment_weights, conv_taps, norm_gains, cotangent):
-    count = lax.axis_size("pipe")
-    replicas = lax.axis_size("dp")
-    stages = count // GROUP
-    position = lax.axis_index("pipe")
-    member = position % GROUP
-    flags = jnp.stack([position // GROUP, member]).astype(jnp.int32)
+    stages = lax.axis_size("g")
+    down, across_count = lax.axis_size("y"), lax.axis_size("x")
+    member = lax.axis_index("q")
+    flags = jnp.stack([lax.axis_index("g"), member]).astype(jnp.int32)
     micro = jnp.minimum(member, MICROS - 1)
     weight = segment_weights[0]
     channels = weight.shape[1]
     row_count = base_ids.shape[2]
-    half = channels // 2
-
+    block = channels // across_count
+    bf = jnp.bfloat16
+
+    across = swapped(weight, 2)
+    x = encode_bases(base_ids[0, micro], embed_table)
+    later, x = lax.optimization_barrier((weight, x))
+    beside = swapped(later, 1)
     own = jnp.concatenate([conv_taps[0], norm_gains, jnp.zeros((4, channels), jnp.float32)])
-    across = [swapped(weight[:half], 2, count), swapped(weight[half:], 2, count)]
-    beside = swapped(weight, 1, count)
+    own, beside = lax.optimization_barrier((own, beside))
     par = placed(
         jnp.zeros((GROUP,) + own.shape, jnp.float32),
-        [own] + [swapped(own, d, count) for d in range(1, GROUP)],
+        [own] + [swapped(own, d) for d in range(1, GROUP)],
         member,
     )
-    corner = [swapped(part, 1, count) for part in across]
     weights = packed(None, flags, [(0, 0, weight), (1, 0, beside)])
-    weights = packed(weights, flags, [(2, 0, across[0]), (3, 0, corner[0]), (2, half, across[1])])
-    weights = packed(weights, flags, [(3, half, corner[1])])
-
-    x = encode_bases(base_ids[0, micro], embed_table)
-    wide = (GROUP, row_count, channels)
-    h = jnp.zeros(wide, jnp.bfloat16)
-    e = jnp.zeros(wide, jnp.bfloat16)
+    across, weights, par, x = lax.optimization_barrier((across, weights, par, x))
+    corner = swapped(across, 1)
+    weights = packed(weights, flags, [(2, 0, across)])
+    weights = packed(weights, flags, [(3, 0, corner)])
+    h = jnp.zeros((GROUP, row_count, channels), bf)
+    e = jnp.zeros((across_count, GROUP, row_count, block), bf)
     states, k = [], None
     for stage in range(stages):
         skip, towers = stage == stages - 1, stage == 0
@@ -326,31 +343,36 @@
             returned = shifted(skip_grad, stages - 1, 0)
         if stage == stages - 2:
             h, e = lax.optimization_barrier((h, e))
-            acts = jnp.concatenate([h[0]] + [traded(h, d, count) for d in range(1, GROUP)])
-    errors = jnp.concatenate([e[0]] + [traded(e, d, count) for d in range(1, GROUP)])
-
-    terms = lax.dot_general(acts, errors, (((0,), (0,)), ((), ())), preferred_element_type=jnp.float32)
-    pieces = terms.astype(jnp.bfloat16).reshape(replicas, channels // replicas, channels)
-    pieces = lax.all_to_all(pieces, "dp", 0, 0)
-    factor = 1.0 / math.sqrt(replicas * MICROS * row_count)
-    piece = jnp.sum(pieces.astype(jnp.float32), axis=0) * factor
-    piece = jnp.broadcast_to(piece.astype(jnp.bfloat16)[None], pieces.shape)
-    whole = lax.all_to_all(piece, "dp", 0, 0)
-    return whole.reshape(1, channels, channels).astype(jnp.float32)
+            acts = gathered(h, member, across_count)
+        if stage == 1:
+            acts, e = lax.optimization_barrier((acts, e))
+    errors = lax.all_to_all(e.reshape(-1, row_count, block), ("x", "q"), 0, 0).reshape(-1, block)
+
+    turned = lax.dot_general(errors, acts, (((0,), (0,)), ((), ())), preferred_element_type=jnp.float32)
+    pieces = lax.all_to_all(turned.astype(bf).reshape(down, block // down, channels), "y", 0, 0)
+    factor = 1.0 / math.sqrt(down * across_count * MICROS * row_count)
+    piece = (jnp.sum(pieces.astype(jnp.float32), axis=0) * factor).astype(bf)
+    piece = jnp.broadcast_to(piece, (across_count * down,) + piece.shape)
+    whole = lax.all_to_all(piece, ("x", "y"), 0, 0).reshape(channels, channels)
+    return whole.T.astype(jnp.float32)[None]
 
 
 def solution(mesh):
+    replicas, _ = mesh.devices.shape
+    shape = (replicas // math.gcd(4, replicas), math.gcd(4, replicas), -1, GROUP)
+    grid = Mesh(mesh.devices.reshape(shape), ("y", "x", "g", "q"))
+    windows = P(("y", "x"), None, None, None)
     return jax.shard_map(
         shards,
-        mesh=mesh,
+        mesh=grid,
         in_specs=(
-            P("dp", None, None, None),
+            windows,
             P(),
-            P("pipe", None, None),
-            P("pipe", None, None),
-            P("pipe", None),
-            P("dp", None, None, None),
+            P(PIPE, None, None),
+            P(PIPE, None, None),
+            P(PIPE, None),
+            windows,
         ),
-        out_specs=P("pipe", None, None),
+        out_specs=P(PIPE, None, None),
         check_vma=False,
     )

time: 199 us -> 202 us (1.015)
  the two profiles are of different devices: /device:TPU:128 before, /device:TPU:8 now
where the time goes in v3:
time: 202 us; the launch traced here: 201 us
  blocking collectives  69.2 us (34%)
  waiting for transfers between devices  52.6 us (26%)
  starting transfers between devices  44.6 us (22%)
  local copies, waits for them, and re-layouts  18.1 us (9%)
  Pallas kernels  13.4 us (7%)
    all_to_all x1, blocking collectives, shards(): whole = lax.all_to_all(piece, ('x', 'y'), 0, 0).reshape(channels, channels)  35.7 us
    ppermute x8, waiting for transfers between devices, shifted(): return lax.ppermute(block, PIPE, pairs)  27.6 us
    all_to_all x1, blocking collectives, shards(): lax.all_to_all(turned.astype(bf).reshape(down, block // down, channels),...  18 us
    ppermute x6, waiting for transfers between devices, swapped(): return lax.ppermute(block, PIPE, pairs)  18 us
    ppermute x6, starting transfers between devices, swapped(): return lax.ppermute(block, PIPE, pairs)  15.8 us
    all_to_all x1, blocking collectives, shards(): lax.all_to_all(e.reshape(-1, row_count, block), ('x', 'q'), 0, 0)  15.5 us
    ppermute x8, starting transfers between devices, shifted(): return lax.ppermute(block, PIPE, pairs)  12.3 us
    ppermute x3, starting transfers between devices, gathered(): lax.ppermute(group, 'x', pairs)  11.4 us
  transfers between devices with their start and end apart: 20, of which 9 were waited for; matrix products, arithmetic and copies ran while one was open for 4% of the time, Pallas kernels for 2%

profile of v3, /device:TPU:8, one launch (start us, length us, event | category | flops | bytes accessed | tf_op | source)
XLA Modules:
  0.0 201.3 jit_solution(12560081368716314030)
XLA Ops:
  2.1 1.9 collective-permute-start.1
  4.0 4.3 %collective-permute-start = (bf16[768,768]{1,0:T(8,128)(2,1)}, bf16[768,768]{1,0:T(8,128)(2,1)S(1)}, u32[]{:S(2)}, u32[]{:S(2)}) collective-permute-start(bf16[768,768]{1,0:T(8,128)(2,1)} %bitcast.38), channel_id=1, source_target_pairs={{0,2},{1,3},{2,0},{3,1},{4,6},{5,7},{6,4},{7,5},{8,10},{9,11},{10,... | collective-permute-start | bytes 3538952 | tf_op jit(solution)/shard_map/ppermute | solution.py:222
  9.9 2.1 %collective-permute-start.2 = (f32[8,768]{1,0:T(8,128)S(1)}, f32[8,768]{1,0:T(8,128)S(1)}, u32[]{:S(2)}, u32[]{:S(2)}) collective-permute-start(f32[8,768]{1,0:T(8,128)S(1)} %maximum_maximum_fusion), channel_id=1, source_target_pairs={{0,1},{1,0},{2,3},{3,2},{4,5},{5,4},{6,7},{7,6},{8,9},{9,8},{10,11... | collective-permute-start | bytes 73736 | tf_op jit(solution)/shard_map/ppermute | solution.py:222
  12.0 2.2 %collective-permute-start.3 = (f32[8,768]{1,0:T(8,128)S(1)}, f32[8,768]{1,0:T(8,128)S(1)}, u32[]{:S(2)}, u32[]{:S(2)}) collective-permute-start(f32[8,768]{1,0:T(8,128)S(1)} %maximum_maximum_fusion), channel_id=1, source_target_pairs={{0,2},{1,3},{2,0},{3,1},{4,6},{5,7},{6,4},{7,5},{8,10},{9,11},{10,... | collective-permute-start | bytes 73736 | tf_op jit(solution)/shard_map/ppermute | solution.py:222
  14.2 3.3 %collective-permute-start.4 = (f32[8,768]{1,0:T(8,128)S(1)}, f32[8,768]{1,0:T(8,128)S(1)}, u32[]{:S(2)}, u32[]{:S(2)}) collective-permute-start(f32[8,768]{1,0:T(8,128)S(1)} %maximum_maximum_fusion), channel_id=1, source_target_pairs={{0,3},{1,2},{2,1},{3,0},{4,7},{5,6},{6,5},{7,4},{8,11},{9,10},{10,... | collective-permute-start | bytes 73736 | tf_op jit(solution)/shard_map/ppermute | solution.py:222
  19.9 15.9 %collective-permute-done.3 = f32[8,768]{1,0:T(8,128)S(1)} collective-permute-done((f32[8,768]{1,0:T(8,128)S(1)}, f32[8,768]{1,0:T(8,128)S(1)}, u32[]{:S(2)}, u32[]{:S(2)}) %collective-permute-start.3) | collective-permute-done | bytes 24608 | tf_op jit(solution)/shard_map/ppermute | solution.py:222
  36.0 2.0 %collective-permute-start.5 = (bf16[768,768]{1,0:T(8,128)(2,1)S(1)}, bf16[768,768]{1,0:T(8,128)(2,1)S(1)}, u32[]{:S(2)}, u32[]{:S(2)}) collective-permute-start(bf16[768,768]{1,0:T(8,128)(2,1)S(1)} %collective-permute-done.rest_0_), channel_id=1, source_target_pairs={{0,1},{1,0},{2,3},{3,2},{4,5},{5,4},{6,7},{7,6},{8,9},{9,8},{10,11... | collective-permute-start | bytes 3538952 | tf_op jit(solution)/shard_map/ppermute | solution.py:222
  38.8 1.9 collective-permute-done.5.rest_0_
  41.6 2.8 %ahead0.1 = (bf16[64,768]{1,0:T(8,128)(2,1)S(1)}, f32[4,64,768]{2,1,0:T(8,128)S(1)}, f32[4,64,768]{2,1,0:T(8,128)S(1)}, f32[4,64,128]{2,1,0:T(8,128)S(1)}, bf16[...) custom-call(s32[2]{0:T(128)S(1)} %pad_add_fusion.flags, ...), custom_call_target="tpu_custom_call", output_to_operand_aliasing={{4}: (4, {})} | custom-call | tf_op jit(solution)/shard_map/ahead0/pallas_call | solution.py:122
  44.3 3.9 %collective-permute-start.6 = (bf16[64,768]{1,0:T(8,128)(2,1)S(1)}, bf16[64,768]{1,0:T(8,128)(2,1)S(1)}, u32[]{:S(2)}, u32[]{:S(2)}) collective-permute-start(bf16[64,768]{1,0:T(8,128)(2,1)S(1)} %get-tuple-element.56), channel_id=1, source_target_pairs={{0,4},{1,5},{2,6},{16,20},{17,21},{18,22},{32,36},{33,37},{34,38},... | collective-permute-start | bytes 294920 | tf_op jit(solution)/shard_map/ppermute | solution.py:268
  48.3 2.3 %collective-permute-done.6.x_ref = bf16[64,768]{1,0:T(8,128)(2,1)S(1)} collective-permute-done((bf16[64,768]{1,0:T(8,128)(2,1)S(1)}, bf16[64,768]{1,0:T(8,128)(2,1)S(1)}, u32[]{:S(2)}, u32[]{:S(2)}) %collective-permute-start.6) | collective-permute-done | bytes 98336 | tf_op jit(solution)/shard_map/ppermute | solution.py:268
  50.6 2.5 %collective-permute-start.9 = (bf16[4,64,768]{2,1,0:T(8,128)(2,1)S(1)}, bf16[4,64,768]{2,1,0:T(8,128)(2,1)S(1)}, u32[]{:S(2)}, u32[]{:S(2)}) collective-permute-start(bf16[4,64,768]{2,1,0:T(8,128)(2,1)S(1)} %get-tuple-element.63), channel_id=1, source_target_pairs={{0,12},{1,13},{2,14},{16,28},{17,29},{18,30},{32,44},{33,45},{34,4... | collective-permute-start | bytes 1179656 | tf_op jit(solution)/shard_map/ppermute | solution.py:268
  55.8 10.2 %collective-permute-done.9.rest_0_ = bf16[4,64,768]{2,1,0:T(8,128)(2,1)S(1)} collective-permute-done((bf16[4,64,768]{2,1,0:T(8,128)(2,1)S(1)}, bf16[4,64,768]{2,1,0:T(8,128)(2,1)S(1)}, u32[]{:S(2)}, u32[]{:S(2)}) %collective-permute-start.9) | collective-permute-done | bytes 393248 | tf_op jit(solution)/shard_map/ppermute | solution.py:268
  72.1 1.9 collective-permute-start.14
  74.0 1.9 collective-permute-start.15
  75.9 1.3 collective-permute-start.16
  77.9 2.6 %collective-permute-done.15 = bf16[1,64,768]{2,1,0:T(8,128)(2,1)S(1)} collective-permute-done((bf16[1,64,768]{2,1,0:T(8,128)(2,1)S(1)}, bf16[1,64,768]{2,1,0:T(8,128)(2,1)S(1)}, u32[]{:S(2)}, u32[]{:S(2)}) %collective-permute-start.15) | collective-permute-done | bytes 98336 | tf_op jit(solution)/shard_map/ppermute | solution.py:279
  81.8 3.4 %collective-permute-start.17 = (bf16[1,256,768]{2,1,0:T(8,128)(2,1)}, bf16[1,256,768]{2,1,0:T(8,128)(2,1)}, u32[]{:S(2)}, u32[]{:S(2)}) collective-permute-start(bf16[1,256,768]{2,1,0:T(8,128)(2,1)} %bitcast.10), channel_id=1, source_target_pairs={{0,16},{16,32},{32,48},{48,0},{1,17},{17,33},{33,49},{49,1},{2,18}... | collective-permute-start | bytes 1179656 | tf_op jit(solution)/shard_map/ppermute | solution.py:287
  85.1 4.6 %collective-permute-start.18 = (bf16[1,256,768]{2,1,0:T(8,128)(2,1)}, bf16[1,256,768]{2,1,0:T(8,128)(2,1)}, u32[]{:S(2)}, u32[]{:S(2)}) collective-permute-start(bf16[1,256,768]{2,1,0:T(8,128)(2,1)} %bitcast.10), channel_id=1, source_target_pairs={{0,32},{16,48},{32,0},{48,16},{1,33},{17,49},{33,1},{49,17},{2,34}... | collective-permute-start | bytes 1179656 | tf_op jit(solution)/shard_map/ppermute | solution.py:287
  89.8 1.3 collective-permute-start.11
  91.1 3.3 %collective-permute-start.19 = (bf16[1,256,768]{2,1,0:T(8,128)(2,1)}, bf16[1,256,768]{2,1,0:T(8,128)(2,1)}, u32[]{:S(2)}, u32[]{:S(2)}) collective-permute-start(bf16[1,256,768]{2,1,0:T(8,128)(2,1)} %bitcast.10), channel_id=1, source_target_pairs={{0,48},{16,0},{32,16},{48,32},{1,49},{17,1},{33,17},{49,33},{2,50}... | collective-permute-start | bytes 1179656 | tf_op jit(solution)/shard_map/ppermute | solution.py:287
  94.5 1.3 collective-permute-start.13
  95.8 2.3 %copy-done.2 = bf16[4,768,768]{2,1,0:T(8,128)(2,1)S(1)} copy-done((bf16[4,768,768]{2,1,0:T(8,128)(2,1)S(1)}, bf16[4,768,768]{2,1,0:T(8,128)(2,1)}, u32[]{:S(2)}) %copy-start.2) | copy-done | bytes 4718616
  99.3 1.3 collective-permute-start.12
  102.9 3.5 %collective-permute-done.18 = bf16[1,256,768]{2,1,0:T(8,128)(2,1)} collective-permute-done((bf16[1,256,768]{2,1,0:T(8,128)(2,1)}, bf16[1,256,768]{2,1,0:T(8,128)(2,1)}, u32[]{:S(2)}, u32[]{:S(2)}) %collective-permute-start.18) | collective-permute-done | bytes 393248 | tf_op jit(solution)/shard_map/ppermute | solution.py:287
  109.3 15.1 %collective-permute-done.12.g_ref = bf16[64,768]{1,0:T(8,128)(2,1)S(1)} collective-permute-done((bf16[64,768]{1,0:T(8,128)(2,1)S(1)}, bf16[64,768]{1,0:T(8,128)(2,1)S(1)}, u32[]{:S(2)}, u32[]{:S(2)}) %collective-permute-start.12) | collective-permute-done | bytes 98336 | tf_op jit(solution)/shard_map/ppermute | solution.py:268
  124.4 2.3 %copy-done.3 = bf16[4,768,768]{2,1,0:T(8,128)(2,1)S(1)} copy-done((bf16[4,768,768]{2,1,0:T(8,128)(2,1)S(1)}, bf16[4,768,768]{2,1,0:T(8,128)(2,1)}, u32[]{:S(2)}) %copy-start.3) | copy-done | bytes 4718616
  126.7 2.5 %behind0.1 = bf16[4,4,64,192]{3,2,1,0:T(8,128)(2,1)S(1)} custom-call(s32[2]{0:T(128)S(1)} %pad_add_fusion.flags, bf16[64,768]{1,0:T(8,128)(2,1)S(1)} %collective-permute-done.12.g_ref, bf16[4,768,768]{2,1,0:T(8,128)(2,1)S(1)} %copy-done.3, f32[4,8,768]{2,1,0:T(8,128)S(1)} %bitcast_dynamic-update-slice_fusion.par_ref, ...), custom_call_target="tpu_custom_call", output_to_operand_aliasing={{}: (8, {})} | custom-call | tf_op jit(solution)/shard_map/behind0/pallas_call | solution.py:202
  129.2 15.5 %all_to_all.15 = bf16[16,64,192]{2,1,0:T(8,128)(2,1)S(1)} all-to-all(bf16[16,64,192]{2,1,0:T(8,128)(2,1)S(1)} %bitcast.36), channel_id=1, replica_groups=mesh['y'=8,'x'=4,'g'=4,'q'=4] {'x','q'}, dimensions={0} | all-to-all | bytes 786432 | tf_op jit(solution)/shard_map/all_to_all | solution.py:349
  145.2 18.0 %all_to_all.16 = bf16[8,24,768]{2,1,0:T(8,128)(2,1)S(1)} all-to-all(bf16[8,24,768]{2,1,0:T(8,128)(2,1)S(1)} %bitcast.42), channel_id=1, replica_groups=mesh['y'=8,'x'=4,'g'=4,'q'=4] {'y'}, dimensions={0} | all-to-all | bytes 589824 | tf_op jit(solution)/shard_map/all_to_all | solution.py:352
  163.4 35.7 %all_to_all.17 = bf16[32,24,768]{2,1,0:T(8,128)(2,1)S(1)} all-to-all(bf16[32,24,768]{2,1,0:T(8,128)(2,1)S(1)} %broadcast_in_dim.42), channel_id=1, replica_groups=mesh['y'=8,'x'=4,'g'=4,'q'=4] {'x','y'}, dimensions={0} | all-to-all | bytes 2359296 | tf_op jit(solution)/shard_map/all_to_all | solution.py:356
  199.3 2.0 copy.17
  (72 shorter events, 25.4 us)
Async XLA Ops:
  0.0 55.7 %copy-start = (bf16[1,3,64,768]{3,2,1,0:T(8,128)(2,1)S(1)}, bf16[1,3,64,768]{3,2,1,0:T(8,128)(2,1)}, u32[]{:S(2)}) copy-start(bf16[1,3,64,768]{3,2,1,0:T(8,128)(2,1)} %param.11) | copy-start | bytes 884740
  2.1 7.8 %collective-permute-start.1 = (bf16[768,768]{1,0:T(8,128)(2,1)}, bf16[768,768]{1,0:T(8,128)(2,1)S(1)}, u32[]{:S(2)}, u32[]{:S(2)}) collective-permute-start(bf16[768,768]{1,0:T(8,128)(2,1)} %bitcast.37), channel_id=1, source_target_pairs={{0,1},{1,0},{2,3},{3,2},{4,5},{5,4},{6,7},{7,6},{8,9},{9,8},{10,11... | collective-permute-start | bytes 3538952 | tf_op jit(solution)/shard_map/ppermute | solution.py:222
  4.0 32.0 %collective-permute-start = (bf16[768,768]{1,0:T(8,128)(2,1)}, bf16[768,768]{1,0:T(8,128)(2,1)S(1)}, u32[]{:S(2)}, u32[]{:S(2)}) collective-permute-start(bf16[768,768]{1,0:T(8,128)(2,1)} %bitcast.38), channel_id=1, source_target_pairs={{0,2},{1,3},{2,0},{3,1},{4,6},{5,7},{6,4},{7,5},{8,10},{9,11},{10,... | collective-permute-start | bytes 3538952 | tf_op jit(solution)/shard_map/ppermute | solution.py:222
  9.9 10.0 %collective-permute-start.2 = (f32[8,768]{1,0:T(8,128)S(1)}, f32[8,768]{1,0:T(8,128)S(1)}, u32[]{:S(2)}, u32[]{:S(2)}) collective-permute-start(f32[8,768]{1,0:T(8,128)S(1)} %maximum_maximum_fusion), channel_id=1, source_target_pairs={{0,1},{1,0},{2,3},{3,2},{4,5},{5,4},{6,7},{7,6},{8,9},{9,8},{10,11... | collective-permute-start | bytes 73736 | tf_op jit(solution)/shard_map/ppermute | solution.py:222
  12.0 23.8 %collective-permute-start.3 = (f32[8,768]{1,0:T(8,128)S(1)}, f32[8,768]{1,0:T(8,128)S(1)}, u32[]{:S(2)}, u32[]{:S(2)}) collective-permute-start(f32[8,768]{1,0:T(8,128)S(1)} %maximum_maximum_fusion), channel_id=1, source_target_pairs={{0,2},{1,3},{2,0},{3,1},{4,6},{5,7},{6,4},{7,5},{8,10},{9,11},{10,... | collective-permute-start | bytes 73736 | tf_op jit(solution)/shard_map/ppermute | solution.py:222
  14.2 21.7 %collective-permute-start.4 = (f32[8,768]{1,0:T(8,128)S(1)}, f32[8,768]{1,0:T(8,128)S(1)}, u32[]{:S(2)}, u32[]{:S(2)}) collective-permute-start(f32[8,768]{1,0:T(8,128)S(1)} %maximum_maximum_fusion), channel_id=1, source_target_pairs={{0,3},{1,2},{2,1},{3,0},{4,7},{5,6},{6,5},{7,4},{8,11},{9,10},{10,... | collective-permute-start | bytes 73736 | tf_op jit(solution)/shard_map/ppermute | solution.py:222
  17.5 1.3 copy-start.4
  36.0 4.7 %collective-permute-start.5 = (bf16[768,768]{1,0:T(8,128)(2,1)S(1)}, bf16[768,768]{1,0:T(8,128)(2,1)S(1)}, u32[]{:S(2)}, u32[]{:S(2)}) collective-permute-start(bf16[768,768]{1,0:T(8,128)(2,1)S(1)} %collective-permute-done.rest_0_), channel_id=1, source_target_pairs={{0,1},{1,0},{2,3},{3,2},{4,5},{5,4},{6,7},{7,6},{8,9},{9,8},{10,11... | collective-permute-start | bytes 3538952 | tf_op jit(solution)/shard_map/ppermute | solution.py:222
  41.5 27.8 %copy-start.1 = (bf16[4,768,768]{2,1,0:T(8,128)(2,1)}, bf16[4,768,768]{2,1,0:T(8,128)(2,1)S(1)}, u32[]{:S(2)}) copy-start(bf16[4,768,768]{2,1,0:T(8,128)(2,1)S(1)} %packed.5.w_ref) | copy-start | bytes 14155780
  44.3 9.4 %copy-start.5 = (f32[4,64,768]{2,1,0:T(8,128)}, f32[4,64,768]{2,1,0:T(8,128)S(1)}, u32[]{:S(2)}) copy-start(f32[4,64,768]{2,1,0:T(8,128)S(1)} %get-tuple-element.84.gp) | copy-start | bytes 2359300
  44.3 6.3 %collective-permute-start.6 = (bf16[64,768]{1,0:T(8,128)(2,1)S(1)}, bf16[64,768]{1,0:T(8,128)(2,1)S(1)}, u32[]{:S(2)}, u32[]{:S(2)}) collective-permute-start(bf16[64,768]{1,0:T(8,128)(2,1)S(1)} %get-tuple-element.56), channel_id=1, source_target_pairs={{0,4},{1,5},{2,6},{16,20},{17,21},{18,22},{32,36},{33,37},{34,38},... | collective-permute-start | bytes 294920 | tf_op jit(solution)/shard_map/ppermute | solution.py:268
  50.6 15.4 %collective-permute-start.9 = (bf16[4,64,768]{2,1,0:T(8,128)(2,1)S(1)}, bf16[4,64,768]{2,1,0:T(8,128)(2,1)S(1)}, u32[]{:S(2)}, u32[]{:S(2)}) collective-permute-start(bf16[4,64,768]{2,1,0:T(8,128)(2,1)S(1)} %get-tuple-element.63), channel_id=1, source_target_pairs={{0,12},{1,13},{2,14},{16,28},{17,29},{18,30},{32,44},{33,45},{34,4... | collective-permute-start | bytes 1179656 | tf_op jit(solution)/shard_map/ppermute | solution.py:268
  53.8 0.7 collective-permute-start.7
  55.1 0.7 collective-permute-start.8
  67.9 0.8 copy-start.7
  68.7 0.7 collective-permute-start.10
  72.1 5.2 %collective-permute-start.14 = (bf16[1,64,768]{2,1,0:T(8,128)(2,1)S(1)}, bf16[1,64,768]{2,1,0:T(8,128)(2,1)S(1)}, u32[]{:S(2)}, u32[]{:S(2)}) collective-permute-start(bf16[1,64,768]{2,1,0:T(8,128)(2,1)S(1)} %get-tuple-element.93), channel_id=1, source_target_pairs={{0,1},{1,0},{2,3},{4,5},{5,4},{6,7},{8,9},{9,8},{10,11},{12,13},{1... | collective-permute-start | bytes 294920 | tf_op jit(solution)/shard_map/ppermute | solution.py:279
  74.0 6.5 %collective-permute-start.15 = (bf16[1,64,768]{2,1,0:T(8,128)(2,1)S(1)}, bf16[1,64,768]{2,1,0:T(8,128)(2,1)S(1)}, u32[]{:S(2)}, u32[]{:S(2)}) collective-permute-start(bf16[1,64,768]{2,1,0:T(8,128)(2,1)S(1)} %get-tuple-element.92), channel_id=1, source_target_pairs={{0,2},{1,3},{2,0},{4,6},{5,7},{6,4},{8,10},{9,11},{10,8},{12,14},{... | collective-permute-start | bytes 294920 | tf_op jit(solution)/shard_map/ppermute | solution.py:279
  75.9 5.2 %collective-permute-start.16 = (bf16[1,64,768]{2,1,0:T(8,128)(2,1)S(1)}, bf16[1,64,768]{2,1,0:T(8,128)(2,1)S(1)}, u32[]{:S(2)}, u32[]{:S(2)}) collective-permute-start(bf16[1,64,768]{2,1,0:T(8,128)(2,1)S(1)} %get-tuple-element.91), channel_id=1, source_target_pairs={{0,3},{1,2},{2,1},{4,7},{5,6},{6,5},{8,11},{9,10},{10,9},{12,15},{... | collective-permute-start | bytes 294920 | tf_op jit(solution)/shard_map/ppermute | solution.py:279
  81.8 20.1 %collective-permute-start.17 = (bf16[1,256,768]{2,1,0:T(8,128)(2,1)}, bf16[1,256,768]{2,1,0:T(8,128)(2,1)}, u32[]{:S(2)}, u32[]{:S(2)}) collective-permute-start(bf16[1,256,768]{2,1,0:T(8,128)(2,1)} %bitcast.10), channel_id=1, source_target_pairs={{0,16},{16,32},{32,48},{48,0},{1,17},{17,33},{33,49},{49,1},{2,18}... | collective-permute-start | bytes 1179656 | tf_op jit(solution)/shard_map/ppermute | solution.py:287
  85.1 21.3 %collective-permute-start.18 = (bf16[1,256,768]{2,1,0:T(8,128)(2,1)}, bf16[1,256,768]{2,1,0:T(8,128)(2,1)}, u32[]{:S(2)}, u32[]{:S(2)}) collective-permute-start(bf16[1,256,768]{2,1,0:T(8,128)(2,1)} %bitcast.10), channel_id=1, source_target_pairs={{0,32},{16,48},{32,0},{48,16},{1,33},{17,49},{33,1},{49,17},{2,34}... | collective-permute-start | bytes 1179656 | tf_op jit(solution)/shard_map/ppermute | solution.py:287
  89.8 6.0 %collective-permute-start.11 = (bf16[64,768]{1,0:T(8,128)(2,1)}, bf16[64,768]{1,0:T(8,128)(2,1)}, u32[]{:S(2)}, u32[]{:S(2)}) collective-permute-start(bf16[64,768]{1,0:T(8,128)(2,1)} %get-tuple-element.75), channel_id=1, source_target_pairs={{8,4},{9,5},{10,6},{24,20},{25,21},{26,22},{40,36},{41,37},{42,38}... | collective-permute-start | bytes 294920 | tf_op jit(solution)/shard_map/ppermute | solution.py:268
  91.1 17.2 %collective-permute-start.19 = (bf16[1,256,768]{2,1,0:T(8,128)(2,1)}, bf16[1,256,768]{2,1,0:T(8,128)(2,1)}, u32[]{:S(2)}, u32[]{:S(2)}) collective-permute-start(bf16[1,256,768]{2,1,0:T(8,128)(2,1)} %bitcast.10), channel_id=1, source_target_pairs={{0,48},{16,0},{32,16},{48,32},{1,49},{17,1},{33,17},{49,33},{2,50}... | collective-permute-start | bytes 1179656 | tf_op jit(solution)/shard_map/ppermute | solution.py:287
  94.5 29.9 %collective-permute-start.13 = (bf16[4,64,768]{2,1,0:T(8,128)(2,1)}, bf16[4,64,768]{2,1,0:T(8,128)(2,1)S(1)}, u32[]{:S(2)}, u32[]{:S(2)}) collective-permute-start(bf16[4,64,768]{2,1,0:T(8,128)(2,1)} %copy-done.7), channel_id=1, source_target_pairs={{12,0},{13,1},{14,2},{28,16},{29,17},{30,18},{44,32},{45,33},{46,3... | collective-permute-start | bytes 1179656 | tf_op jit(solution)/shard_map/ppermute | solution.py:268
  95.8 2.3 %copy-start.2 = (bf16[4,768,768]{2,1,0:T(8,128)(2,1)S(1)}, bf16[4,768,768]{2,1,0:T(8,128)(2,1)}, u32[]{:S(2)}) copy-start(bf16[4,768,768]{2,1,0:T(8,128)(2,1)} %copy-done.1) | copy-start | bytes 14155780
  99.3 25.0 %collective-permute-start.12 = (bf16[64,768]{1,0:T(8,128)(2,1)S(1)}, bf16[64,768]{1,0:T(8,128)(2,1)S(1)}, u32[]{:S(2)}, u32[]{:S(2)}) collective-permute-start(bf16[64,768]{1,0:T(8,128)(2,1)S(1)} %get-tuple-element.82), channel_id=1, source_target_pairs={{4,0},{5,1},{6,2},{20,16},{21,17},{22,18},{36,32},{37,33},{38,34},... | collective-permute-start | bytes 294920 | tf_op jit(solution)/shard_map/ppermute | solution.py:268
  100.7 23.6 %copy-start.6 = (f32[4,64,768]{2,1,0:T(8,128)S(1)}, f32[4,64,768]{2,1,0:T(8,128)}, u32[]{:S(2)}) copy-start(f32[4,64,768]{2,1,0:T(8,128)} %copy-done.5) | copy-start | bytes 2359300
  124.4 2.3 %copy-start.3 = (bf16[4,768,768]{2,1,0:T(8,128)(2,1)S(1)}, bf16[4,768,768]{2,1,0:T(8,128)(2,1)}, u32[]{:S(2)}) copy-start(bf16[4,768,768]{2,1,0:T(8,128)(2,1)} %copy-done.1) | copy-start | bytes 14155780

commit v4 on v3

--- a/solution.py
+++ b/solution.py
@@ -56,6 +56,7 @@
     def _():
         y = x_ref[...]
         for j in range(GROUP):
+            d = jnp.bitwise_xor(member, j)
             squares = None
             for cs in chunks_of(channels):
                 u = y[:, cs].astype(jnp.float32)
@@ -83,7 +84,7 @@
                     SCALE + (3.0 * SCALE * CUBIC) * v2
                 )
                 act = (v * half).astype(jnp.bfloat16)
-                hb[j, :, cs] = act
+                hb[d, :, cs] = act
                 part = jnp.dot(act, w_ref[j, cs, :], preferred_element_type=jnp.float32)
                 total = part if total is None else total + part
             y = (ub[...] + total).astype(jnp.bfloat16)
@@ -268,56 +269,81 @@
     return lax.ppermute(block, PIPE, pairs)
 
 
-def gathered(h, member, across_count):
-    group = jnp.zeros(h.shape, h.dtype)
-    own = lax.dynamic_index_in_dim(h, member, 0, keepdims=True)
-    group = lax.dynamic_update_slice(group, own, (member, 0, 0))
+def traded(h):
+    parts = [h[:1]]
     for d in range(1, GROUP):
-        slot = jnp.bitwise_xor(member, d)
         pairs = [(i, i ^ d) for i in range(lax.axis_size(PIPE)) if i % GROUP < MICROS]
-        sent = lax.dynamic_index_in_dim(h, slot, 0, keepdims=True)
-        group = lax.dynamic_update_slice(group, lax.ppermute(sent, PIPE, pairs), (slot, 0, 0))
-    group = group.reshape(1, -1, h.shape[2])
-    here = lax.axis_index("x")
-    acts = jnp.zeros((across_count,) + group.shape[1:], h.dtype)
-    acts = lax.dynamic_update_slice(acts, group, (here, 0, 0))
-    for shift in range(1, across_count):
-        pairs = [(i, (i + shift) % across_count) for i in range(across_count)]
-        slot = (here - shift) % across_count
-        acts = lax.dynamic_update_slice(acts, lax.ppermute(group, "x", pairs), (slot, 0, 0))
-    return acts.reshape(-1, h.shape[2])
+        parts.append(lax.ppermute(h[d : d + 1], PIPE, pairs))
+    return parts
+
+
+def beside(group, count):
+    if count == 1:
+        return [group]
+    return [group, lax.ppermute(group, "xl", [(i, i ^ 1) for i in range(count)])]
+
+
+def term_kernel(places, errors, *rest):
+    acts, out, ordered = rest[:-2], rest[-2], rest[-1]
+    rows = errors.shape[1]
+    total = None
+    for shift, part in enumerate(acts):
+        source = jnp.bitwise_xor(places[0], shift) * GROUP
+        for d in range(GROUP):
+            ordered[d * rows : (d + 1) * rows] = errors[source + jnp.bitwise_xor(places[1], d)]
+        term = lax.dot_general(
+            ordered[...],
+            part[...].reshape(GROUP * rows, part.shape[2]),
+            (((0,), (0,)), ((), ())),
+            preferred_element_type=jnp.float32,
+        )
+        total = term if total is None else total + term
+    out[...] = total.astype(out.dtype)
+
+
+def gradient_block(places, errors, acts):
+    args = held(errors, *acts)
+    return pl.pallas_call(
+        term_kernel,
+        out_shape=kept((errors.shape[2], acts[0].shape[2]), jnp.bfloat16),
+        in_specs=[SM] + [VM] * len(args),
+        out_specs=VM,
+        scratch_shapes=[pltpu.VMEM((GROUP * errors.shape[1], errors.shape[2]), jnp.bfloat16)],
+        compiler_params=PARAMS,
+        name="terms",
+    )(places, *args)
 
 
 def shards(base_ids, embed_table, segment_weights, conv_taps, norm_gains, cotangent):
     stages = lax.axis_size("g")
-    down, across_count = lax.axis_size("y"), lax.axis_size("x")
+    pair, rest = lax.axis_size("xl"), lax.axis_size("xh") * lax.axis_size("y")
     member = lax.axis_index("q")
     flags = jnp.stack([lax.axis_index("g"), member]).astype(jnp.int32)
     micro = jnp.minimum(member, MICROS - 1)
     weight = segment_weights[0]
     channels = weight.shape[1]
     row_count = base_ids.shape[2]
-    block = channels // across_count
+    block = channels // pair
     bf = jnp.bfloat16
 
     across = swapped(weight, 2)
     x = encode_bases(base_ids[0, micro], embed_table)
     later, x = lax.optimization_barrier((weight, x))
-    beside = swapped(later, 1)
+    core_weight = swapped(later, 1)
     own = jnp.concatenate([conv_taps[0], norm_gains, jnp.zeros((4, channels), jnp.float32)])
-    own, beside = lax.optimization_barrier((own, beside))
+    own, core_weight = lax.optimization_barrier((own, core_weight))
     par = placed(
         jnp.zeros((GROUP,) + own.shape, jnp.float32),
         [own] + [swapped(own, d) for d in range(1, GROUP)],
         member,
     )
-    weights = packed(None, flags, [(0, 0, weight), (1, 0, beside)])
+    weights = packed(None, flags, [(0, 0, weight), (1, 0, core_weight)])
     across, weights, par, x = lax.optimization_barrier((across, weights, par, x))
     corner = swapped(across, 1)
     weights = packed(weights, flags, [(2, 0, across)])
     weights = packed(weights, flags, [(3, 0, corner)])
     h = jnp.zeros((GROUP, row_count, channels), bf)
-    e = jnp.zeros((across_count, GROUP, row_count, block), bf)
+    e = jnp.zeros((pair, GROUP, row_count, block), bf)
     states, k = [], None
     for stage in range(stages):
         skip, towers = stage == stages - 1, stage == 0
@@ -343,25 +369,29 @@
             returned = shifted(skip_grad, stages - 1, 0)
         if stage == stages - 2:
             h, e = lax.optimization_barrier((h, e))
-            acts = gathered(h, member, across_count)
+            group = jnp.concatenate(traded(h))
         if stage == 1:
-            acts, e = lax.optimization_barrier((acts, e))
-    errors = lax.all_to_all(e.reshape(-1, row_count, block), ("x", "q"), 0, 0).reshape(-1, block)
-
-    turned = lax.dot_general(errors, acts, (((0,), (0,)), ((), ())), preferred_element_type=jnp.float32)
-    pieces = lax.all_to_all(turned.astype(bf).reshape(down, block // down, channels), "y", 0, 0)
-    factor = 1.0 / math.sqrt(down * across_count * MICROS * row_count)
+            group, e = lax.optimization_barrier((group, e))
+    acts = beside(group, pair)
+    errors = lax.all_to_all(e.reshape(-1, row_count, block), ("xl", "q"), 0, 0)
+    places = jnp.stack([lax.axis_index("xl"), member]).astype(jnp.int32)
+    turned = gradient_block(places, errors, acts)
+
+    pieces = lax.all_to_all(turned.reshape(rest, block // rest, channels), ("xh", "y"), 0, 0)
+    factor = 1.0 / math.sqrt(pair * rest * MICROS * row_count)
     piece = (jnp.sum(pieces.astype(jnp.float32), axis=0) * factor).astype(bf)
-    piece = jnp.broadcast_to(piece, (across_count * down,) + piece.shape)
-    whole = lax.all_to_all(piece, ("x", "y"), 0, 0).reshape(channels, channels)
+    piece = jnp.broadcast_to(piece, (pair * rest,) + piece.shape)
+    whole = lax.all_to_all(piece, ("xl", "xh", "y"), 0, 0).reshape(channels, channels)
     return whole.T.astype(jnp.float32)[None]
 
 
 def solution(mesh):
     replicas, _ = mesh.devices.shape
-    shape = (replicas // math.gcd(4, replicas), math.gcd(4, replicas), -1, GROUP)
-    grid = Mesh(mesh.devices.reshape(shape), ("y", "x", "g", "q"))
-    windows = P(("y", "x"), None, None, None)
+    low = math.gcd(2, replicas)
+    high = math.gcd(2, replicas // low)
+    shape = (replicas // (low * high), high, low, -1, GROUP)
+    grid = Mesh(mesh.devices.reshape(shape), ("y", "xh", "xl", "g", "q"))
+    windows = P(("y", "xh", "xl"), None, None, None)
     return jax.shard_map(
         shards,
         mesh=grid,

time: 202 us -> 197 us (0.975)
  the two profiles are of different devices: /device:TPU:8 before, /device:TPU:64 now
where the time goes in v4:
time: 197 us; the launch traced here: 196 us
  blocking collectives  64.1 us (33%)
  waiting for transfers between devices  60.6 us (31%)
  starting transfers between devices  44.8 us (23%)
  Pallas kernels  18.2 us (9%)
  local copies, waits for them, and re-layouts  5.82 us (3%)
    all_to_all x1, blocking collectives, shards(): lax.all_to_all(piece, ('xl', 'xh', 'y'), 0, 0).reshape(channels, channels)  35.6 us
    ppermute x8, waiting for transfers between devices, shifted(): return lax.ppermute(block, PIPE, pairs)  30.7 us
    all_to_all x1, blocking collectives, shards(): lax.all_to_all(turned.reshape(rest, block // rest, channels), ('xh', 'y')...  28.5 us
    ppermute x6, starting transfers between devices, swapped(): return lax.ppermute(block, PIPE, pairs)  18.4 us
    ppermute x6, waiting for transfers between devices, swapped(): return lax.ppermute(block, PIPE, pairs)  18 us
    ppermute x3, starting transfers between devices, traded(): parts.append(lax.ppermute(h[d:d + 1], PIPE, pairs))  11.9 us
    ppermute x1, waiting for transfers between devices, beside(): lax.ppermute(group, 'xl', [(i, i ^ 1) for i in range(count)])  11.9 us
    pallas_call x4, Pallas kernels, backward_stage(): pl.pallas_call(functools.partial(backward_kernel, stage, last, first), ou...  9.25 us
  transfers between devices with their start and end apart: 19, of which 7 were waited for; matrix products, arithmetic and copies ran while one was open for 1% of the time, Pallas kernels for 3%

profile of v4, /device:TPU:64, one launch (start us, length us, event | category | flops | bytes accessed | tf_op | source)
XLA Modules:
  0.0 196.4 jit_solution(9286325541668058799)
XLA Ops:
  0.9 1.2 convolution_convert_fusion.x_ref
  2.1 1.9 collective-permute-start.1
  4.0 6.9 %collective-permute-start = (bf16[768,768]{1,0:T(8,128)(2,1)}, bf16[768,768]{1,0:T(8,128)(2,1)S(1)}, u32[]{:S(2)}, u32[]{:S(2)}) collective-permute-start(bf16[768,768]{1,0:T(8,128)(2,1)} %bitcast.32), channel_id=1, source_target_pairs={{0,2},{1,3},{2,0},{3,1},{4,6},{5,7},{6,4},{7,5},{8,10},{9,11},{10,... | collective-permute-start | bytes 3538952 | tf_op jit(solution)/shard_map/ppermute | solution.py:223
  12.6 2.1 %collective-permute-start.2 = (f32[8,768]{1,0:T(8,128)S(1)}, f32[8,768]{1,0:T(8,128)S(1)}, u32[]{:S(2)}, u32[]{:S(2)}) collective-permute-start(f32[8,768]{1,0:T(8,128)S(1)} %maximum_maximum_fusion), channel_id=1, source_target_pairs={{0,1},{1,0},{2,3},{3,2},{4,5},{5,4},{6,7},{7,6},{8,9},{9,8},{10,11... | collective-permute-start | bytes 73736 | tf_op jit(solution)/shard_map/ppermute | solution.py:223
  14.7 2.2 %collective-permute-start.3 = (f32[8,768]{1,0:T(8,128)S(1)}, f32[8,768]{1,0:T(8,128)S(1)}, u32[]{:S(2)}, u32[]{:S(2)}) collective-permute-start(f32[8,768]{1,0:T(8,128)S(1)} %maximum_maximum_fusion), channel_id=1, source_target_pairs={{0,2},{1,3},{2,0},{3,1},{4,6},{5,7},{6,4},{7,5},{8,10},{9,11},{10,... | collective-permute-start | bytes 73736 | tf_op jit(solution)/shard_map/ppermute | solution.py:223
  16.9 3.3 %collective-permute-start.4 = (f32[8,768]{1,0:T(8,128)S(1)}, f32[8,768]{1,0:T(8,128)S(1)}, u32[]{:S(2)}, u32[]{:S(2)}) collective-permute-start(f32[8,768]{1,0:T(8,128)S(1)} %maximum_maximum_fusion), channel_id=1, source_target_pairs={{0,3},{1,2},{2,1},{3,0},{4,7},{5,6},{6,5},{7,4},{8,11},{9,10},{10,... | collective-permute-start | bytes 73736 | tf_op jit(solution)/shard_map/ppermute | solution.py:223
  20.2 1.3 copy-done.1
  22.6 15.9 %collective-permute-done.3 = f32[8,768]{1,0:T(8,128)S(1)} collective-permute-done((f32[8,768]{1,0:T(8,128)S(1)}, f32[8,768]{1,0:T(8,128)S(1)}, u32[]{:S(2)}, u32[]{:S(2)}) %collective-permute-start.3) | collective-permute-done | bytes 24608 | tf_op jit(solution)/shard_map/ppermute | solution.py:223
  38.6 2.0 %collective-permute-start.5 = (bf16[768,768]{1,0:T(8,128)(2,1)S(1)}, bf16[768,768]{1,0:T(8,128)(2,1)S(1)}, u32[]{:S(2)}, u32[]{:S(2)}) collective-permute-start(bf16[768,768]{1,0:T(8,128)(2,1)S(1)} %collective-permute-done.rest_0_), channel_id=1, source_target_pairs={{0,1},{1,0},{2,3},{3,2},{4,5},{5,4},{6,7},{7,6},{8,9},{9,8},{10,11... | collective-permute-start | bytes 3538952 | tf_op jit(solution)/shard_map/ppermute | solution.py:223
  41.5 1.9 collective-permute-done.5.rest_0_
  44.2 2.8 %ahead0.1 = (bf16[64,768]{1,0:T(8,128)(2,1)S(1)}, f32[4,64,768]{2,1,0:T(8,128)S(1)}, f32[4,64,768]{2,1,0:T(8,128)S(1)}, f32[4,64,128]{2,1,0:T(8,128)S(1)}, bf16[...) custom-call(s32[2]{0:T(128)S(1)} %pad_add_fusion.1.flags, ...), custom_call_target="tpu_custom_call", output_to_operand_aliasing={{4}: (4, {})} | custom-call | tf_op jit(solution)/shard_map/ahead0/pallas_call | solution.py:123
  47.0 1.3 collective-permute-start.6
  48.3 4.3 %collective-permute-done.6.x_ref = bf16[64,768]{1,0:T(8,128)(2,1)S(1)} collective-permute-done((bf16[64,768]{1,0:T(8,128)(2,1)S(1)}, bf16[64,768]{1,0:T(8,128)(2,1)S(1)}, u32[]{:S(2)}, u32[]{:S(2)}) %collective-permute-start.6) | collective-permute-done | bytes 98336 | tf_op jit(solution)/shard_map/ppermute | solution.py:269
  52.5 1.3 collective-permute-start.9
  56.5 2.7 %collective-permute-done.9.rest_0_ = bf16[4,64,768]{2,1,0:T(8,128)(2,1)S(1)} collective-permute-done((bf16[4,64,768]{2,1,0:T(8,128)(2,1)S(1)}, bf16[4,64,768]{2,1,0:T(8,128)(2,1)S(1)}, u32[]{:S(2)}, u32[]{:S(2)}) %collective-permute-start.9) | collective-permute-done | bytes 393248 | tf_op jit(solution)/shard_map/ppermute | solution.py:269
  59.1 1.2 ahead3.1
  61.2 1.8 behind3.1
  63.6 1.8 behind2.1
  66.1 1.3 collective-permute-start.13
  67.4 8.0 %collective-permute-start.16 = (bf16[1,64,768]{2,1,0:T(8,128)(2,1)S(1)}, bf16[1,64,768]{2,1,0:T(8,128)(2,1)S(1)}, u32[]{:S(2)}, u32[]{:S(2)}) collective-permute-start(bf16[1,64,768]{2,1,0:T(8,128)(2,1)S(1)} %get-tuple-element.92), channel_id=1, source_target_pairs={{0,3},{1,2},{2,1},{4,7},{5,6},{6,5},{8,11},{9,10},{10,9},{12,15},{... | collective-permute-start | bytes 294920 | tf_op jit(solution)/shard_map/ppermute | solution.py:276
  75.4 2.6 %collective-permute-start.15 = (bf16[1,64,768]{2,1,0:T(8,128)(2,1)S(1)}, bf16[1,64,768]{2,1,0:T(8,128)(2,1)S(1)}, u32[]{:S(2)}, u32[]{:S(2)}) collective-permute-start(bf16[1,64,768]{2,1,0:T(8,128)(2,1)S(1)} %get-tuple-element.93), channel_id=1, source_target_pairs={{0,2},{1,3},{2,0},{4,6},{5,7},{6,4},{8,10},{9,11},{10,8},{12,14},{... | collective-permute-start | bytes 294920 | tf_op jit(solution)/shard_map/ppermute | solution.py:276
  78.1 1.3 collective-permute-start.14
  79.4 2.0 %behind1.1 = (bf16[2,4,64,384]{3,2,1,0:T(8,128)(2,1)}, bf16[64,768]{1,0:T(8,128)(2,1)S(1)}) custom-call(s32[2]{0:T(128)S(1)} %pad_add_fusion.1.flags, bf16[64,768]{1,0:T(8,128)(2,1)S(1)} %collective-permute-done.11.g_ref, bf16[4,768,768]{2,1,0:T(8,128)(2,1)S(1)} %packed.5.w_ref, ...), custom_call_target="tpu_custom_call", output_to_operand_aliasing={{0}: (7, {})} | custom-call | tf_op jit(solution)/shard_map/behind1/pallas_call | solution.py:203
  81.4 1.3 collective-permute-start.12
  82.7 23.8 %collective-permute-done.12.g_ref = bf16[64,768]{1,0:T(8,128)(2,1)S(1)} collective-permute-done((bf16[64,768]{1,0:T(8,128)(2,1)S(1)}, bf16[64,768]{1,0:T(8,128)(2,1)S(1)}, u32[]{:S(2)}, u32[]{:S(2)}) %collective-permute-start.12) | collective-permute-done | bytes 98336 | tf_op jit(solution)/shard_map/ppermute | solution.py:269
  106.5 3.7 %behind0.1 = bf16[2,4,64,384]{3,2,1,0:T(8,128)(2,1)} custom-call(s32[2]{0:T(128)S(1)} %pad_add_fusion.1.flags, bf16[64,768]{1,0:T(8,128)(2,1)S(1)} %collective-permute-done.12.g_ref, bf16[4,768,768]{2,1,0:T(8,128)(2,1)S(1)} %packed.5.w_ref, f32[4,8,768]{2,1,0:T(8,128)S(1)} %bitcast_dynamic-update-slice_fusion.par_ref, ...), custom_call_target="tpu_custom_call", output_to_operand_aliasing={{}: (8, {})} | custom-call | tf_op jit(solution)/shard_map/behind0/pallas_call | solution.py:203
  110.2 3.4 %all-to-all-start = ((bf16[8,64,384]{2,1,0:T(8,128)(2,1)}), bf16[8,64,384]{2,1,0:T(8,128)(2,1)S(1)}, u32[]{:S(2)}, u32[]{:S(2)}) async-start(bf16[8,64,384]{2,1,0:T(8,128)(2,1)} %bitcast.11), calls=%async_computation | async-start | bytes 786432 | tf_op jit(solution)/shard_map/all_to_all | solution.py:376
  113.6 3.2 %collective-permute-start.17 = (bf16[4,64,768]{2,1,0:T(8,128)(2,1)S(1)}, bf16[4,64,768]{2,1,0:T(8,128)(2,1)S(1)}, u32[]{:S(2)}, u32[]{:S(2)}) collective-permute-start(bf16[4,64,768]{2,1,0:T(8,128)(2,1)S(1)} %pad_maximum_fusion.rest_0_), channel_id=1, source_target_pairs={{0,16},{16,0},{1,17},{17,1},{2,18},{18,2},{3,19},{19,3},{4,20},{20... | collective-permute-start | bytes 1179656 | tf_op jit(solution)/shard_map/ppermute | solution.py:283
  117.0 11.9 %collective-permute-done.17.rest_1_ = bf16[4,64,768]{2,1,0:T(8,128)(2,1)S(1)} collective-permute-done((bf16[4,64,768]{2,1,0:T(8,128)(2,1)S(1)}, bf16[4,64,768]{2,1,0:T(8,128)(2,1)S(1)}, u32[]{:S(2)}, u32[]{:S(2)}) %collective-permute-start.17) | collective-permute-done | bytes 393248 | tf_op jit(solution)/shard_map/ppermute | solution.py:283
  129.9 28.5 %all_to_all.15 = bf16[16,24,768]{2,1,0:T(8,128)(2,1)S(1)} all-to-all(bf16[16,24,768]{2,1,0:T(8,128)(2,1)S(1)} %bitcast.30), channel_id=1, replica_groups=mesh['y'=8,'xh'=2,'xl'=2,'g'=4,'q'=4] {'xh','y'}, dimensions={0} | all-to-all | bytes 1179648 | tf_op jit(solution)/shard_map/all_to_all | solution.py:380
  158.6 35.6 %all_to_all.16 = bf16[32,24,768]{2,1,0:T(8,128)(2,1)S(1)} all-to-all(bf16[32,24,768]{2,1,0:T(8,128)(2,1)S(1)} %broadcast_in_dim.42), channel_id=1, replica_groups=mesh['y'=8,'xh'=2,'xl'=2,'g'=4,'q'=4] {'xl','xh','y'}, dimensions={0} | all-to-all | bytes 2359296 | tf_op jit(solution)/shard_map/all_to_all | solution.py:384
  194.4 2.0 copy.17
  (50 shorter events, 11.6 us)
Async XLA Ops:
  0.0 56.4 %copy-start = (bf16[1,3,64,768]{3,2,1,0:T(8,128)(2,1)S(1)}, bf16[1,3,64,768]{3,2,1,0:T(8,128)(2,1)}, u32[]{:S(2)}) copy-start(bf16[1,3,64,768]{3,2,1,0:T(8,128)(2,1)} %param.11) | copy-start | bytes 884740
  2.1 10.5 %collective-permute-start.1 = (bf16[768,768]{1,0:T(8,128)(2,1)}, bf16[768,768]{1,0:T(8,128)(2,1)S(1)}, u32[]{:S(2)}, u32[]{:S(2)}) collective-permute-start(bf16[768,768]{1,0:T(8,128)(2,1)} %bitcast.31), channel_id=1, source_target_pairs={{0,1},{1,0},{2,3},{3,2},{4,5},{5,4},{6,7},{7,6},{8,9},{9,8},{10,11... | collective-permute-start | bytes 3538952 | tf_op jit(solution)/shard_map/ppermute | solution.py:223
  4.0 34.6 %collective-permute-start = (bf16[768,768]{1,0:T(8,128)(2,1)}, bf16[768,768]{1,0:T(8,128)(2,1)S(1)}, u32[]{:S(2)}, u32[]{:S(2)}) collective-permute-start(bf16[768,768]{1,0:T(8,128)(2,1)} %bitcast.32), channel_id=1, source_target_pairs={{0,2},{1,3},{2,0},{3,1},{4,6},{5,7},{6,4},{7,5},{8,10},{9,11},{10,... | collective-permute-start | bytes 3538952 | tf_op jit(solution)/shard_map/ppermute | solution.py:223
  12.6 10.0 %collective-permute-start.2 = (f32[8,768]{1,0:T(8,128)S(1)}, f32[8,768]{1,0:T(8,128)S(1)}, u32[]{:S(2)}, u32[]{:S(2)}) collective-permute-start(f32[8,768]{1,0:T(8,128)S(1)} %maximum_maximum_fusion), channel_id=1, source_target_pairs={{0,1},{1,0},{2,3},{3,2},{4,5},{5,4},{6,7},{7,6},{8,9},{9,8},{10,11... | collective-permute-start | bytes 73736 | tf_op jit(solution)/shard_map/ppermute | solution.py:223
  14.7 23.8 %collective-permute-start.3 = (f32[8,768]{1,0:T(8,128)S(1)}, f32[8,768]{1,0:T(8,128)S(1)}, u32[]{:S(2)}, u32[]{:S(2)}) collective-permute-start(f32[8,768]{1,0:T(8,128)S(1)} %maximum_maximum_fusion), channel_id=1, source_target_pairs={{0,2},{1,3},{2,0},{3,1},{4,6},{5,7},{6,4},{7,5},{8,10},{9,11},{10,... | collective-permute-start | bytes 73736 | tf_op jit(solution)/shard_map/ppermute | solution.py:223
  16.9 21.7 %collective-permute-start.4 = (f32[8,768]{1,0:T(8,128)S(1)}, f32[8,768]{1,0:T(8,128)S(1)}, u32[]{:S(2)}, u32[]{:S(2)}) collective-permute-start(f32[8,768]{1,0:T(8,128)S(1)} %maximum_maximum_fusion), channel_id=1, source_target_pairs={{0,3},{1,2},{2,1},{3,0},{4,7},{5,6},{6,5},{7,4},{8,11},{9,10},{10,... | collective-permute-start | bytes 73736 | tf_op jit(solution)/shard_map/ppermute | solution.py:223
  20.2 1.3 copy-start.1
  38.6 4.7 %collective-permute-start.5 = (bf16[768,768]{1,0:T(8,128)(2,1)S(1)}, bf16[768,768]{1,0:T(8,128)(2,1)S(1)}, u32[]{:S(2)}, u32[]{:S(2)}) collective-permute-start(bf16[768,768]{1,0:T(8,128)(2,1)S(1)} %collective-permute-done.rest_0_), channel_id=1, source_target_pairs={{0,1},{1,0},{2,3},{3,2},{4,5},{5,4},{6,7},{7,6},{8,9},{9,8},{10,11... | collective-permute-start | bytes 3538952 | tf_op jit(solution)/shard_map/ppermute | solution.py:223
  47.0 5.6 %collective-permute-start.6 = (bf16[64,768]{1,0:T(8,128)(2,1)S(1)}, bf16[64,768]{1,0:T(8,128)(2,1)S(1)}, u32[]{:S(2)}, u32[]{:S(2)}) collective-permute-start(bf16[64,768]{1,0:T(8,128)(2,1)S(1)} %get-tuple-element.56), channel_id=1, source_target_pairs={{0,4},{1,5},{2,6},{16,20},{17,21},{18,22},{32,36},{33,37},{34,38},... | collective-permute-start | bytes 294920 | tf_op jit(solution)/shard_map/ppermute | solution.py:269
  52.5 6.6 %collective-permute-start.9 = (bf16[4,64,768]{2,1,0:T(8,128)(2,1)S(1)}, bf16[4,64,768]{2,1,0:T(8,128)(2,1)S(1)}, u32[]{:S(2)}, u32[]{:S(2)}) collective-permute-start(bf16[4,64,768]{2,1,0:T(8,128)(2,1)S(1)} %get-tuple-element.63), channel_id=1, source_target_pairs={{0,12},{1,13},{2,14},{16,28},{17,29},{18,30},{32,44},{33,45},{34,4... | collective-permute-start | bytes 1179656 | tf_op jit(solution)/shard_map/ppermute | solution.py:269
  54.4 0.7 collective-permute-start.7
  55.7 0.7 collective-permute-start.8
  63.0 0.7 collective-permute-start.10
  65.4 13.9 %collective-permute-start.11 = (bf16[64,768]{1,0:T(8,128)(2,1)S(1)}, bf16[64,768]{1,0:T(8,128)(2,1)S(1)}, u32[]{:S(2)}, u32[]{:S(2)}) collective-permute-start(bf16[64,768]{1,0:T(8,128)(2,1)S(1)} %get-tuple-element.75), channel_id=1, source_target_pairs={{8,4},{9,5},{10,6},{24,20},{25,21},{26,22},{40,36},{41,37},{42,38}... | collective-permute-start | bytes 294920 | tf_op jit(solution)/shard_map/ppermute | solution.py:269
  66.1 40.4 %collective-permute-start.13 = (bf16[4,64,768]{2,1,0:T(8,128)(2,1)S(1)}, bf16[4,64,768]{2,1,0:T(8,128)(2,1)S(1)}, u32[]{:S(2)}, u32[]{:S(2)}) collective-permute-start(bf16[4,64,768]{2,1,0:T(8,128)(2,1)S(1)} %get-tuple-element.86), channel_id=1, source_target_pairs={{12,0},{13,1},{14,2},{28,16},{29,17},{30,18},{44,32},{45,33},{46,3... | collective-permute-start | bytes 1179656 | tf_op jit(solution)/shard_map/ppermute | solution.py:269
  67.4 15.2 %collective-permute-start.16 = (bf16[1,64,768]{2,1,0:T(8,128)(2,1)S(1)}, bf16[1,64,768]{2,1,0:T(8,128)(2,1)S(1)}, u32[]{:S(2)}, u32[]{:S(2)}) collective-permute-start(bf16[1,64,768]{2,1,0:T(8,128)(2,1)S(1)} %get-tuple-element.92), channel_id=1, source_target_pairs={{0,3},{1,2},{2,1},{4,7},{5,6},{6,5},{8,11},{9,10},{10,9},{12,15},{... | collective-permute-start | bytes 294920 | tf_op jit(solution)/shard_map/ppermute | solution.py:276
  75.4 7.2 %collective-permute-start.15 = (bf16[1,64,768]{2,1,0:T(8,128)(2,1)S(1)}, bf16[1,64,768]{2,1,0:T(8,128)(2,1)S(1)}, u32[]{:S(2)}, u32[]{:S(2)}) collective-permute-start(bf16[1,64,768]{2,1,0:T(8,128)(2,1)S(1)} %get-tuple-element.93), channel_id=1, source_target_pairs={{0,2},{1,3},{2,0},{4,6},{5,7},{6,4},{8,10},{9,11},{10,8},{12,14},{... | collective-permute-start | bytes 294920 | tf_op jit(solution)/shard_map/ppermute | solution.py:276
  78.1 4.6 %collective-permute-start.14 = (bf16[1,64,768]{2,1,0:T(8,128)(2,1)S(1)}, bf16[1,64,768]{2,1,0:T(8,128)(2,1)S(1)}, u32[]{:S(2)}, u32[]{:S(2)}) collective-permute-start(bf16[1,64,768]{2,1,0:T(8,128)(2,1)S(1)} %get-tuple-element.94), channel_id=1, source_target_pairs={{0,1},{1,0},{2,3},{4,5},{5,4},{6,7},{8,9},{9,8},{10,11},{12,13},{1... | collective-permute-start | bytes 294920 | tf_op jit(solution)/shard_map/ppermute | solution.py:276
  81.4 25.2 %collective-permute-start.12 = (bf16[64,768]{1,0:T(8,128)(2,1)S(1)}, bf16[64,768]{1,0:T(8,128)(2,1)S(1)}, u32[]{:S(2)}, u32[]{:S(2)}) collective-permute-start(bf16[64,768]{1,0:T(8,128)(2,1)S(1)} %get-tuple-element.82), channel_id=1, source_target_pairs={{4,0},{5,1},{6,2},{20,16},{21,17},{22,18},{36,32},{37,33},{38,34},... | collective-permute-start | bytes 294920 | tf_op jit(solution)/shard_map/ppermute | solution.py:269
  110.2 18.6 %all-to-all-start = ((bf16[8,64,384]{2,1,0:T(8,128)(2,1)}), bf16[8,64,384]{2,1,0:T(8,128)(2,1)S(1)}, u32[]{:S(2)}, u32[]{:S(2)}) async-start(bf16[8,64,384]{2,1,0:T(8,128)(2,1)} %bitcast.11), calls=%async_computation | async-start | bytes 786432 | tf_op jit(solution)/shard_map/all_to_all | solution.py:376
  113.6 15.2 %collective-permute-start.17 = (bf16[4,64,768]{2,1,0:T(8,128)(2,1)S(1)}, bf16[4,64,768]{2,1,0:T(8,128)(2,1)S(1)}, u32[]{:S(2)}, u32[]{:S(2)}) collective-permute-start(bf16[4,64,768]{2,1,0:T(8,128)(2,1)S(1)} %pad_maximum_fusion.rest_0_), channel_id=1, source_target_pairs={{0,16},{16,0},{1,17},{17,1},{2,18},{18,2},{3,19},{19,3},{4,20},{20... | collective-permute-start | bytes 1179656 | tf_op jit(solution)/shard_map/ppermute | solution.py:283

commit v5 on v3

--- a/solution.py
+++ b/solution.py
@@ -56,6 +56,7 @@
     def _():
         y = x_ref[...]
         for j in range(GROUP):
+            d = jnp.bitwise_xor(member, j)
             squares = None
             for cs in chunks_of(channels):
                 u = y[:, cs].astype(jnp.float32)
@@ -83,7 +84,7 @@
                     SCALE + (3.0 * SCALE * CUBIC) * v2
                 )
                 act = (v * half).astype(jnp.bfloat16)
-                hb[j, :, cs] = act
+                hb[d, :, cs] = act
                 part = jnp.dot(act, w_ref[j, cs, :], preferred_element_type=jnp.float32)
                 total = part if total is None else total + part
             y = (ub[...] + total).astype(jnp.bfloat16)
@@ -151,14 +152,14 @@
     def _():
         dx = g_ref[...]
         for j in reversed(range(GROUP)):
+            d = jnp.bitwise_xor(member, j)
             for cs in chunks_of(channels):
                 g = dx[:, cs].astype(jnp.float32)
                 if first:
                     g = g + k_ref[j, :, cs].astype(jnp.float32)
                 gb[:, cs] = g
             e = gb[...].astype(jnp.bfloat16)
-            for i in range(eb.shape[0]):
-                eb[i, j] = e[:, i * eb.shape[3] : (i + 1) * eb.shape[3]]
+            eb[d] = e
             if first and j == 0:
                 continue
             dots = None
@@ -194,7 +195,7 @@
         args.append(k)
     args.append(e)
     args = [flags] + held(*args)
-    out_shape = [kept(e.shape, bf)]
+    out_shape = [kept(wide, bf)]
     if not first:
         out_shape.append(kept((rows, channels), bf))
     if last:
@@ -268,36 +269,35 @@
     return lax.ppermute(block, PIPE, pairs)
 
 
-def gathered(h, member, across_count):
-    group = jnp.zeros(h.shape, h.dtype)
-    own = lax.dynamic_index_in_dim(h, member, 0, keepdims=True)
-    group = lax.dynamic_update_slice(group, own, (member, 0, 0))
-    for d in range(1, GROUP):
-        slot = jnp.bitwise_xor(member, d)
-        pairs = [(i, i ^ d) for i in range(lax.axis_size(PIPE)) if i % GROUP < MICROS]
-        sent = lax.dynamic_index_in_dim(h, slot, 0, keepdims=True)
-        group = lax.dynamic_update_slice(group, lax.ppermute(sent, PIPE, pairs), (slot, 0, 0))
-    group = group.reshape(1, -1, h.shape[2])
-    here = lax.axis_index("x")
-    acts = jnp.zeros((across_count,) + group.shape[1:], h.dtype)
-    acts = lax.dynamic_update_slice(acts, group, (here, 0, 0))
-    for shift in range(1, across_count):
-        pairs = [(i, (i + shift) % across_count) for i in range(across_count)]
-        slot = (here - shift) % across_count
-        acts = lax.dynamic_update_slice(acts, lax.ppermute(group, "x", pairs), (slot, 0, 0))
-    return acts.reshape(-1, h.shape[2])
+def traded(block, distance):
+    pairs = [(i, i ^ distance) for i in range(lax.axis_size(PIPE)) if i % GROUP < MICROS]
+    return lax.ppermute(block[distance], PIPE, pairs)
+
+
+def together(block):
+    return jnp.concatenate([block[0]] + [traded(block, d) for d in range(1, GROUP)])
+
+
+def summed_part(block, axis):
+    count = lax.axis_size(axis)
+    parts = lax.all_to_all(block.reshape(count, -1, block.shape[1]), axis, 0, 0)
+    return jnp.sum(parts.astype(jnp.float32), axis=0)
+
+
+def all_parts(block, axis):
+    count = lax.axis_size(axis)
+    parts = lax.all_to_all(jnp.broadcast_to(block, (count,) + block.shape), axis, 0, 0)
+    return parts.reshape(-1, block.shape[1])
 
 
 def shards(base_ids, embed_table, segment_weights, conv_taps, norm_gains, cotangent):
     stages = lax.axis_size("g")
-    down, across_count = lax.axis_size("y"), lax.axis_size("x")
     member = lax.axis_index("q")
     flags = jnp.stack([lax.axis_index("g"), member]).astype(jnp.int32)
     micro = jnp.minimum(member, MICROS - 1)
     weight = segment_weights[0]
     channels = weight.shape[1]
     row_count = base_ids.shape[2]
-    block = channels // across_count
     bf = jnp.bfloat16
 
     across = swapped(weight, 2)
@@ -316,8 +316,10 @@
     corner = swapped(across, 1)
     weights = packed(weights, flags, [(2, 0, across)])
     weights = packed(weights, flags, [(3, 0, corner)])
-    h = jnp.zeros((GROUP, row_count, channels), bf)
-    e = jnp.zeros((across_count, GROUP, row_count, block), bf)
+
+    wide = (GROUP, row_count, channels)
+    h = jnp.zeros(wide, bf)
+    e = jnp.zeros(wide, bf)
     states, k = [], None
     for stage in range(stages):
         skip, towers = stage == stages - 1, stage == 0
@@ -343,24 +345,21 @@
             returned = shifted(skip_grad, stages - 1, 0)
         if stage == stages - 2:
             h, e = lax.optimization_barrier((h, e))
-            acts = gathered(h, member, across_count)
-        if stage == 1:
-            acts, e = lax.optimization_barrier((acts, e))
-    errors = lax.all_to_all(e.reshape(-1, row_count, block), ("x", "q"), 0, 0).reshape(-1, block)
-
-    turned = lax.dot_general(errors, acts, (((0,), (0,)), ((), ())), preferred_element_type=jnp.float32)
-    pieces = lax.all_to_all(turned.astype(bf).reshape(down, block // down, channels), "y", 0, 0)
-    factor = 1.0 / math.sqrt(down * across_count * MICROS * row_count)
-    piece = (jnp.sum(pieces.astype(jnp.float32), axis=0) * factor).astype(bf)
-    piece = jnp.broadcast_to(piece, (across_count * down,) + piece.shape)
-    whole = lax.all_to_all(piece, ("x", "y"), 0, 0).reshape(channels, channels)
-    return whole.T.astype(jnp.float32)[None]
+            acts = together(h)
+    errors = together(e)
+
+    terms = lax.dot_general(acts, errors, (((0,), (0,)), ((), ())), preferred_element_type=jnp.float32)
+    factor = 1.0 / math.sqrt(lax.axis_size(("y", "x")) * MICROS * row_count)
+    part = summed_part(terms.astype(bf), "x").astype(bf)
+    part = (summed_part(part, "y") * factor).astype(bf)
+    whole = all_parts(all_parts(part, "y"), "x")
+    return whole.astype(jnp.float32)[None]
 
 
 def solution(mesh):
     replicas, _ = mesh.devices.shape
-    shape = (replicas // math.gcd(4, replicas), math.gcd(4, replicas), -1, GROUP)
-    grid = Mesh(mesh.devices.reshape(shape), ("y", "x", "g", "q"))
+    wide = math.gcd(4, replicas)
+    grid = Mesh(mesh.devices.reshape(replicas // wide, wide, -1, GROUP), ("y", "x", "g", "q"))
     windows = P(("y", "x"), None, None, None)
     return jax.shard_map(
         shards,

time: 202 us -> 183 us (0.906)
  the two profiles are of different devices: /device:TPU:8 before, /device:TPU:128 now
where the time goes in v5:
time: 183 us
  blocking collectives  65.9 us (36%)
  waiting for transfers between devices  55.9 us (31%)
  starting transfers between devices  39.8 us (22%)
  Pallas kernels  12.9 us (7%)
  local copies, waits for them, and re-layouts  3.16 us (2%)
  other arithmetic  2.73 us (1%)
    all_to_all x2, blocking collectives, summed_part(): parts = lax.all_to_all(block.reshape(count, -1, block.shape[1]), axis, 0, 0)  36.9 us
    ppermute x8, waiting for transfers between devices, shifted(): return lax.ppermute(block, PIPE, pairs)  36.7 us
    all_to_all x2, blocking collectives, all_parts(): lax.all_to_all(jnp.broadcast_to(block, (count,) + block.shape), axis, 0, 0)  29 us
    ppermute x6, waiting for transfers between devices, swapped(): return lax.ppermute(block, PIPE, pairs)  18 us
    ppermute x6, starting transfers between devices, traded(): return lax.ppermute(block[distance], PIPE, pairs)  16.1 us
    ppermute x6, starting transfers between devices, swapped(): return lax.ppermute(block, PIPE, pairs)  15.8 us
    ppermute x8, starting transfers between devices, shifted(): return lax.ppermute(block, PIPE, pairs)  7.87 us
    pallas_call x4, Pallas kernels, forward_stage(): pl.pallas_call(functools.partial(forward_kernel, stage, skip, towers), ou...  5.21 us
  transfers between devices with their start and end apart: 20, of which 8 were waited for; matrix products, arithmetic and copies ran while one was open for 1% of the time, Pallas kernels for 5%

profile of v5, /device:TPU:128, one launch (start us, length us, event | category | flops | bytes accessed | tf_op | source)
XLA Modules:
  0.0 182.5 jit_solution(11684759855325701786)
XLA Ops:
  0.9 1.2 convolution_convert_fusion.1.x_ref
  2.1 1.9 %collective-permute-start.1 = (bf16[768,768]{1,0:T(8,128)(2,1)}, bf16[768,768]{1,0:T(8,128)(2,1)S(1)}, u32[]{:S(2)}, u32[]{:S(2)}) collective-permute-start(bf16[768,768]{1,0:T(8,128)(2,1)} %bitcast.43), channel_id=1, source_target_pairs={{0,1},{1,0},{2,3},{3,2},{4,5},{5,4},{6,7},{7,6},{8,9},{9,8},{10,11... | collective-permute-start | bytes 3538952 | tf_op jit(solution)/shard_map/ppermute | solution.py:223
  4.0 4.3 %collective-permute-start = (bf16[768,768]{1,0:T(8,128)(2,1)}, bf16[768,768]{1,0:T(8,128)(2,1)S(1)}, u32[]{:S(2)}, u32[]{:S(2)}) collective-permute-start(bf16[768,768]{1,0:T(8,128)(2,1)} %bitcast.44), channel_id=1, source_target_pairs={{0,2},{1,3},{2,0},{3,1},{4,6},{5,7},{6,4},{7,5},{8,10},{9,11},{10,... | collective-permute-start | bytes 3538952 | tf_op jit(solution)/shard_map/ppermute | solution.py:223
  9.9 2.1 %collective-permute-start.2 = (f32[8,768]{1,0:T(8,128)S(1)}, f32[8,768]{1,0:T(8,128)S(1)}, u32[]{:S(2)}, u32[]{:S(2)}) collective-permute-start(f32[8,768]{1,0:T(8,128)S(1)} %maximum_maximum_fusion), channel_id=1, source_target_pairs={{0,1},{1,0},{2,3},{3,2},{4,5},{5,4},{6,7},{7,6},{8,9},{9,8},{10,11... | collective-permute-start | bytes 73736 | tf_op jit(solution)/shard_map/ppermute | solution.py:223
  12.0 2.2 %collective-permute-start.3 = (f32[8,768]{1,0:T(8,128)S(1)}, f32[8,768]{1,0:T(8,128)S(1)}, u32[]{:S(2)}, u32[]{:S(2)}) collective-permute-start(f32[8,768]{1,0:T(8,128)S(1)} %maximum_maximum_fusion), channel_id=1, source_target_pairs={{0,2},{1,3},{2,0},{3,1},{4,6},{5,7},{6,4},{7,5},{8,10},{9,11},{10,... | collective-permute-start | bytes 73736 | tf_op jit(solution)/shard_map/ppermute | solution.py:223
  14.2 3.3 %collective-permute-start.4 = (f32[8,768]{1,0:T(8,128)S(1)}, f32[8,768]{1,0:T(8,128)S(1)}, u32[]{:S(2)}, u32[]{:S(2)}) collective-permute-start(f32[8,768]{1,0:T(8,128)S(1)} %maximum_maximum_fusion), channel_id=1, source_target_pairs={{0,3},{1,2},{2,1},{3,0},{4,7},{5,6},{6,5},{7,4},{8,11},{9,10},{10,... | collective-permute-start | bytes 73736 | tf_op jit(solution)/shard_map/ppermute | solution.py:223
  17.6 1.3 copy-done.1
  18.8 1.1 packed.3.rest_1_
  19.9 15.9 %collective-permute-done.3 = f32[8,768]{1,0:T(8,128)S(1)} collective-permute-done((f32[8,768]{1,0:T(8,128)S(1)}, f32[8,768]{1,0:T(8,128)S(1)}, u32[]{:S(2)}, u32[]{:S(2)}) %collective-permute-start.3) | collective-permute-done | bytes 24608 | tf_op jit(solution)/shard_map/ppermute | solution.py:223
  36.0 2.0 %collective-permute-start.5 = (bf16[768,768]{1,0:T(8,128)(2,1)S(1)}, bf16[768,768]{1,0:T(8,128)(2,1)S(1)}, u32[]{:S(2)}, u32[]{:S(2)}) collective-permute-start(bf16[768,768]{1,0:T(8,128)(2,1)S(1)} %collective-permute-done.rest_0_), channel_id=1, source_target_pairs={{0,1},{1,0},{2,3},{3,2},{4,5},{5,4},{6,7},{7,6},{8,9},{9,8},{10,11... | collective-permute-start | bytes 3538952 | tf_op jit(solution)/shard_map/ppermute | solution.py:223
  38.8 1.9 %collective-permute-done.5.rest_0_ = bf16[768,768]{1,0:T(8,128)(2,1)S(1)} collective-permute-done((bf16[768,768]{1,0:T(8,128)(2,1)S(1)}, bf16[768,768]{1,0:T(8,128)(2,1)S(1)}, u32[]{:S(2)}, u32[]{:S(2)}) %collective-permute-start.5) | collective-permute-done | bytes 1179680 | tf_op jit(solution)/shard_map/ppermute | solution.py:223
  42.2 1.3 collective-permute-start.6
  43.5 8.8 %collective-permute-done.6.x_ref = bf16[64,768]{1,0:T(8,128)(2,1)S(1)} collective-permute-done((bf16[64,768]{1,0:T(8,128)(2,1)S(1)}, bf16[64,768]{1,0:T(8,128)(2,1)S(1)}, u32[]{:S(2)}, u32[]{:S(2)}) %collective-permute-start.6) | collective-permute-done | bytes 98336 | tf_op jit(solution)/shard_map/ppermute | solution.py:269
  52.9 2.8 %ahead1.1 = (bf16[64,768]{1,0:T(8,128)(2,1)S(1)}, f32[4,64,768]{2,1,0:T(8,128)S(1)}, f32[4,64,768]{2,1,0:T(8,128)S(1)}, f32[4,64,128]{2,1,0:T(8,128)S(1)}, bf16[4,64,768]{2,1,0:T(8,128)(2,1)S(1)}) custom-call(s32[2]{0:T(128)S(1)} %pad_add_fusion.flags, bf16[64,768]{1,0:T(8,128)(2,1)S(1)} %collective-permute-done.6.x_ref, ...), custom_call_target="tpu_custom_call", output_to_operand_aliasing={{4}: (4, {})} | custom-call | tf_op jit(solution)/shard_map/ahead1/pallas_call | solution.py:123
  55.7 1.3 collective-permute-start.7
  57.0 2.2 %collective-permute-done.7.x_ref = bf16[64,768]{1,0:T(8,128)(2,1)S(1)} collective-permute-done((bf16[64,768]{1,0:T(8,128)(2,1)S(1)}, bf16[64,768]{1,0:T(8,128)(2,1)S(1)}, u32[]{:S(2)}, u32[]{:S(2)}) %collective-permute-start.7) | collective-permute-done | bytes 98336 | tf_op jit(solution)/shard_map/ppermute | solution.py:269
  60.5 1.2 ahead3.1
  64.4 1.3 collective-permute-start.14
  65.7 25.7 %collective-permute-done.14.g_ref = bf16[64,768]{1,0:T(8,128)(2,1)S(1)} collective-permute-done((bf16[64,768]{1,0:T(8,128)(2,1)S(1)}, bf16[64,768]{1,0:T(8,128)(2,1)S(1)}, u32[]{:S(2)}, u32[]{:S(2)}) %collective-permute-start.14) | collective-permute-done | bytes 98336 | tf_op jit(solution)/shard_map/ppermute | solution.py:269
  91.4 3.3 %behind1.1 = (bf16[4,64,768]{2,1,0:T(8,128)(2,1)S(1)}, bf16[64,768]{1,0:T(8,128)(2,1)S(1)}) custom-call(s32[2]{0:T(128)S(1)} %pad_add_fusion.flags, bf16[64,768]{1,0:T(8,128)(2,1)S(1)} %collective-permute-done.14.g_ref, bf16[4,768,768]{2,1,0:T(8,128)(2,1)S(1)} %packed.5.w_ref, ...), custom_call_target="tpu_custom_call", output_to_operand_aliasing={{0}: (7, {})} | custom-call | tf_op jit(solution)/shard_map/behind1/pallas_call | solution.py:203
  94.7 1.3 collective-permute-start.15
  96.0 1.3 collective-permute-start.13
  97.3 5.0 %collective-permute-start.12 = (bf16[64,768]{1,0:T(8,128)(2,1)S(1)}, bf16[64,768]{1,0:T(8,128)(2,1)S(1)}, u32[]{:S(2)}, u32[]{:S(2)}) collective-permute-start(bf16[64,768]{1,0:T(8,128)(2,1)S(1)} %get-tuple-element.93), channel_id=1, source_target_pairs={{0,2},{1,3},{2,0},{4,6},{5,7},{6,4},{8,10},{9,11},{10,8},{12,14},{... | collective-permute-start | bytes 294920 | tf_op jit(solution)/shard_map/ppermute | solution.py:274
  102.4 1.9 %collective-permute-start.11 = (bf16[64,768]{1,0:T(8,128)(2,1)S(1)}, bf16[64,768]{1,0:T(8,128)(2,1)S(1)}, u32[]{:S(2)}, u32[]{:S(2)}) collective-permute-start(bf16[64,768]{1,0:T(8,128)(2,1)S(1)} %get-tuple-element.94), channel_id=1, source_target_pairs={{0,1},{1,0},{2,3},{4,5},{5,4},{6,7},{8,9},{9,8},{10,11},{12,13},{1... | collective-permute-start | bytes 294920 | tf_op jit(solution)/shard_map/ppermute | solution.py:274
  105.0 1.3 collective-permute-start.19
  106.3 4.7 %collective-permute-start.18 = (bf16[64,768]{1,0:T(8,128)(2,1)S(1)}, bf16[64,768]{1,0:T(8,128)(2,1)S(1)}, u32[]{:S(2)}, u32[]{:S(2)}) collective-permute-start(bf16[64,768]{1,0:T(8,128)(2,1)S(1)} %get-tuple-element.89), channel_id=1, source_target_pairs={{0,2},{1,3},{2,0},{4,6},{5,7},{6,4},{8,10},{9,11},{10,8},{12,14},{... | collective-permute-start | bytes 294920 | tf_op jit(solution)/shard_map/ppermute | solution.py:274
  110.9 1.9 %collective-permute-start.17 = (bf16[64,768]{1,0:T(8,128)(2,1)S(1)}, bf16[64,768]{1,0:T(8,128)(2,1)S(1)}, u32[]{:S(2)}, u32[]{:S(2)}) collective-permute-start(bf16[64,768]{1,0:T(8,128)(2,1)S(1)} %get-tuple-element.90), channel_id=1, source_target_pairs={{0,1},{1,0},{2,3},{4,5},{5,4},{6,7},{8,9},{9,8},{10,11},{12,13},{1... | collective-permute-start | bytes 294920 | tf_op jit(solution)/shard_map/ppermute | solution.py:274
  114.7 19.5 %all_to_all.23 = bf16[4,192,768]{2,1,0:T(8,128)(2,1)S(1)} all-to-all(bf16[4,192,768]{2,1,0:T(8,128)(2,1)S(1)} %bitcast.47), channel_id=1, replica_groups=mesh['y'=8,'x'=4,'g'=4,'q'=4] {'x'}, dimensions={0} | all-to-all | bytes 2359296 | tf_op jit(solution)/shard_map/all_to_all | solution.py:283
  134.5 17.3 %all_to_all.20 = bf16[8,24,768]{2,1,0:T(8,128)(2,1)S(1)} all-to-all(bf16[8,24,768]{2,1,0:T(8,128)(2,1)S(1)} %bitcast.48), channel_id=1, replica_groups=mesh['y'=8,'x'=4,'g'=4,'q'=4] {'y'}, dimensions={0} | all-to-all | bytes 589824 | tf_op jit(solution)/shard_map/all_to_all | solution.py:283
  151.9 13.2 %all_to_all.21 = bf16[8,24,768]{2,1,0:T(8,128)(2,1)S(1)} all-to-all(bf16[8,24,768]{2,1,0:T(8,128)(2,1)S(1)} %broadcast_in_dim.32), channel_id=1, replica_groups=mesh['y'=8,'x'=4,'g'=4,'q'=4] {'y'}, dimensions={0} | all-to-all | bytes 589824 | tf_op jit(solution)/shard_map/all_to_all | solution.py:289
  165.2 15.8 %all_to_all.22 = bf16[4,192,768]{2,1,0:T(8,128)(2,1)S(1)} all-to-all(bf16[4,192,768]{2,1,0:T(8,128)(2,1)S(1)} %broadcast_in_dim.33), channel_id=1, replica_groups=mesh['y'=8,'x'=4,'g'=4,'q'=4] {'x'}, dimensions={0} | all-to-all | bytes 2359296 | tf_op jit(solution)/shard_map/all_to_all | solution.py:289
  181.0 1.6 bitcast_convert_fusion
  (54 shorter events, 12.3 us)
Async XLA Ops:
  0.0 60.5 %copy-start = (bf16[1,3,64,768]{3,2,1,0:T(8,128)(2,1)S(1)}, bf16[1,3,64,768]{3,2,1,0:T(8,128)(2,1)}, u32[]{:S(2)}) copy-start(bf16[1,3,64,768]{3,2,1,0:T(8,128)(2,1)} %param.11) | copy-start | bytes 884740
  2.1 7.8 %collective-permute-start.1 = (bf16[768,768]{1,0:T(8,128)(2,1)}, bf16[768,768]{1,0:T(8,128)(2,1)S(1)}, u32[]{:S(2)}, u32[]{:S(2)}) collective-permute-start(bf16[768,768]{1,0:T(8,128)(2,1)} %bitcast.43), channel_id=1, source_target_pairs={{0,1},{1,0},{2,3},{3,2},{4,5},{5,4},{6,7},{7,6},{8,9},{9,8},{10,11... | collective-permute-start | bytes 3538952 | tf_op jit(solution)/shard_map/ppermute | solution.py:223
  4.0 32.0 %collective-permute-start = (bf16[768,768]{1,0:T(8,128)(2,1)}, bf16[768,768]{1,0:T(8,128)(2,1)S(1)}, u32[]{:S(2)}, u32[]{:S(2)}) collective-permute-start(bf16[768,768]{1,0:T(8,128)(2,1)} %bitcast.44), channel_id=1, source_target_pairs={{0,2},{1,3},{2,0},{3,1},{4,6},{5,7},{6,4},{7,5},{8,10},{9,11},{10,... | collective-permute-start | bytes 3538952 | tf_op jit(solution)/shard_map/ppermute | solution.py:223
  9.9 10.0 %collective-permute-start.2 = (f32[8,768]{1,0:T(8,128)S(1)}, f32[8,768]{1,0:T(8,128)S(1)}, u32[]{:S(2)}, u32[]{:S(2)}) collective-permute-start(f32[8,768]{1,0:T(8,128)S(1)} %maximum_maximum_fusion), channel_id=1, source_target_pairs={{0,1},{1,0},{2,3},{3,2},{4,5},{5,4},{6,7},{7,6},{8,9},{9,8},{10,11... | collective-permute-start | bytes 73736 | tf_op jit(solution)/shard_map/ppermute | solution.py:223
  12.0 23.8 %collective-permute-start.3 = (f32[8,768]{1,0:T(8,128)S(1)}, f32[8,768]{1,0:T(8,128)S(1)}, u32[]{:S(2)}, u32[]{:S(2)}) collective-permute-start(f32[8,768]{1,0:T(8,128)S(1)} %maximum_maximum_fusion), channel_id=1, source_target_pairs={{0,2},{1,3},{2,0},{3,1},{4,6},{5,7},{6,4},{7,5},{8,10},{9,11},{10,... | collective-permute-start | bytes 73736 | tf_op jit(solution)/shard_map/ppermute | solution.py:223
  14.2 21.7 %collective-permute-start.4 = (f32[8,768]{1,0:T(8,128)S(1)}, f32[8,768]{1,0:T(8,128)S(1)}, u32[]{:S(2)}, u32[]{:S(2)}) collective-permute-start(f32[8,768]{1,0:T(8,128)S(1)} %maximum_maximum_fusion), channel_id=1, source_target_pairs={{0,3},{1,2},{2,1},{3,0},{4,7},{5,6},{6,5},{7,4},{8,11},{9,10},{10,... | collective-permute-start | bytes 73736 | tf_op jit(solution)/shard_map/ppermute | solution.py:223
  17.5 1.3 copy-start.1
  36.0 4.7 %collective-permute-start.5 = (bf16[768,768]{1,0:T(8,128)(2,1)S(1)}, bf16[768,768]{1,0:T(8,128)(2,1)S(1)}, u32[]{:S(2)}, u32[]{:S(2)}) collective-permute-start(bf16[768,768]{1,0:T(8,128)(2,1)S(1)} %collective-permute-done.rest_0_), channel_id=1, source_target_pairs={{0,1},{1,0},{2,3},{3,2},{4,5},{5,4},{6,7},{7,6},{8,9},{9,8},{10,11... | collective-permute-start | bytes 3538952 | tf_op jit(solution)/shard_map/ppermute | solution.py:223
  42.2 10.1 %collective-permute-start.6 = (bf16[64,768]{1,0:T(8,128)(2,1)S(1)}, bf16[64,768]{1,0:T(8,128)(2,1)S(1)}, u32[]{:S(2)}, u32[]{:S(2)}) collective-permute-start(bf16[64,768]{1,0:T(8,128)(2,1)S(1)} %get-tuple-element.54), channel_id=1, source_target_pairs={{0,4},{1,5},{2,6},{16,20},{17,21},{18,22},{32,36},{33,37},{34,38},... | collective-permute-start | bytes 294920 | tf_op jit(solution)/shard_map/ppermute | solution.py:269
  52.2 8.3 %collective-permute-start.9 = (bf16[4,64,768]{2,1,0:T(8,128)(2,1)S(1)}, bf16[4,64,768]{2,1,0:T(8,128)(2,1)S(1)}, u32[]{:S(2)}, u32[]{:S(2)}) collective-permute-start(bf16[4,64,768]{2,1,0:T(8,128)(2,1)S(1)} %get-tuple-element.61), channel_id=1, source_target_pairs={{0,12},{1,13},{2,14},{16,28},{17,29},{18,30},{32,44},{33,45},{34,4... | collective-permute-start | bytes 1179656 | tf_op jit(solution)/shard_map/ppermute | solution.py:269
  55.7 3.5 %collective-permute-start.7 = (bf16[64,768]{1,0:T(8,128)(2,1)S(1)}, bf16[64,768]{1,0:T(8,128)(2,1)S(1)}, u32[]{:S(2)}, u32[]{:S(2)}) collective-permute-start(bf16[64,768]{1,0:T(8,128)(2,1)S(1)} %get-tuple-element.58), channel_id=1, source_target_pairs={{4,8},{5,9},{6,10},{20,24},{21,25},{22,26},{36,40},{37,41},{38,42}... | collective-permute-start | bytes 294920 | tf_op jit(solution)/shard_map/ppermute | solution.py:269
  59.8 0.7 collective-permute-start.8
  62.4 0.7 collective-permute-start.10
  63.1 41.2 %collective-permute-start.16 = (bf16[4,64,768]{2,1,0:T(8,128)(2,1)S(1)}, bf16[4,64,768]{2,1,0:T(8,128)(2,1)S(1)}, u32[]{:S(2)}, u32[]{:S(2)}) collective-permute-start(bf16[4,64,768]{2,1,0:T(8,128)(2,1)S(1)} %get-tuple-element.85), channel_id=1, source_target_pairs={{12,0},{13,1},{14,2},{28,16},{29,17},{30,18},{44,32},{45,33},{46,3... | collective-permute-start | bytes 1179656 | tf_op jit(solution)/shard_map/ppermute | solution.py:269
  64.4 27.0 %collective-permute-start.14 = (bf16[64,768]{1,0:T(8,128)(2,1)S(1)}, bf16[64,768]{1,0:T(8,128)(2,1)S(1)}, u32[]{:S(2)}, u32[]{:S(2)}) collective-permute-start(bf16[64,768]{1,0:T(8,128)(2,1)S(1)} %get-tuple-element.76), channel_id=1, source_target_pairs={{8,4},{9,5},{10,6},{24,20},{25,21},{26,22},{40,36},{41,37},{42,38}... | collective-permute-start | bytes 294920 | tf_op jit(solution)/shard_map/ppermute | solution.py:269
  94.7 9.6 %collective-permute-start.15 = (bf16[64,768]{1,0:T(8,128)(2,1)S(1)}, bf16[64,768]{1,0:T(8,128)(2,1)S(1)}, u32[]{:S(2)}, u32[]{:S(2)}) collective-permute-start(bf16[64,768]{1,0:T(8,128)(2,1)S(1)} %get-tuple-element.81), channel_id=1, source_target_pairs={{4,0},{5,1},{6,2},{20,16},{21,17},{22,18},{36,32},{37,33},{38,34},... | collective-permute-start | bytes 294920 | tf_op jit(solution)/shard_map/ppermute | solution.py:269
  96.0 14.9 %collective-permute-start.13 = (bf16[64,768]{1,0:T(8,128)(2,1)S(1)}, bf16[64,768]{1,0:T(8,128)(2,1)S(1)}, u32[]{:S(2)}, u32[]{:S(2)}) collective-permute-start(bf16[64,768]{1,0:T(8,128)(2,1)S(1)} %get-tuple-element.92), channel_id=1, source_target_pairs={{0,3},{1,2},{2,1},{4,7},{5,6},{6,5},{8,11},{9,10},{10,9},{12,15},{... | collective-permute-start | bytes 294920 | tf_op jit(solution)/shard_map/ppermute | solution.py:274
  97.3 15.6 %collective-permute-start.12 = (bf16[64,768]{1,0:T(8,128)(2,1)S(1)}, bf16[64,768]{1,0:T(8,128)(2,1)S(1)}, u32[]{:S(2)}, u32[]{:S(2)}) collective-permute-start(bf16[64,768]{1,0:T(8,128)(2,1)S(1)} %get-tuple-element.93), channel_id=1, source_target_pairs={{0,2},{1,3},{2,0},{4,6},{5,7},{6,4},{8,10},{9,11},{10,8},{12,14},{... | collective-permute-start | bytes 294920 | tf_op jit(solution)/shard_map/ppermute | solution.py:274
  102.4 10.5 %collective-permute-start.11 = (bf16[64,768]{1,0:T(8,128)(2,1)S(1)}, bf16[64,768]{1,0:T(8,128)(2,1)S(1)}, u32[]{:S(2)}, u32[]{:S(2)}) collective-permute-start(bf16[64,768]{1,0:T(8,128)(2,1)S(1)} %get-tuple-element.94), channel_id=1, source_target_pairs={{0,1},{1,0},{2,3},{4,5},{5,4},{6,7},{8,9},{9,8},{10,11},{12,13},{1... | collective-permute-start | bytes 294920 | tf_op jit(solution)/shard_map/ppermute | solution.py:274
  105.0 7.9 %collective-permute-start.19 = (bf16[64,768]{1,0:T(8,128)(2,1)S(1)}, bf16[64,768]{1,0:T(8,128)(2,1)S(1)}, u32[]{:S(2)}, u32[]{:S(2)}) collective-permute-start(bf16[64,768]{1,0:T(8,128)(2,1)S(1)} %get-tuple-element.88), channel_id=1, source_target_pairs={{0,3},{1,2},{2,1},{4,7},{5,6},{6,5},{8,11},{9,10},{10,9},{12,15},{... | collective-permute-start | bytes 294920 | tf_op jit(solution)/shard_map/ppermute | solution.py:274
  106.3 7.2 %collective-permute-start.18 = (bf16[64,768]{1,0:T(8,128)(2,1)S(1)}, bf16[64,768]{1,0:T(8,128)(2,1)S(1)}, u32[]{:S(2)}, u32[]{:S(2)}) collective-permute-start(bf16[64,768]{1,0:T(8,128)(2,1)S(1)} %get-tuple-element.89), channel_id=1, source_target_pairs={{0,2},{1,3},{2,0},{4,6},{5,7},{6,4},{8,10},{9,11},{10,8},{12,14},{... | collective-permute-start | bytes 294920 | tf_op jit(solution)/shard_map/ppermute | solution.py:274
  110.9 3.2 %collective-permute-start.17 = (bf16[64,768]{1,0:T(8,128)(2,1)S(1)}, bf16[64,768]{1,0:T(8,128)(2,1)S(1)}, u32[]{:S(2)}, u32[]{:S(2)}) collective-permute-start(bf16[64,768]{1,0:T(8,128)(2,1)S(1)} %get-tuple-element.90), channel_id=1, source_target_pairs={{0,1},{1,0},{2,3},{4,5},{5,4},{6,7},{8,9},{9,8},{10,11},{12,13},{1... | collective-permute-start | bytes 294920 | tf_op jit(solution)/shard_map/ppermute | solution.py:274

commit v6 on v5

--- a/solution.py
+++ b/solution.py
@@ -11,7 +11,7 @@
 
 GROUP = 4
 MICROS = 3
-CHUNK = 256
+CHUNK = 384
 PIPE = ("g", "q")
 ANY = pl.BlockSpec(memory_space=pl.ANY)
 VM = pl.BlockSpec(memory_space=pltpu.VMEM)
@@ -301,11 +301,10 @@
     bf = jnp.bfloat16
 
     across = swapped(weight, 2)
+    beside = swapped(weight, 1)
+    own = jnp.concatenate([conv_taps[0], norm_gains, jnp.zeros((4, channels), jnp.float32)])
+    own, base_ids, beside = lax.optimization_barrier((own, base_ids, beside))
     x = encode_bases(base_ids[0, micro], embed_table)
-    later, x = lax.optimization_barrier((weight, x))
-    beside = swapped(later, 1)
-    own = jnp.concatenate([conv_taps[0], norm_gains, jnp.zeros((4, channels), jnp.float32)])
-    own, beside = lax.optimization_barrier((own, beside))
     par = placed(
         jnp.zeros((GROUP,) + own.shape, jnp.float32),
         [own] + [swapped(own, d) for d in range(1, GROUP)],
@@ -346,6 +345,8 @@
         if stage == stages - 2:
             h, e = lax.optimization_barrier((h, e))
             acts = together(h)
+        if stage == 1:
+            acts, e = lax.optimization_barrier((acts, e))
     errors = together(e)
 
     terms = lax.dot_general(acts, errors, (((0,), (0,)), ((), ())), preferred_element_type=jnp.float32)

time: 183 us -> 179 us (0.978)
  the two profiles are of different devices: /device:TPU:128 before, /device:TPU:8 now
where the time goes in v6:
time: 179 us; the launch traced here: 178 us
  blocking collectives  67.3 us (38%)
  waiting for transfers between devices  47.5 us (27%)
  starting transfers between devices  42.9 us (24%)
  Pallas kernels  11.8 us (7%)
  local copies, waits for them, and re-layouts  3.16 us (2%)
  other arithmetic  2.76 us (2%)
    all_to_all x2, blocking collectives, summed_part(): parts = lax.all_to_all(block.reshape(count, -1, block.shape[1]), axis, 0, 0)  38.2 us
    ppermute x8, waiting for transfers between devices, shifted(): return lax.ppermute(block, PIPE, pairs)  30.4 us
    all_to_all x2, blocking collectives, all_parts(): lax.all_to_all(jnp.broadcast_to(block, (count,) + block.shape), axis, 0, 0)  29 us
    ppermute x6, starting transfers between devices, swapped(): return lax.ppermute(block, PIPE, pairs)  15.9 us
    ppermute x6, waiting for transfers between devices, swapped(): return lax.ppermute(block, PIPE, pairs)  15.9 us
    ppermute x6, starting transfers between devices, traded(): return lax.ppermute(block[distance], PIPE, pairs)  14.9 us
    ppermute x8, starting transfers between devices, shifted(): return lax.ppermute(block, PIPE, pairs)  12.1 us
    pallas_call x4, Pallas kernels, forward_stage(): pl.pallas_call(functools.partial(forward_kernel, stage, skip, towers), ou...  4.85 us
  transfers between devices with their start and end apart: 20, of which 8 were waited for; matrix products, arithmetic and copies ran while one was open for 2% of the time, Pallas kernels for 2%

profile of v6, /device:TPU:8, one launch (start us, length us, event | category | flops | bytes accessed | tf_op | source)
XLA Modules:
  0.0 177.6 jit_solution(17386854200442338566)
XLA Ops:
  0.0 2.0 %collective-permute-start.1 = (bf16[768,768]{1,0:T(8,128)(2,1)}, bf16[768,768]{1,0:T(8,128)(2,1)S(1)}, u32[]{:S(2)}, u32[]{:S(2)}) collective-permute-start(bf16[768,768]{1,0:T(8,128)(2,1)} %bitcast.44), channel_id=1, source_target_pairs={{0,1},{1,0},{2,3},{3,2},{4,5},{5,4},{6,7},{7,6},{8,9},{9,8},{10,11... | collective-permute-start | bytes 3538952 | tf_op jit(solution)/shard_map/ppermute | solution.py:223
  2.1 4.3 %collective-permute-start = (bf16[768,768]{1,0:T(8,128)(2,1)}, bf16[768,768]{1,0:T(8,128)(2,1)S(1)}, u32[]{:S(2)}, u32[]{:S(2)}) collective-permute-start(bf16[768,768]{1,0:T(8,128)(2,1)} %bitcast.45), channel_id=1, source_target_pairs={{0,2},{1,3},{2,0},{3,1},{4,6},{5,7},{6,4},{7,5},{8,10},{9,11},{10,... | collective-permute-start | bytes 3538952 | tf_op jit(solution)/shard_map/ppermute | solution.py:223
  8.1 2.1 %collective-permute-start.2 = (f32[8,768]{1,0:T(8,128)S(1)}, f32[8,768]{1,0:T(8,128)S(1)}, u32[]{:S(2)}, u32[]{:S(2)}) collective-permute-start(f32[8,768]{1,0:T(8,128)S(1)} %maximum_maximum_fusion), channel_id=1, source_target_pairs={{0,1},{1,0},{2,3},{3,2},{4,5},{5,4},{6,7},{7,6},{8,9},{9,8},{10,11... | collective-permute-start | bytes 73736 | tf_op jit(solution)/shard_map/ppermute | solution.py:223
  10.2 2.2 %collective-permute-start.3 = (f32[8,768]{1,0:T(8,128)S(1)}, f32[8,768]{1,0:T(8,128)S(1)}, u32[]{:S(2)}, u32[]{:S(2)}) collective-permute-start(f32[8,768]{1,0:T(8,128)S(1)} %maximum_maximum_fusion), channel_id=1, source_target_pairs={{0,2},{1,3},{2,0},{3,1},{4,6},{5,7},{6,4},{7,5},{8,10},{9,11},{10,... | collective-permute-start | bytes 73736 | tf_op jit(solution)/shard_map/ppermute | solution.py:223
  12.4 3.3 %collective-permute-start.4 = (f32[8,768]{1,0:T(8,128)S(1)}, f32[8,768]{1,0:T(8,128)S(1)}, u32[]{:S(2)}, u32[]{:S(2)}) collective-permute-start(f32[8,768]{1,0:T(8,128)S(1)} %maximum_maximum_fusion), channel_id=1, source_target_pairs={{0,3},{1,2},{2,1},{3,0},{4,7},{5,6},{6,5},{7,4},{8,11},{9,10},{10,... | collective-permute-start | bytes 73736 | tf_op jit(solution)/shard_map/ppermute | solution.py:223
  16.4 1.2 convolution_convert_fusion.1.x_ref
  17.7 1.3 copy-done.1
  19.0 1.1 packed.3.rest_1_
  20.0 13.8 %collective-permute-done.3 = f32[8,768]{1,0:T(8,128)S(1)} collective-permute-done((f32[8,768]{1,0:T(8,128)S(1)}, f32[8,768]{1,0:T(8,128)S(1)}, u32[]{:S(2)}, u32[]{:S(2)}) %collective-permute-start.3) | collective-permute-done | bytes 24608 | tf_op jit(solution)/shard_map/ppermute | solution.py:223
  34.0 2.0 %collective-permute-start.5 = (bf16[768,768]{1,0:T(8,128)(2,1)S(1)}, bf16[768,768]{1,0:T(8,128)(2,1)S(1)}, u32[]{:S(2)}, u32[]{:S(2)}) collective-permute-start(bf16[768,768]{1,0:T(8,128)(2,1)S(1)} %collective-permute-done.rest_0_), channel_id=1, source_target_pairs={{0,1},{1,0},{2,3},{3,2},{4,5},{5,4},{6,7},{7,6},{8,9},{9,8},{10,11... | collective-permute-start | bytes 3538952 | tf_op jit(solution)/shard_map/ppermute | solution.py:223
  36.9 1.9 %collective-permute-done.5.rest_0_ = bf16[768,768]{1,0:T(8,128)(2,1)S(1)} collective-permute-done((bf16[768,768]{1,0:T(8,128)(2,1)S(1)}, bf16[768,768]{1,0:T(8,128)(2,1)S(1)}, u32[]{:S(2)}, u32[]{:S(2)}) %collective-permute-start.5) | collective-permute-done | bytes 1179680 | tf_op jit(solution)/shard_map/ppermute | solution.py:223
  39.6 2.4 %ahead0.1 = (bf16[64,768]{1,0:T(8,128)(2,1)S(1)}, f32[4,64,768]{2,1,0:T(8,128)S(1)}, f32[4,64,768]{2,1,0:T(8,128)S(1)}, f32[4,64,128]{2,1,0:T(8,128)S(1)}, bf16[...) custom-call(s32[2]{0:T(128)S(1)} %pad_add_fusion.flags, ...), custom_call_target="tpu_custom_call", output_to_operand_aliasing={{4}: (4, {})} | custom-call | tf_op jit(solution)/shard_map/ahead0/pallas_call | solution.py:123
  42.0 4.3 %collective-permute-start.6 = (bf16[64,768]{1,0:T(8,128)(2,1)S(1)}, bf16[64,768]{1,0:T(8,128)(2,1)S(1)}, u32[]{:S(2)}, u32[]{:S(2)}) collective-permute-start(bf16[64,768]{1,0:T(8,128)(2,1)S(1)} %get-tuple-element.54), channel_id=1, source_target_pairs={{0,4},{1,5},{2,6},{16,20},{17,21},{18,22},{32,36},{33,37},{34,38},... | collective-permute-start | bytes 294920 | tf_op jit(solution)/shard_map/ppermute | solution.py:269
  46.3 2.3 %collective-permute-done.6.x_ref = bf16[64,768]{1,0:T(8,128)(2,1)S(1)} collective-permute-done((bf16[64,768]{1,0:T(8,128)(2,1)S(1)}, bf16[64,768]{1,0:T(8,128)(2,1)S(1)}, u32[]{:S(2)}, u32[]{:S(2)}) %collective-permute-start.6) | collective-permute-done | bytes 98336 | tf_op jit(solution)/shard_map/ppermute | solution.py:269
  48.6 2.5 %collective-permute-start.9 = (bf16[4,64,768]{2,1,0:T(8,128)(2,1)S(1)}, bf16[4,64,768]{2,1,0:T(8,128)(2,1)S(1)}, u32[]{:S(2)}, u32[]{:S(2)}) collective-permute-start(bf16[4,64,768]{2,1,0:T(8,128)(2,1)S(1)} %get-tuple-element.61), channel_id=1, source_target_pairs={{0,12},{1,13},{2,14},{16,28},{17,29},{18,30},{32,44},{33,45},{34,4... | collective-permute-start | bytes 1179656 | tf_op jit(solution)/shard_map/ppermute | solution.py:269
  53.8 10.2 %collective-permute-done.9.rest_0_ = bf16[4,64,768]{2,1,0:T(8,128)(2,1)S(1)} collective-permute-done((bf16[4,64,768]{2,1,0:T(8,128)(2,1)S(1)}, bf16[4,64,768]{2,1,0:T(8,128)(2,1)S(1)}, u32[]{:S(2)}, u32[]{:S(2)}) %collective-permute-start.9) | collective-permute-done | bytes 393248 | tf_op jit(solution)/shard_map/ppermute | solution.py:269
  64.0 1.2 ahead3.1
  67.9 1.3 collective-permute-start.16
  69.2 1.3 collective-permute-start.13
  70.5 3.5 %collective-permute-start.12 = (bf16[64,768]{1,0:T(8,128)(2,1)S(1)}, bf16[64,768]{1,0:T(8,128)(2,1)S(1)}, u32[]{:S(2)}, u32[]{:S(2)}) collective-permute-start(bf16[64,768]{1,0:T(8,128)(2,1)S(1)} %get-tuple-element.95), channel_id=1, source_target_pairs={{0,2},{1,3},{2,0},{4,6},{5,7},{6,4},{8,10},{9,11},{10,8},{12,14},{... | collective-permute-start | bytes 294920 | tf_op jit(solution)/shard_map/ppermute | solution.py:274
  74.0 1.9 %collective-permute-start.11 = (bf16[64,768]{1,0:T(8,128)(2,1)S(1)}, bf16[64,768]{1,0:T(8,128)(2,1)S(1)}, u32[]{:S(2)}, u32[]{:S(2)}) collective-permute-start(bf16[64,768]{1,0:T(8,128)(2,1)S(1)} %get-tuple-element.96), channel_id=1, source_target_pairs={{0,1},{1,0},{2,3},{4,5},{5,4},{6,7},{8,9},{9,8},{10,11},{12,13},{1... | collective-permute-start | bytes 294920 | tf_op jit(solution)/shard_map/ppermute | solution.py:274
  76.6 1.3 collective-permute-start.15
  77.9 17.8 %collective-permute-done.15.g_ref = bf16[64,768]{1,0:T(8,128)(2,1)S(1)} collective-permute-done((bf16[64,768]{1,0:T(8,128)(2,1)S(1)}, bf16[64,768]{1,0:T(8,128)(2,1)S(1)}, u32[]{:S(2)}, u32[]{:S(2)}) %collective-permute-start.15) | collective-permute-done | bytes 98336 | tf_op jit(solution)/shard_map/ppermute | solution.py:269
  95.7 2.5 %behind0.1 = bf16[4,64,768]{2,1,0:T(8,128)(2,1)S(1)} custom-call(s32[2]{0:T(128)S(1)} %pad_add_fusion.flags, bf16[64,768]{1,0:T(8,128)(2,1)S(1)} %collective-permute-done.15.g_ref, bf16[4,768,768]{2,1,0:T(8,128)(2,1)S(1)} %packed.5.w_ref, f32[4,8,768]{2,1,0:T(8,128)S(1)} %bitcast_dynamic-update-slice_fusion.par_ref, ...), custom_call_target="tpu_custom_call", output_to_operand_aliasing={{}: (8, {})} | custom-call | tf_op jit(solution)/shard_map/behind0/pallas_call | solution.py:203
  98.3 1.3 collective-permute-start.19
  99.6 5.1 %collective-permute-start.18 = (bf16[64,768]{1,0:T(8,128)(2,1)S(1)}, bf16[64,768]{1,0:T(8,128)(2,1)S(1)}, u32[]{:S(2)}, u32[]{:S(2)}) collective-permute-start(bf16[64,768]{1,0:T(8,128)(2,1)S(1)} %get-tuple-element.91), channel_id=1, source_target_pairs={{0,2},{1,3},{2,0},{4,6},{5,7},{6,4},{8,10},{9,11},{10,8},{12,14},{... | collective-permute-start | bytes 294920 | tf_op jit(solution)/shard_map/ppermute | solution.py:274
  104.6 1.9 %collective-permute-start.17 = (bf16[64,768]{1,0:T(8,128)(2,1)S(1)}, bf16[64,768]{1,0:T(8,128)(2,1)S(1)}, u32[]{:S(2)}, u32[]{:S(2)}) collective-permute-start(bf16[64,768]{1,0:T(8,128)(2,1)S(1)} %get-tuple-element.92), channel_id=1, source_target_pairs={{0,1},{1,0},{2,3},{4,5},{5,4},{6,7},{8,9},{9,8},{10,11},{12,13},{1... | collective-permute-start | bytes 294920 | tf_op jit(solution)/shard_map/ppermute | solution.py:274
  108.3 20.9 %all_to_all.23 = bf16[4,192,768]{2,1,0:T(8,128)(2,1)S(1)} all-to-all(bf16[4,192,768]{2,1,0:T(8,128)(2,1)S(1)} %bitcast.48), channel_id=1, replica_groups=mesh['y'=8,'x'=4,'g'=4,'q'=4] {'x'}, dimensions={0} | all-to-all | bytes 2359296 | tf_op jit(solution)/shard_map/all_to_all | solution.py:283
  129.5 17.3 %all_to_all.20 = bf16[8,24,768]{2,1,0:T(8,128)(2,1)S(1)} all-to-all(bf16[8,24,768]{2,1,0:T(8,128)(2,1)S(1)} %bitcast.49), channel_id=1, replica_groups=mesh['y'=8,'x'=4,'g'=4,'q'=4] {'y'}, dimensions={0} | all-to-all | bytes 589824 | tf_op jit(solution)/shard_map/all_to_all | solution.py:283
  147.0 13.2 %all_to_all.21 = bf16[8,24,768]{2,1,0:T(8,128)(2,1)S(1)} all-to-all(bf16[8,24,768]{2,1,0:T(8,128)(2,1)S(1)} %broadcast_in_dim.32), channel_id=1, replica_groups=mesh['y'=8,'x'=4,'g'=4,'q'=4] {'y'}, dimensions={0} | all-to-all | bytes 589824 | tf_op jit(solution)/shard_map/all_to_all | solution.py:289
  160.2 15.8 %all_to_all.22 = bf16[4,192,768]{2,1,0:T(8,128)(2,1)S(1)} all-to-all(bf16[4,192,768]{2,1,0:T(8,128)(2,1)S(1)} %broadcast_in_dim.33), channel_id=1, replica_groups=mesh['y'=8,'x'=4,'g'=4,'q'=4] {'x'}, dimensions={0} | all-to-all | bytes 2359296 | tf_op jit(solution)/shard_map/all_to_all | solution.py:289
  176.0 1.6 bitcast_convert_fusion
  (55 shorter events, 12.3 us)
Async XLA Ops:
  0.0 53.8 %copy-start = (bf16[1,3,64,768]{3,2,1,0:T(8,128)(2,1)S(1)}, bf16[1,3,64,768]{3,2,1,0:T(8,128)(2,1)}, u32[]{:S(2)}) copy-start(bf16[1,3,64,768]{3,2,1,0:T(8,128)(2,1)} %param.11) | copy-start | bytes 884740
  0.0 8.1 %collective-permute-start.1 = (bf16[768,768]{1,0:T(8,128)(2,1)}, bf16[768,768]{1,0:T(8,128)(2,1)S(1)}, u32[]{:S(2)}, u32[]{:S(2)}) collective-permute-start(bf16[768,768]{1,0:T(8,128)(2,1)} %bitcast.44), channel_id=1, source_target_pairs={{0,1},{1,0},{2,3},{3,2},{4,5},{5,4},{6,7},{7,6},{8,9},{9,8},{10,11... | collective-permute-start | bytes 3538952 | tf_op jit(solution)/shard_map/ppermute | solution.py:223
  2.1 32.0 %collective-permute-start = (bf16[768,768]{1,0:T(8,128)(2,1)}, bf16[768,768]{1,0:T(8,128)(2,1)S(1)}, u32[]{:S(2)}, u32[]{:S(2)}) collective-permute-start(bf16[768,768]{1,0:T(8,128)(2,1)} %bitcast.45), channel_id=1, source_target_pairs={{0,2},{1,3},{2,0},{3,1},{4,6},{5,7},{6,4},{7,5},{8,10},{9,11},{10,... | collective-permute-start | bytes 3538952 | tf_op jit(solution)/shard_map/ppermute | solution.py:223
  8.1 11.9 %collective-permute-start.2 = (f32[8,768]{1,0:T(8,128)S(1)}, f32[8,768]{1,0:T(8,128)S(1)}, u32[]{:S(2)}, u32[]{:S(2)}) collective-permute-start(f32[8,768]{1,0:T(8,128)S(1)} %maximum_maximum_fusion), channel_id=1, source_target_pairs={{0,1},{1,0},{2,3},{3,2},{4,5},{5,4},{6,7},{7,6},{8,9},{9,8},{10,11... | collective-permute-start | bytes 73736 | tf_op jit(solution)/shard_map/ppermute | solution.py:223
  10.2 23.7 %collective-permute-start.3 = (f32[8,768]{1,0:T(8,128)S(1)}, f32[8,768]{1,0:T(8,128)S(1)}, u32[]{:S(2)}, u32[]{:S(2)}) collective-permute-start(f32[8,768]{1,0:T(8,128)S(1)} %maximum_maximum_fusion), channel_id=1, source_target_pairs={{0,2},{1,3},{2,0},{3,1},{4,6},{5,7},{6,4},{7,5},{8,10},{9,11},{10,... | collective-permute-start | bytes 73736 | tf_op jit(solution)/shard_map/ppermute | solution.py:223
  12.4 21.6 %collective-permute-start.4 = (f32[8,768]{1,0:T(8,128)S(1)}, f32[8,768]{1,0:T(8,128)S(1)}, u32[]{:S(2)}, u32[]{:S(2)}) collective-permute-start(f32[8,768]{1,0:T(8,128)S(1)} %maximum_maximum_fusion), channel_id=1, source_target_pairs={{0,3},{1,2},{2,1},{3,0},{4,7},{5,6},{6,5},{7,4},{8,11},{9,10},{10,... | collective-permute-start | bytes 73736 | tf_op jit(solution)/shard_map/ppermute | solution.py:223
  17.7 1.3 copy-start.1
  34.0 4.7 %collective-permute-start.5 = (bf16[768,768]{1,0:T(8,128)(2,1)S(1)}, bf16[768,768]{1,0:T(8,128)(2,1)S(1)}, u32[]{:S(2)}, u32[]{:S(2)}) collective-permute-start(bf16[768,768]{1,0:T(8,128)(2,1)S(1)} %collective-permute-done.rest_0_), channel_id=1, source_target_pairs={{0,1},{1,0},{2,3},{3,2},{4,5},{5,4},{6,7},{7,6},{8,9},{9,8},{10,11... | collective-permute-start | bytes 3538952 | tf_op jit(solution)/shard_map/ppermute | solution.py:223
  42.0 6.6 %collective-permute-start.6 = (bf16[64,768]{1,0:T(8,128)(2,1)S(1)}, bf16[64,768]{1,0:T(8,128)(2,1)S(1)}, u32[]{:S(2)}, u32[]{:S(2)}) collective-permute-start(bf16[64,768]{1,0:T(8,128)(2,1)S(1)} %get-tuple-element.54), channel_id=1, source_target_pairs={{0,4},{1,5},{2,6},{16,20},{17,21},{18,22},{32,36},{33,37},{34,38},... | collective-permute-start | bytes 294920 | tf_op jit(solution)/shard_map/ppermute | solution.py:269
  48.6 15.4 %collective-permute-start.9 = (bf16[4,64,768]{2,1,0:T(8,128)(2,1)S(1)}, bf16[4,64,768]{2,1,0:T(8,128)(2,1)S(1)}, u32[]{:S(2)}, u32[]{:S(2)}) collective-permute-start(bf16[4,64,768]{2,1,0:T(8,128)(2,1)S(1)} %get-tuple-element.61), channel_id=1, source_target_pairs={{0,12},{1,13},{2,14},{16,28},{17,29},{18,30},{32,44},{33,45},{34,4... | collective-permute-start | bytes 1179656 | tf_op jit(solution)/shard_map/ppermute | solution.py:269
  51.8 0.7 collective-permute-start.7
  53.1 0.7 collective-permute-start.8
  65.9 0.7 collective-permute-start.10
  67.2 8.7 %collective-permute-start.14 = (bf16[64,768]{1,0:T(8,128)(2,1)S(1)}, bf16[64,768]{1,0:T(8,128)(2,1)S(1)}, u32[]{:S(2)}, u32[]{:S(2)}) collective-permute-start(bf16[64,768]{1,0:T(8,128)(2,1)S(1)} %get-tuple-element.76), channel_id=1, source_target_pairs={{8,4},{9,5},{10,6},{24,20},{25,21},{26,22},{40,36},{41,37},{42,38}... | collective-permute-start | bytes 294920 | tf_op jit(solution)/shard_map/ppermute | solution.py:269
  67.9 27.8 %collective-permute-start.16 = (bf16[4,64,768]{2,1,0:T(8,128)(2,1)S(1)}, bf16[4,64,768]{2,1,0:T(8,128)(2,1)S(1)}, u32[]{:S(2)}, u32[]{:S(2)}) collective-permute-start(bf16[4,64,768]{2,1,0:T(8,128)(2,1)S(1)} %get-tuple-element.87), channel_id=1, source_target_pairs={{12,0},{13,1},{14,2},{28,16},{29,17},{30,18},{44,32},{45,33},{46,3... | collective-permute-start | bytes 1179656 | tf_op jit(solution)/shard_map/ppermute | solution.py:269
  69.2 8.6 %collective-permute-start.13 = (bf16[64,768]{1,0:T(8,128)(2,1)S(1)}, bf16[64,768]{1,0:T(8,128)(2,1)S(1)}, u32[]{:S(2)}, u32[]{:S(2)}) collective-permute-start(bf16[64,768]{1,0:T(8,128)(2,1)S(1)} %get-tuple-element.94), channel_id=1, source_target_pairs={{0,3},{1,2},{2,1},{4,7},{5,6},{6,5},{8,11},{9,10},{10,9},{12,15},{... | collective-permute-start | bytes 294920 | tf_op jit(solution)/shard_map/ppermute | solution.py:274
  70.5 7.3 %collective-permute-start.12 = (bf16[64,768]{1,0:T(8,128)(2,1)S(1)}, bf16[64,768]{1,0:T(8,128)(2,1)S(1)}, u32[]{:S(2)}, u32[]{:S(2)}) collective-permute-start(bf16[64,768]{1,0:T(8,128)(2,1)S(1)} %get-tuple-element.95), channel_id=1, source_target_pairs={{0,2},{1,3},{2,0},{4,6},{5,7},{6,4},{8,10},{9,11},{10,8},{12,14},{... | collective-permute-start | bytes 294920 | tf_op jit(solution)/shard_map/ppermute | solution.py:274
  74.0 3.9 %collective-permute-start.11 = (bf16[64,768]{1,0:T(8,128)(2,1)S(1)}, bf16[64,768]{1,0:T(8,128)(2,1)S(1)}, u32[]{:S(2)}, u32[]{:S(2)}) collective-permute-start(bf16[64,768]{1,0:T(8,128)(2,1)S(1)} %get-tuple-element.96), channel_id=1, source_target_pairs={{0,1},{1,0},{2,3},{4,5},{5,4},{6,7},{8,9},{9,8},{10,11},{12,13},{1... | collective-permute-start | bytes 294920 | tf_op jit(solution)/shard_map/ppermute | solution.py:274
  76.6 19.2 %collective-permute-start.15 = (bf16[64,768]{1,0:T(8,128)(2,1)S(1)}, bf16[64,768]{1,0:T(8,128)(2,1)S(1)}, u32[]{:S(2)}, u32[]{:S(2)}) collective-permute-start(bf16[64,768]{1,0:T(8,128)(2,1)S(1)} %get-tuple-element.83), channel_id=1, source_target_pairs={{4,0},{5,1},{6,2},{20,16},{21,17},{22,18},{36,32},{37,33},{38,34},... | collective-permute-start | bytes 294920 | tf_op jit(solution)/shard_map/ppermute | solution.py:269
  98.3 8.3 %collective-permute-start.19 = (bf16[64,768]{1,0:T(8,128)(2,1)S(1)}, bf16[64,768]{1,0:T(8,128)(2,1)S(1)}, u32[]{:S(2)}, u32[]{:S(2)}) collective-permute-start(bf16[64,768]{1,0:T(8,128)(2,1)S(1)} %get-tuple-element.90), channel_id=1, source_target_pairs={{0,3},{1,2},{2,1},{4,7},{5,6},{6,5},{8,11},{9,10},{10,9},{12,15},{... | collective-permute-start | bytes 294920 | tf_op jit(solution)/shard_map/ppermute | solution.py:274
  99.6 7.6 %collective-permute-start.18 = (bf16[64,768]{1,0:T(8,128)(2,1)S(1)}, bf16[64,768]{1,0:T(8,128)(2,1)S(1)}, u32[]{:S(2)}, u32[]{:S(2)}) collective-permute-start(bf16[64,768]{1,0:T(8,128)(2,1)S(1)} %get-tuple-element.91), channel_id=1, source_target_pairs={{0,2},{1,3},{2,0},{4,6},{5,7},{6,4},{8,10},{9,11},{10,8},{12,14},{... | collective-permute-start | bytes 294920 | tf_op jit(solution)/shard_map/ppermute | solution.py:274
  104.6 3.2 %collective-permute-start.17 = (bf16[64,768]{1,0:T(8,128)(2,1)S(1)}, bf16[64,768]{1,0:T(8,128)(2,1)S(1)}, u32[]{:S(2)}, u32[]{:S(2)}) collective-permute-start(bf16[64,768]{1,0:T(8,128)(2,1)S(1)} %get-tuple-element.92), channel_id=1, source_target_pairs={{0,1},{1,0},{2,3},{4,5},{5,4},{6,7},{8,9},{9,8},{10,11},{12,13},{1... | collective-permute-start | bytes 294920 | tf_op jit(solution)/shard_map/ppermute | solution.py:274

commit v7 on v6

--- a/solution.py
+++ b/solution.py
@@ -13,6 +13,7 @@
 MICROS = 3
 CHUNK = 384
 PIPE = ("g", "q")
+NEAR = ("yl", "x")
 ANY = pl.BlockSpec(memory_space=pl.ANY)
 VM = pl.BlockSpec(memory_space=pltpu.VMEM)
 SM = pl.BlockSpec(memory_space=pltpu.SMEM)
@@ -350,18 +351,20 @@
     errors = together(e)
 
     terms = lax.dot_general(acts, errors, (((0,), (0,)), ((), ())), preferred_element_type=jnp.float32)
-    factor = 1.0 / math.sqrt(lax.axis_size(("y", "x")) * MICROS * row_count)
-    part = summed_part(terms.astype(bf), "x").astype(bf)
-    part = (summed_part(part, "y") * factor).astype(bf)
-    whole = all_parts(all_parts(part, "y"), "x")
+    factor = 1.0 / math.sqrt(lax.axis_size(NEAR + ("yh",)) * MICROS * row_count)
+    part = summed_part(terms.astype(bf), NEAR).astype(bf)
+    part = (summed_part(part, "yh") * factor).astype(bf)
+    whole = all_parts(all_parts(part, "yh"), NEAR)
     return whole.astype(jnp.float32)[None]
 
 
 def solution(mesh):
     replicas, _ = mesh.devices.shape
     wide = math.gcd(4, replicas)
-    grid = Mesh(mesh.devices.reshape(replicas // wide, wide, -1, GROUP), ("y", "x", "g", "q"))
-    windows = P(("y", "x"), None, None, None)
+    low = math.gcd(2, replicas // wide)
+    shape = (replicas // (wide * low), low, wide, -1, GROUP)
+    grid = Mesh(mesh.devices.reshape(shape), ("yh", "yl", "x", "g", "q"))
+    windows = P(("yh", "yl", "x"), None, None, None)
     return jax.shard_map(
         shards,
         mesh=grid,

time: 179 us -> 175 us (0.978)
  blocking collectives: 67.3 us -> 63.7 us
    all_to_all x2, blocking collectives: 38.2 us -> 36.3 us  [summed_part(): parts = lax.all_to_all(block.reshape(count, -1, block.shape[1]), axis, 0, 0)]
where the time goes in v7:
time: 175 us; the launch traced here: 174 us
  blocking collectives  63.7 us (36%)
  waiting for transfers between devices  47.5 us (27%)
  starting transfers between devices  42.9 us (25%)
  Pallas kernels  11.8 us (7%)
  local copies, waits for them, and re-layouts  3.15 us (2%)
  other arithmetic  2.63 us (2%)
    all_to_all x2, blocking collectives, summed_part(): parts = lax.all_to_all(block.reshape(count, -1, block.shape[1]), axis, 0, 0)  36.3 us
    ppermute x8, waiting for transfers between devices, shifted(): return lax.ppermute(block, PIPE, pairs)  30.4 us
    all_to_all x2, blocking collectives, all_parts(): lax.all_to_all(jnp.broadcast_to(block, (count,) + block.shape), axis, 0, 0)  27.4 us
    ppermute x6, starting transfers between devices, swapped(): return lax.ppermute(block, PIPE, pairs)  15.9 us
    ppermute x6, waiting for transfers between devices, swapped(): return lax.ppermute(block, PIPE, pairs)  15.9 us
    ppermute x6, starting transfers between devices, traded(): return lax.ppermute(block[distance], PIPE, pairs)  14.9 us
    ppermute x8, starting transfers between devices, shifted(): return lax.ppermute(block, PIPE, pairs)  12.1 us
    pallas_call x4, Pallas kernels, forward_stage(): pl.pallas_call(functools.partial(forward_kernel, stage, skip, towers), ou...  4.85 us
  transfers between devices with their start and end apart: 20, of which 8 were waited for; matrix products, arithmetic and copies ran while one was open for 2% of the time, Pallas kernels for 2%

profile of v7, /device:TPU:8, one launch (start us, length us, event | category | flops | bytes accessed | tf_op | source)
XLA Modules:
  0.0 173.9 jit_solution(16601941475069497276)
XLA Ops:
  0.0 2.0 %collective-permute-start.1 = (bf16[768,768]{1,0:T(8,128)(2,1)}, bf16[768,768]{1,0:T(8,128)(2,1)S(1)}, u32[]{:S(2)}, u32[]{:S(2)}) collective-permute-start(bf16[768,768]{1,0:T(8,128)(2,1)} %bitcast.44), channel_id=1, source_target_pairs={{0,1},{1,0},{2,3},{3,2},{4,5},{5,4},{6,7},{7,6},{8,9},{9,8},{10,11... | collective-permute-start | bytes 3538952 | tf_op jit(solution)/shard_map/ppermute | solution.py:224
  2.1 4.3 %collective-permute-start = (bf16[768,768]{1,0:T(8,128)(2,1)}, bf16[768,768]{1,0:T(8,128)(2,1)S(1)}, u32[]{:S(2)}, u32[]{:S(2)}) collective-permute-start(bf16[768,768]{1,0:T(8,128)(2,1)} %bitcast.45), channel_id=1, source_target_pairs={{0,2},{1,3},{2,0},{3,1},{4,6},{5,7},{6,4},{7,5},{8,10},{9,11},{10,... | collective-permute-start | bytes 3538952 | tf_op jit(solution)/shard_map/ppermute | solution.py:224
  8.1 2.1 %collective-permute-start.2 = (f32[8,768]{1,0:T(8,128)S(1)}, f32[8,768]{1,0:T(8,128)S(1)}, u32[]{:S(2)}, u32[]{:S(2)}) collective-permute-start(f32[8,768]{1,0:T(8,128)S(1)} %maximum_maximum_fusion), channel_id=1, source_target_pairs={{0,1},{1,0},{2,3},{3,2},{4,5},{5,4},{6,7},{7,6},{8,9},{9,8},{10,11... | collective-permute-start | bytes 73736 | tf_op jit(solution)/shard_map/ppermute | solution.py:224
  10.2 2.2 %collective-permute-start.3 = (f32[8,768]{1,0:T(8,128)S(1)}, f32[8,768]{1,0:T(8,128)S(1)}, u32[]{:S(2)}, u32[]{:S(2)}) collective-permute-start(f32[8,768]{1,0:T(8,128)S(1)} %maximum_maximum_fusion), channel_id=1, source_target_pairs={{0,2},{1,3},{2,0},{3,1},{4,6},{5,7},{6,4},{7,5},{8,10},{9,11},{10,... | collective-permute-start | bytes 73736 | tf_op jit(solution)/shard_map/ppermute | solution.py:224
  12.4 3.3 %collective-permute-start.4 = (f32[8,768]{1,0:T(8,128)S(1)}, f32[8,768]{1,0:T(8,128)S(1)}, u32[]{:S(2)}, u32[]{:S(2)}) collective-permute-start(f32[8,768]{1,0:T(8,128)S(1)} %maximum_maximum_fusion), channel_id=1, source_target_pairs={{0,3},{1,2},{2,1},{3,0},{4,7},{5,6},{6,5},{7,4},{8,11},{9,10},{10,... | collective-permute-start | bytes 73736 | tf_op jit(solution)/shard_map/ppermute | solution.py:224
  16.4 1.2 convolution_convert_fusion.1.x_ref
  17.7 1.3 copy-done.1
  19.0 1.1 packed.3.rest_1_
  20.0 13.8 %collective-permute-done.3 = f32[8,768]{1,0:T(8,128)S(1)} collective-permute-done((f32[8,768]{1,0:T(8,128)S(1)}, f32[8,768]{1,0:T(8,128)S(1)}, u32[]{:S(2)}, u32[]{:S(2)}) %collective-permute-start.3) | collective-permute-done | bytes 24608 | tf_op jit(solution)/shard_map/ppermute | solution.py:224
  34.0 2.0 %collective-permute-start.5 = (bf16[768,768]{1,0:T(8,128)(2,1)S(1)}, bf16[768,768]{1,0:T(8,128)(2,1)S(1)}, u32[]{:S(2)}, u32[]{:S(2)}) collective-permute-start(bf16[768,768]{1,0:T(8,128)(2,1)S(1)} %collective-permute-done.rest_0_), channel_id=1, source_target_pairs={{0,1},{1,0},{2,3},{3,2},{4,5},{5,4},{6,7},{7,6},{8,9},{9,8},{10,11... | collective-permute-start | bytes 3538952 | tf_op jit(solution)/shard_map/ppermute | solution.py:224
  36.9 1.9 %collective-permute-done.5.rest_0_ = bf16[768,768]{1,0:T(8,128)(2,1)S(1)} collective-permute-done((bf16[768,768]{1,0:T(8,128)(2,1)S(1)}, bf16[768,768]{1,0:T(8,128)(2,1)S(1)}, u32[]{:S(2)}, u32[]{:S(2)}) %collective-permute-start.5) | collective-permute-done | bytes 1179680 | tf_op jit(solution)/shard_map/ppermute | solution.py:224
  39.6 2.4 %ahead0.1 = (bf16[64,768]{1,0:T(8,128)(2,1)S(1)}, f32[4,64,768]{2,1,0:T(8,128)S(1)}, f32[4,64,768]{2,1,0:T(8,128)S(1)}, f32[4,64,128]{2,1,0:T(8,128)S(1)}, bf16[...) custom-call(s32[2]{0:T(128)S(1)} %pad_add_fusion.flags, ...), custom_call_target="tpu_custom_call", output_to_operand_aliasing={{4}: (4, {})} | custom-call | tf_op jit(solution)/shard_map/ahead0/pallas_call | solution.py:124
  42.0 4.3 %collective-permute-start.6 = (bf16[64,768]{1,0:T(8,128)(2,1)S(1)}, bf16[64,768]{1,0:T(8,128)(2,1)S(1)}, u32[]{:S(2)}, u32[]{:S(2)}) collective-permute-start(bf16[64,768]{1,0:T(8,128)(2,1)S(1)} %get-tuple-element.54), channel_id=1, source_target_pairs={{0,4},{1,5},{2,6},{16,20},{17,21},{18,22},{32,36},{33,37},{34,38},... | collective-permute-start | bytes 294920 | tf_op jit(solution)/shard_map/ppermute | solution.py:270
  46.3 2.3 %collective-permute-done.6.x_ref = bf16[64,768]{1,0:T(8,128)(2,1)S(1)} collective-permute-done((bf16[64,768]{1,0:T(8,128)(2,1)S(1)}, bf16[64,768]{1,0:T(8,128)(2,1)S(1)}, u32[]{:S(2)}, u32[]{:S(2)}) %collective-permute-start.6) | collective-permute-done | bytes 98336 | tf_op jit(solution)/shard_map/ppermute | solution.py:270
  48.6 2.5 %collective-permute-start.9 = (bf16[4,64,768]{2,1,0:T(8,128)(2,1)S(1)}, bf16[4,64,768]{2,1,0:T(8,128)(2,1)S(1)}, u32[]{:S(2)}, u32[]{:S(2)}) collective-permute-start(bf16[4,64,768]{2,1,0:T(8,128)(2,1)S(1)} %get-tuple-element.61), channel_id=1, source_target_pairs={{0,12},{1,13},{2,14},{16,28},{17,29},{18,30},{32,44},{33,45},{34,4... | collective-permute-start | bytes 1179656 | tf_op jit(solution)/shard_map/ppermute | solution.py:270
  53.8 10.2 %collective-permute-done.9.rest_0_ = bf16[4,64,768]{2,1,0:T(8,128)(2,1)S(1)} collective-permute-done((bf16[4,64,768]{2,1,0:T(8,128)(2,1)S(1)}, bf16[4,64,768]{2,1,0:T(8,128)(2,1)S(1)}, u32[]{:S(2)}, u32[]{:S(2)}) %collective-permute-start.9) | collective-permute-done | bytes 393248 | tf_op jit(solution)/shard_map/ppermute | solution.py:270
  64.0 1.2 ahead3.1
  67.9 1.3 collective-permute-start.16
  69.2 1.3 collective-permute-start.13
  70.5 3.5 %collective-permute-start.12 = (bf16[64,768]{1,0:T(8,128)(2,1)S(1)}, bf16[64,768]{1,0:T(8,128)(2,1)S(1)}, u32[]{:S(2)}, u32[]{:S(2)}) collective-permute-start(bf16[64,768]{1,0:T(8,128)(2,1)S(1)} %get-tuple-element.95), channel_id=1, source_target_pairs={{0,2},{1,3},{2,0},{4,6},{5,7},{6,4},{8,10},{9,11},{10,8},{12,14},{... | collective-permute-start | bytes 294920 | tf_op jit(solution)/shard_map/ppermute | solution.py:275
  74.0 1.9 %collective-permute-start.11 = (bf16[64,768]{1,0:T(8,128)(2,1)S(1)}, bf16[64,768]{1,0:T(8,128)(2,1)S(1)}, u32[]{:S(2)}, u32[]{:S(2)}) collective-permute-start(bf16[64,768]{1,0:T(8,128)(2,1)S(1)} %get-tuple-element.96), channel_id=1, source_target_pairs={{0,1},{1,0},{2,3},{4,5},{5,4},{6,7},{8,9},{9,8},{10,11},{12,13},{1... | collective-permute-start | bytes 294920 | tf_op jit(solution)/shard_map/ppermute | solution.py:275
  76.6 1.3 collective-permute-start.15
  77.9 17.8 %collective-permute-done.15.g_ref = bf16[64,768]{1,0:T(8,128)(2,1)S(1)} collective-permute-done((bf16[64,768]{1,0:T(8,128)(2,1)S(1)}, bf16[64,768]{1,0:T(8,128)(2,1)S(1)}, u32[]{:S(2)}, u32[]{:S(2)}) %collective-permute-start.15) | collective-permute-done | bytes 98336 | tf_op jit(solution)/shard_map/ppermute | solution.py:270
  95.7 2.5 %behind0.1 = bf16[4,64,768]{2,1,0:T(8,128)(2,1)S(1)} custom-call(s32[2]{0:T(128)S(1)} %pad_add_fusion.flags, bf16[64,768]{1,0:T(8,128)(2,1)S(1)} %collective-permute-done.15.g_ref, bf16[4,768,768]{2,1,0:T(8,128)(2,1)S(1)} %packed.5.w_ref, f32[4,8,768]{2,1,0:T(8,128)S(1)} %bitcast_dynamic-update-slice_fusion.par_ref, ...), custom_call_target="tpu_custom_call", output_to_operand_aliasing={{}: (8, {})} | custom-call | tf_op jit(solution)/shard_map/behind0/pallas_call | solution.py:204
  98.3 1.3 collective-permute-start.19
  99.6 5.1 %collective-permute-start.18 = (bf16[64,768]{1,0:T(8,128)(2,1)S(1)}, bf16[64,768]{1,0:T(8,128)(2,1)S(1)}, u32[]{:S(2)}, u32[]{:S(2)}) collective-permute-start(bf16[64,768]{1,0:T(8,128)(2,1)S(1)} %get-tuple-element.91), channel_id=1, source_target_pairs={{0,2},{1,3},{2,0},{4,6},{5,7},{6,4},{8,10},{9,11},{10,8},{12,14},{... | collective-permute-start | bytes 294920 | tf_op jit(solution)/shard_map/ppermute | solution.py:275
  104.6 1.9 %collective-permute-start.17 = (bf16[64,768]{1,0:T(8,128)(2,1)S(1)}, bf16[64,768]{1,0:T(8,128)(2,1)S(1)}, u32[]{:S(2)}, u32[]{:S(2)}) collective-permute-start(bf16[64,768]{1,0:T(8,128)(2,1)S(1)} %get-tuple-element.92), channel_id=1, source_target_pairs={{0,1},{1,0},{2,3},{4,5},{5,4},{6,7},{8,9},{9,8},{10,11},{12,13},{1... | collective-permute-start | bytes 294920 | tf_op jit(solution)/shard_map/ppermute | solution.py:275
  108.3 21.6 %all_to_all.23 = bf16[8,96,768]{2,1,0:T(8,128)(2,1)S(1)} all-to-all(bf16[8,96,768]{2,1,0:T(8,128)(2,1)S(1)} %bitcast.48), channel_id=1, replica_groups=mesh['yh'=4,'yl'=2,'x'=4,'g'=4,'q'=4] {'yl','x'}, dimensions={0} | all-to-all | bytes 2359296 | tf_op jit(solution)/shard_map/all_to_all | solution.py:284
  130.1 14.7 %all_to_all.20 = bf16[4,24,768]{2,1,0:T(8,128)(2,1)S(1)} all-to-all(bf16[4,24,768]{2,1,0:T(8,128)(2,1)S(1)} %bitcast.49), channel_id=1, replica_groups=mesh['yh'=4,'yl'=2,'x'=4,'g'=4,'q'=4] {'yh'}, dimensions={0} | all-to-all | bytes 294912 | tf_op jit(solution)/shard_map/all_to_all | solution.py:284
  144.9 11.0 %all_to_all.21 = bf16[4,24,768]{2,1,0:T(8,128)(2,1)S(1)} all-to-all(bf16[4,24,768]{2,1,0:T(8,128)(2,1)S(1)} %broadcast_in_dim.32), channel_id=1, replica_groups=mesh['yh'=4,'yl'=2,'x'=4,'g'=4,'q'=4] {'yh'}, dimensions={0} | all-to-all | bytes 294912 | tf_op jit(solution)/shard_map/all_to_all | solution.py:290
  156.0 16.3 %all_to_all.22 = bf16[8,96,768]{2,1,0:T(8,128)(2,1)S(1)} all-to-all(bf16[8,96,768]{2,1,0:T(8,128)(2,1)S(1)} %broadcast_in_dim.33), channel_id=1, replica_groups=mesh['yh'=4,'yl'=2,'x'=4,'g'=4,'q'=4] {'yl','x'}, dimensions={0} | all-to-all | bytes 2359296 | tf_op jit(solution)/shard_map/all_to_all | solution.py:290
  172.3 1.6 bitcast_convert_fusion
  (55 shorter events, 12.2 us)
Async XLA Ops:
  0.0 53.8 %copy-start = (bf16[1,3,64,768]{3,2,1,0:T(8,128)(2,1)S(1)}, bf16[1,3,64,768]{3,2,1,0:T(8,128)(2,1)}, u32[]{:S(2)}) copy-start(bf16[1,3,64,768]{3,2,1,0:T(8,128)(2,1)} %param.11) | copy-start | bytes 884740
  0.0 8.1 %collective-permute-start.1 = (bf16[768,768]{1,0:T(8,128)(2,1)}, bf16[768,768]{1,0:T(8,128)(2,1)S(1)}, u32[]{:S(2)}, u32[]{:S(2)}) collective-permute-start(bf16[768,768]{1,0:T(8,128)(2,1)} %bitcast.44), channel_id=1, source_target_pairs={{0,1},{1,0},{2,3},{3,2},{4,5},{5,4},{6,7},{7,6},{8,9},{9,8},{10,11... | collective-permute-start | bytes 3538952 | tf_op jit(solution)/shard_map/ppermute | solution.py:224
  2.1 32.0 %collective-permute-start = (bf16[768,768]{1,0:T(8,128)(2,1)}, bf16[768,768]{1,0:T(8,128)(2,1)S(1)}, u32[]{:S(2)}, u32[]{:S(2)}) collective-permute-start(bf16[768,768]{1,0:T(8,128)(2,1)} %bitcast.45), channel_id=1, source_target_pairs={{0,2},{1,3},{2,0},{3,1},{4,6},{5,7},{6,4},{7,5},{8,10},{9,11},{10,... | collective-permute-start | bytes 3538952 | tf_op jit(solution)/shard_map/ppermute | solution.py:224
  8.1 11.9 %collective-permute-start.2 = (f32[8,768]{1,0:T(8,128)S(1)}, f32[8,768]{1,0:T(8,128)S(1)}, u32[]{:S(2)}, u32[]{:S(2)}) collective-permute-start(f32[8,768]{1,0:T(8,128)S(1)} %maximum_maximum_fusion), channel_id=1, source_target_pairs={{0,1},{1,0},{2,3},{3,2},{4,5},{5,4},{6,7},{7,6},{8,9},{9,8},{10,11... | collective-permute-start | bytes 73736 | tf_op jit(solution)/shard_map/ppermute | solution.py:224
  10.2 23.7 %collective-permute-start.3 = (f32[8,768]{1,0:T(8,128)S(1)}, f32[8,768]{1,0:T(8,128)S(1)}, u32[]{:S(2)}, u32[]{:S(2)}) collective-permute-start(f32[8,768]{1,0:T(8,128)S(1)} %maximum_maximum_fusion), channel_id=1, source_target_pairs={{0,2},{1,3},{2,0},{3,1},{4,6},{5,7},{6,4},{7,5},{8,10},{9,11},{10,... | collective-permute-start | bytes 73736 | tf_op jit(solution)/shard_map/ppermute | solution.py:224
  12.4 21.6 %collective-permute-start.4 = (f32[8,768]{1,0:T(8,128)S(1)}, f32[8,768]{1,0:T(8,128)S(1)}, u32[]{:S(2)}, u32[]{:S(2)}) collective-permute-start(f32[8,768]{1,0:T(8,128)S(1)} %maximum_maximum_fusion), channel_id=1, source_target_pairs={{0,3},{1,2},{2,1},{3,0},{4,7},{5,6},{6,5},{7,4},{8,11},{9,10},{10,... | collective-permute-start | bytes 73736 | tf_op jit(solution)/shard_map/ppermute | solution.py:224
  17.7 1.3 copy-start.1
  34.0 4.7 %collective-permute-start.5 = (bf16[768,768]{1,0:T(8,128)(2,1)S(1)}, bf16[768,768]{1,0:T(8,128)(2,1)S(1)}, u32[]{:S(2)}, u32[]{:S(2)}) collective-permute-start(bf16[768,768]{1,0:T(8,128)(2,1)S(1)} %collective-permute-done.rest_0_), channel_id=1, source_target_pairs={{0,1},{1,0},{2,3},{3,2},{4,5},{5,4},{6,7},{7,6},{8,9},{9,8},{10,11... | collective-permute-start | bytes 3538952 | tf_op jit(solution)/shard_map/ppermute | solution.py:224
  42.0 6.6 %collective-permute-start.6 = (bf16[64,768]{1,0:T(8,128)(2,1)S(1)}, bf16[64,768]{1,0:T(8,128)(2,1)S(1)}, u32[]{:S(2)}, u32[]{:S(2)}) collective-permute-start(bf16[64,768]{1,0:T(8,128)(2,1)S(1)} %get-tuple-element.54), channel_id=1, source_target_pairs={{0,4},{1,5},{2,6},{16,20},{17,21},{18,22},{32,36},{33,37},{34,38},... | collective-permute-start | bytes 294920 | tf_op jit(solution)/shard_map/ppermute | solution.py:270
  48.6 15.4 %collective-permute-start.9 = (bf16[4,64,768]{2,1,0:T(8,128)(2,1)S(1)}, bf16[4,64,768]{2,1,0:T(8,128)(2,1)S(1)}, u32[]{:S(2)}, u32[]{:S(2)}) collective-permute-start(bf16[4,64,768]{2,1,0:T(8,128)(2,1)S(1)} %get-tuple-element.61), channel_id=1, source_target_pairs={{0,12},{1,13},{2,14},{16,28},{17,29},{18,30},{32,44},{33,45},{34,4... | collective-permute-start | bytes 1179656 | tf_op jit(solution)/shard_map/ppermute | solution.py:270
  51.8 0.7 collective-permute-start.7
  53.1 0.7 collective-permute-start.8
  65.9 0.7 collective-permute-start.10
  67.2 8.7 %collective-permute-start.14 = (bf16[64,768]{1,0:T(8,128)(2,1)S(1)}, bf16[64,768]{1,0:T(8,128)(2,1)S(1)}, u32[]{:S(2)}, u32[]{:S(2)}) collective-permute-start(bf16[64,768]{1,0:T(8,128)(2,1)S(1)} %get-tuple-element.76), channel_id=1, source_target_pairs={{8,4},{9,5},{10,6},{24,20},{25,21},{26,22},{40,36},{41,37},{42,38}... | collective-permute-start | bytes 294920 | tf_op jit(solution)/shard_map/ppermute | solution.py:270
  67.9 27.8 %collective-permute-start.16 = (bf16[4,64,768]{2,1,0:T(8,128)(2,1)S(1)}, bf16[4,64,768]{2,1,0:T(8,128)(2,1)S(1)}, u32[]{:S(2)}, u32[]{:S(2)}) collective-permute-start(bf16[4,64,768]{2,1,0:T(8,128)(2,1)S(1)} %get-tuple-element.87), channel_id=1, source_target_pairs={{12,0},{13,1},{14,2},{28,16},{29,17},{30,18},{44,32},{45,33},{46,3... | collective-permute-start | bytes 1179656 | tf_op jit(solution)/shard_map/ppermute | solution.py:270
  69.2 8.6 %collective-permute-start.13 = (bf16[64,768]{1,0:T(8,128)(2,1)S(1)}, bf16[64,768]{1,0:T(8,128)(2,1)S(1)}, u32[]{:S(2)}, u32[]{:S(2)}) collective-permute-start(bf16[64,768]{1,0:T(8,128)(2,1)S(1)} %get-tuple-element.94), channel_id=1, source_target_pairs={{0,3},{1,2},{2,1},{4,7},{5,6},{6,5},{8,11},{9,10},{10,9},{12,15},{... | collective-permute-start | bytes 294920 | tf_op jit(solution)/shard_map/ppermute | solution.py:275
  70.5 7.3 %collective-permute-start.12 = (bf16[64,768]{1,0:T(8,128)(2,1)S(1)}, bf16[64,768]{1,0:T(8,128)(2,1)S(1)}, u32[]{:S(2)}, u32[]{:S(2)}) collective-permute-start(bf16[64,768]{1,0:T(8,128)(2,1)S(1)} %get-tuple-element.95), channel_id=1, source_target_pairs={{0,2},{1,3},{2,0},{4,6},{5,7},{6,4},{8,10},{9,11},{10,8},{12,14},{... | collective-permute-start | bytes 294920 | tf_op jit(solution)/shard_map/ppermute | solution.py:275
  74.0 3.9 %collective-permute-start.11 = (bf16[64,768]{1,0:T(8,128)(2,1)S(1)}, bf16[64,768]{1,0:T(8,128)(2,1)S(1)}, u32[]{:S(2)}, u32[]{:S(2)}) collective-permute-start(bf16[64,768]{1,0:T(8,128)(2,1)S(1)} %get-tuple-element.96), channel_id=1, source_target_pairs={{0,1},{1,0},{2,3},{4,5},{5,4},{6,7},{8,9},{9,8},{10,11},{12,13},{1... | collective-permute-start | bytes 294920 | tf_op jit(solution)/shard_map/ppermute | solution.py:275
  76.6 19.2 %collective-permute-start.15 = (bf16[64,768]{1,0:T(8,128)(2,1)S(1)}, bf16[64,768]{1,0:T(8,128)(2,1)S(1)}, u32[]{:S(2)}, u32[]{:S(2)}) collective-permute-start(bf16[64,768]{1,0:T(8,128)(2,1)S(1)} %get-tuple-element.83), channel_id=1, source_target_pairs={{4,0},{5,1},{6,2},{20,16},{21,17},{22,18},{36,32},{37,33},{38,34},... | collective-permute-start | bytes 294920 | tf_op jit(solution)/shard_map/ppermute | solution.py:270
  98.3 8.3 %collective-permute-start.19 = (bf16[64,768]{1,0:T(8,128)(2,1)S(1)}, bf16[64,768]{1,0:T(8,128)(2,1)S(1)}, u32[]{:S(2)}, u32[]{:S(2)}) collective-permute-start(bf16[64,768]{1,0:T(8,128)(2,1)S(1)} %get-tuple-element.90), channel_id=1, source_target_pairs={{0,3},{1,2},{2,1},{4,7},{5,6},{6,5},{8,11},{9,10},{10,9},{12,15},{... | collective-permute-start | bytes 294920 | tf_op jit(solution)/shard_map/ppermute | solution.py:275
  99.6 7.6 %collective-permute-start.18 = (bf16[64,768]{1,0:T(8,128)(2,1)S(1)}, bf16[64,768]{1,0:T(8,128)(2,1)S(1)}, u32[]{:S(2)}, u32[]{:S(2)}) collective-permute-start(bf16[64,768]{1,0:T(8,128)(2,1)S(1)} %get-tuple-element.91), channel_id=1, source_target_pairs={{0,2},{1,3},{2,0},{4,6},{5,7},{6,4},{8,10},{9,11},{10,8},{12,14},{... | collective-permute-start | bytes 294920 | tf_op jit(solution)/shard_map/ppermute | solution.py:275
  104.6 3.2 %collective-permute-start.17 = (bf16[64,768]{1,0:T(8,128)(2,1)S(1)}, bf16[64,768]{1,0:T(8,128)(2,1)S(1)}, u32[]{:S(2)}, u32[]{:S(2)}) collective-permute-start(bf16[64,768]{1,0:T(8,128)(2,1)S(1)} %get-tuple-element.92), channel_id=1, source_target_pairs={{0,1},{1,0},{2,3},{4,5},{5,4},{6,7},{8,9},{9,8},{10,11},{12,13},{1... | collective-permute-start | bytes 294920 | tf_op jit(solution)/shard_map/ppermute | solution.py:275

commit v8 on v7

--- a/solution.py
+++ b/solution.py
@@ -17,7 +17,7 @@
 ANY = pl.BlockSpec(memory_space=pl.ANY)
 VM = pl.BlockSpec(memory_space=pltpu.VMEM)
 SM = pl.BlockSpec(memory_space=pltpu.SMEM)
-PARAMS = pltpu.CompilerParams(vmem_limit_bytes=4 * 1024 * 1024)
+PARAMS = pltpu.CompilerParams(vmem_limit_bytes=6 * 1024 * 1024)
 CUBIC = 0.044715
 SCALE = math.sqrt(2.0 / math.pi)
 
@@ -213,6 +213,38 @@
     )(*args)
 
 
+def turn_kernel(stage, flags, x_ref, w_ref, par_ref, k_ref, g_ref, h_ref, e_ref, *rest):
+    h_out, e_out, dx_ref, gk_ref, y, uh, gp, inv_b, ub, gb, mb = rest
+    forward_kernel(stage, True, False, flags, x_ref, w_ref, par_ref, k_ref, h_ref, y, uh, gp, inv_b, h_out, ub)
+    backward_kernel(stage, True, False, flags, g_ref, w_ref, par_ref, uh, gp, inv_b, e_ref, e_out, dx_ref, gk_ref, gb, mb)
+
+
+def turning_stage(stage, flags, x, weights, par, k, g, h, e):
+    rows, channels = x.shape
+    f32, bf = jnp.float32, jnp.bfloat16
+    wide = (GROUP, rows, channels)
+    args = [flags] + held(x, weights, par, k, g, h, e)
+    full = pltpu.VMEM((rows, channels), f32)
+    return pl.pallas_call(
+        functools.partial(turn_kernel, stage),
+        out_shape=[kept(wide, bf), kept(wide, bf), kept((rows, channels), bf), kept(wide, bf)],
+        in_specs=[SM] + [VM] * (len(args) - 1),
+        out_specs=[VM] * 4,
+        scratch_shapes=[
+            pltpu.VMEM((rows, channels), bf),
+            pltpu.VMEM(wide, f32),
+            pltpu.VMEM(wide, f32),
+            pltpu.VMEM((GROUP, rows, 128), f32),
+            full,
+            full,
+            full,
+        ],
+        input_output_aliases={6: 0, 7: 1},
+        compiler_params=PARAMS,
+        name=f"turn{stage}",
+    )(*args)
+
+
 def encode_bases(base_rows, embed_table):
     one_hot = (base_rows[:, :, None] == jnp.arange(4, dtype=jnp.int32)).astype(jnp.bfloat16)
     one_hot = one_hot.reshape(base_rows.shape[0], -1)
@@ -321,28 +353,26 @@
     h = jnp.zeros(wide, bf)
     e = jnp.zeros(wide, bf)
     states, k = [], None
-    for stage in range(stages):
-        skip, towers = stage == stages - 1, stage == 0
-        outs = forward_stage(stage, skip, towers, flags, x, weights, par, k, h)
+    for stage in range(stages - 1):
+        towers = stage == 0
+        outs = forward_stage(stage, False, towers, flags, x, weights, par, k, h)
         states.append(outs[1:4])
         h = outs[4]
-        if stage < stages - 1:
-            x = shifted(outs[0], stage, stage + 1)
+        x = shifted(outs[0], stage, stage + 1)
         if towers:
             x, tower = lax.optimization_barrier((x, outs[5]))
             k = shifted(tower, 0, stages - 1)
 
-    g = cotangent[0, micro]
-    returned = None
-    for stage in reversed(range(stages)):
-        last, first = stage == stages - 1, stage == 0
-        outs = backward_stage(stage, last, first, flags, g, weights, par, states[stage], returned, e)
+    h, e, dx, skip_grad = turning_stage(stages - 1, flags, x, weights, par, k, cotangent[0, micro], h, e)
+    g = shifted(dx, stages - 1, stages - 2)
+    g, skip_grad = lax.optimization_barrier((g, skip_grad))
+    returned = shifted(skip_grad, stages - 1, 0)
+    for stage in reversed(range(stages - 1)):
+        first = stage == 0
+        outs = backward_stage(stage, False, first, flags, g, weights, par, states[stage], returned, e)
         e = outs[0]
         if stage > 0:
             g = shifted(outs[1], stage, stage - 1)
-        if last:
-            g, skip_grad = lax.optimization_barrier((g, outs[2]))
-            returned = shifted(skip_grad, stages - 1, 0)
         if stage == stages - 2:
             h, e = lax.optimization_barrier((h, e))
             acts = together(h)

time: 175 us -> 175 us (level)
  the two profiles are of different devices: /device:TPU:8 before, /device:TPU:64 now
where the time goes in v8:
time: 175 us; the launch traced here: 174 us
  blocking collectives  62 us (35%)
  waiting for transfers between devices  48.4 us (28%)
  starting transfers between devices  44.8 us (26%)
  Pallas kernels  10.6 us (6%)
  local copies, waits for them, and re-layouts  3.15 us (2%)
  other arithmetic  2.63 us (2%)
    all_to_all x2, blocking collectives, summed_part(): parts = lax.all_to_all(block.reshape(count, -1, block.shape[1]), axis, 0, 0)  34.9 us
    all_to_all x2, blocking collectives, all_parts(): lax.all_to_all(jnp.broadcast_to(block, (count,) + block.shape), axis, 0, 0)  27.1 us
    ppermute x8, waiting for transfers between devices, shifted(): return lax.ppermute(block, PIPE, pairs)  25.6 us
    ppermute x6, starting transfers between devices, swapped(): return lax.ppermute(block, PIPE, pairs)  18.6 us
    ppermute x6, starting transfers between devices, traded(): return lax.ppermute(block[distance], PIPE, pairs)  18.4 us
    ppermute x6, waiting for transfers between devices, swapped(): return lax.ppermute(block, PIPE, pairs)  15.9 us
    ppermute x8, starting transfers between devices, shifted(): return lax.ppermute(block, PIPE, pairs)  7.85 us
    ppermute x6, waiting for transfers between devices, traded(): return lax.ppermute(block[distance], PIPE, pairs)  6.94 us
  transfers between devices with their start and end apart: 20, of which 9 were waited for; matrix products, arithmetic and copies ran while one was open for 2% of the time, Pallas kernels for 2%

profile of v8, /device:TPU:64, one launch (start us, length us, event | category | flops | bytes accessed | tf_op | source)
XLA Modules:
  0.0 173.8 jit_solution(16413908599534461554)
XLA Ops:
  0.0 2.0 %collective-permute-start.1 = (bf16[768,768]{1,0:T(8,128)(2,1)}, bf16[768,768]{1,0:T(8,128)(2,1)S(1)}, u32[]{:S(2)}, u32[]{:S(2)}) collective-permute-start(bf16[768,768]{1,0:T(8,128)(2,1)} %bitcast.44), channel_id=1, source_target_pairs={{0,1},{1,0},{2,3},{3,2},{4,5},{5,4},{6,7},{7,6},{8,9},{9,8},{10,11... | collective-permute-start | bytes 3538952 | tf_op jit(solution)/shard_map/ppermute | solution.py:256
  2.1 6.9 %collective-permute-start = (bf16[768,768]{1,0:T(8,128)(2,1)}, bf16[768,768]{1,0:T(8,128)(2,1)S(1)}, u32[]{:S(2)}, u32[]{:S(2)}) collective-permute-start(bf16[768,768]{1,0:T(8,128)(2,1)} %bitcast.45), channel_id=1, source_target_pairs={{0,2},{1,3},{2,0},{3,1},{4,6},{5,7},{6,4},{7,5},{8,10},{9,11},{10,... | collective-permute-start | bytes 3538952 | tf_op jit(solution)/shard_map/ppermute | solution.py:256
  10.8 2.1 %collective-permute-start.2 = (f32[8,768]{1,0:T(8,128)S(1)}, f32[8,768]{1,0:T(8,128)S(1)}, u32[]{:S(2)}, u32[]{:S(2)}) collective-permute-start(f32[8,768]{1,0:T(8,128)S(1)} %maximum_maximum_fusion), channel_id=1, source_target_pairs={{0,1},{1,0},{2,3},{3,2},{4,5},{5,4},{6,7},{7,6},{8,9},{9,8},{10,11... | collective-permute-start | bytes 73736 | tf_op jit(solution)/shard_map/ppermute | solution.py:256
  12.9 2.2 %collective-permute-start.3 = (f32[8,768]{1,0:T(8,128)S(1)}, f32[8,768]{1,0:T(8,128)S(1)}, u32[]{:S(2)}, u32[]{:S(2)}) collective-permute-start(f32[8,768]{1,0:T(8,128)S(1)} %maximum_maximum_fusion), channel_id=1, source_target_pairs={{0,2},{1,3},{2,0},{3,1},{4,6},{5,7},{6,4},{7,5},{8,10},{9,11},{10,... | collective-permute-start | bytes 73736 | tf_op jit(solution)/shard_map/ppermute | solution.py:256
  15.1 3.3 %collective-permute-start.4 = (f32[8,768]{1,0:T(8,128)S(1)}, f32[8,768]{1,0:T(8,128)S(1)}, u32[]{:S(2)}, u32[]{:S(2)}) collective-permute-start(f32[8,768]{1,0:T(8,128)S(1)} %maximum_maximum_fusion), channel_id=1, source_target_pairs={{0,3},{1,2},{2,1},{3,0},{4,7},{5,6},{6,5},{7,4},{8,11},{9,10},{10,... | collective-permute-start | bytes 73736 | tf_op jit(solution)/shard_map/ppermute | solution.py:256
  20.4 1.3 copy-done.1
  22.7 13.8 %collective-permute-done.3 = f32[8,768]{1,0:T(8,128)S(1)} collective-permute-done((f32[8,768]{1,0:T(8,128)S(1)}, f32[8,768]{1,0:T(8,128)S(1)}, u32[]{:S(2)}, u32[]{:S(2)}) %collective-permute-start.3) | collective-permute-done | bytes 24608 | tf_op jit(solution)/shard_map/ppermute | solution.py:256
  36.7 2.0 %collective-permute-start.5 = (bf16[768,768]{1,0:T(8,128)(2,1)S(1)}, bf16[768,768]{1,0:T(8,128)(2,1)S(1)}, u32[]{:S(2)}, u32[]{:S(2)}) collective-permute-start(bf16[768,768]{1,0:T(8,128)(2,1)S(1)} %collective-permute-done.rest_0_), channel_id=1, source_target_pairs={{0,1},{1,0},{2,3},{3,2},{4,5},{5,4},{6,7},{7,6},{8,9},{9,8},{10,11... | collective-permute-start | bytes 3538952 | tf_op jit(solution)/shard_map/ppermute | solution.py:256
  39.5 1.9 %collective-permute-done.5.rest_0_ = bf16[768,768]{1,0:T(8,128)(2,1)S(1)} collective-permute-done((bf16[768,768]{1,0:T(8,128)(2,1)S(1)}, bf16[768,768]{1,0:T(8,128)(2,1)S(1)}, u32[]{:S(2)}, u32[]{:S(2)}) %collective-permute-start.5) | collective-permute-done | bytes 1179680 | tf_op jit(solution)/shard_map/ppermute | solution.py:256
  42.3 2.4 %ahead0.1 = (bf16[64,768]{1,0:T(8,128)(2,1)S(1)}, f32[4,64,768]{2,1,0:T(8,128)S(1)}, f32[4,64,768]{2,1,0:T(8,128)S(1)}, f32[4,64,128]{2,1,0:T(8,128)S(1)}, bf16[...) custom-call(s32[2]{0:T(128)S(1)} %pad_add_fusion.flags, ...), custom_call_target="tpu_custom_call", output_to_operand_aliasing={{4}: (4, {})} | custom-call | tf_op jit(solution)/shard_map/ahead0/pallas_call | solution.py:124
  44.7 1.3 collective-permute-start.6
  46.0 4.3 %collective-permute-done.6.x_ref = bf16[64,768]{1,0:T(8,128)(2,1)S(1)} collective-permute-done((bf16[64,768]{1,0:T(8,128)(2,1)S(1)}, bf16[64,768]{1,0:T(8,128)(2,1)S(1)}, u32[]{:S(2)}, u32[]{:S(2)}) %collective-permute-start.6) | collective-permute-done | bytes 98336 | tf_op jit(solution)/shard_map/ppermute | solution.py:302
  50.2 1.3 collective-permute-start.9
  54.2 2.7 %collective-permute-done.9.k_ref = bf16[4,64,768]{2,1,0:T(8,128)(2,1)S(1)} collective-permute-done((bf16[4,64,768]{2,1,0:T(8,128)(2,1)S(1)}, bf16[4,64,768]{2,1,0:T(8,128)(2,1)S(1)}, u32[]{:S(2)}, u32[]{:S(2)}) %collective-permute-start.9) | collective-permute-done | bytes 393248 | tf_op jit(solution)/shard_map/ppermute | solution.py:302
  59.5 1.3 collective-permute-start.16
  60.8 1.3 collective-permute-start.11
  62.2 9.9 %collective-permute-start.12 = (bf16[64,768]{1,0:T(8,128)(2,1)S(1)}, bf16[64,768]{1,0:T(8,128)(2,1)S(1)}, u32[]{:S(2)}, u32[]{:S(2)}) collective-permute-start(bf16[64,768]{1,0:T(8,128)(2,1)S(1)} %get-tuple-element.89), channel_id=1, source_target_pairs={{0,2},{1,3},{2,0},{4,6},{5,7},{6,4},{8,10},{9,11},{10,8},{12,14},{... | collective-permute-start | bytes 294920 | tf_op jit(solution)/shard_map/ppermute | solution.py:307
  72.1 1.9 %collective-permute-start.13 = (bf16[64,768]{1,0:T(8,128)(2,1)S(1)}, bf16[64,768]{1,0:T(8,128)(2,1)S(1)}, u32[]{:S(2)}, u32[]{:S(2)}) collective-permute-start(bf16[64,768]{1,0:T(8,128)(2,1)S(1)} %get-tuple-element.88), channel_id=1, source_target_pairs={{0,3},{1,2},{2,1},{4,7},{5,6},{6,5},{8,11},{9,10},{10,9},{12,15},{... | collective-permute-start | bytes 294920 | tf_op jit(solution)/shard_map/ppermute | solution.py:307
  74.7 1.3 collective-permute-start.15
  76.0 2.1 %collective-permute-done.13 = bf16[64,768]{1,0:T(8,128)(2,1)S(1)} collective-permute-done((bf16[64,768]{1,0:T(8,128)(2,1)S(1)}, bf16[64,768]{1,0:T(8,128)(2,1)S(1)}, u32[]{:S(2)}, u32[]{:S(2)}) %collective-permute-start.13) | collective-permute-done | bytes 98336 | tf_op jit(solution)/shard_map/ppermute | solution.py:307
  78.1 18.6 %collective-permute-done.15.g_ref = bf16[64,768]{1,0:T(8,128)(2,1)S(1)} collective-permute-done((bf16[64,768]{1,0:T(8,128)(2,1)S(1)}, bf16[64,768]{1,0:T(8,128)(2,1)S(1)}, u32[]{:S(2)}, u32[]{:S(2)}) %collective-permute-start.15) | collective-permute-done | bytes 98336 | tf_op jit(solution)/shard_map/ppermute | solution.py:302
  96.7 2.5 %behind0.1 = bf16[4,64,768]{2,1,0:T(8,128)(2,1)S(1)} custom-call(s32[2]{0:T(128)S(1)} %pad_add_fusion.flags, bf16[64,768]{1,0:T(8,128)(2,1)S(1)} %collective-permute-done.15.g_ref, bf16[4,768,768]{2,1,0:T(8,128)(2,1)S(1)} %packed.5.w_ref, f32[4,8,768]{2,1,0:T(8,128)S(1)} %bitcast_dynamic-update-slice_fusion.par_ref, ...), custom_call_target="tpu_custom_call", output_to_operand_aliasing={{}: (8, {})} | custom-call | tf_op jit(solution)/shard_map/behind0/pallas_call | solution.py:204
  99.2 1.3 collective-permute-start.17
  100.5 2.0 %collective-permute-start.18 = (bf16[64,768]{1,0:T(8,128)(2,1)S(1)}, bf16[64,768]{1,0:T(8,128)(2,1)S(1)}, u32[]{:S(2)}, u32[]{:S(2)}) collective-permute-start(bf16[64,768]{1,0:T(8,128)(2,1)S(1)} %get-tuple-element.85), channel_id=1, source_target_pairs={{0,2},{1,3},{2,0},{4,6},{5,7},{6,4},{8,10},{9,11},{10,8},{12,14},{... | collective-permute-start | bytes 294920 | tf_op jit(solution)/shard_map/ppermute | solution.py:307
  102.6 1.9 %collective-permute-start.19 = (bf16[64,768]{1,0:T(8,128)(2,1)S(1)}, bf16[64,768]{1,0:T(8,128)(2,1)S(1)}, u32[]{:S(2)}, u32[]{:S(2)}) collective-permute-start(bf16[64,768]{1,0:T(8,128)(2,1)S(1)} %get-tuple-element.84), channel_id=1, source_target_pairs={{0,3},{1,2},{2,1},{4,7},{5,6},{6,5},{8,11},{9,10},{10,9},{12,15},{... | collective-permute-start | bytes 294920 | tf_op jit(solution)/shard_map/ppermute | solution.py:307
  104.5 2.5 %collective-permute-done.18 = bf16[64,768]{1,0:T(8,128)(2,1)S(1)} collective-permute-done((bf16[64,768]{1,0:T(8,128)(2,1)S(1)}, bf16[64,768]{1,0:T(8,128)(2,1)S(1)}, u32[]{:S(2)}, u32[]{:S(2)}) %collective-permute-start.18) | collective-permute-done | bytes 98336 | tf_op jit(solution)/shard_map/ppermute | solution.py:307
  107.0 2.4 %collective-permute-done.19 = bf16[64,768]{1,0:T(8,128)(2,1)S(1)} collective-permute-done((bf16[64,768]{1,0:T(8,128)(2,1)S(1)}, bf16[64,768]{1,0:T(8,128)(2,1)S(1)}, u32[]{:S(2)}, u32[]{:S(2)}) %collective-permute-start.19) | collective-permute-done | bytes 98336 | tf_op jit(solution)/shard_map/ppermute | solution.py:307
  109.9 20.4 %all_to_all.23 = bf16[8,96,768]{2,1,0:T(8,128)(2,1)S(1)} all-to-all(bf16[8,96,768]{2,1,0:T(8,128)(2,1)S(1)} %bitcast.48), channel_id=1, replica_groups=mesh['yh'=4,'yl'=2,'x'=4,'g'=4,'q'=4] {'yl','x'}, dimensions={0} | all-to-all | bytes 2359296 | tf_op jit(solution)/shard_map/all_to_all | solution.py:316
  130.5 14.5 %all_to_all.20 = bf16[4,24,768]{2,1,0:T(8,128)(2,1)S(1)} all-to-all(bf16[4,24,768]{2,1,0:T(8,128)(2,1)S(1)} %bitcast.49), channel_id=1, replica_groups=mesh['yh'=4,'yl'=2,'x'=4,'g'=4,'q'=4] {'yh'}, dimensions={0} | all-to-all | bytes 294912 | tf_op jit(solution)/shard_map/all_to_all | solution.py:316
  145.0 10.9 %all_to_all.21 = bf16[4,24,768]{2,1,0:T(8,128)(2,1)S(1)} all-to-all(bf16[4,24,768]{2,1,0:T(8,128)(2,1)S(1)} %broadcast_in_dim.32), channel_id=1, replica_groups=mesh['yh'=4,'yl'=2,'x'=4,'g'=4,'q'=4] {'yh'}, dimensions={0} | all-to-all | bytes 294912 | tf_op jit(solution)/shard_map/all_to_all | solution.py:322
  156.0 16.2 %all_to_all.22 = bf16[8,96,768]{2,1,0:T(8,128)(2,1)S(1)} all-to-all(bf16[8,96,768]{2,1,0:T(8,128)(2,1)S(1)} %broadcast_in_dim.33), channel_id=1, replica_groups=mesh['yh'=4,'yl'=2,'x'=4,'g'=4,'q'=4] {'yl','x'}, dimensions={0} | all-to-all | bytes 2359296 | tf_op jit(solution)/shard_map/all_to_all | solution.py:322
  172.2 1.6 bitcast_convert_fusion
  (54 shorter events, 13.2 us)
Async XLA Ops:
  0.0 54.1 %copy-start = (bf16[1,3,64,768]{3,2,1,0:T(8,128)(2,1)S(1)}, bf16[1,3,64,768]{3,2,1,0:T(8,128)(2,1)}, u32[]{:S(2)}) copy-start(bf16[1,3,64,768]{3,2,1,0:T(8,128)(2,1)} %param.11) | copy-start | bytes 884740
  0.0 10.8 %collective-permute-start.1 = (bf16[768,768]{1,0:T(8,128)(2,1)}, bf16[768,768]{1,0:T(8,128)(2,1)S(1)}, u32[]{:S(2)}, u32[]{:S(2)}) collective-permute-start(bf16[768,768]{1,0:T(8,128)(2,1)} %bitcast.44), channel_id=1, source_target_pairs={{0,1},{1,0},{2,3},{3,2},{4,5},{5,4},{6,7},{7,6},{8,9},{9,8},{10,11... | collective-permute-start | bytes 3538952 | tf_op jit(solution)/shard_map/ppermute | solution.py:256
  2.1 34.6 %collective-permute-start = (bf16[768,768]{1,0:T(8,128)(2,1)}, bf16[768,768]{1,0:T(8,128)(2,1)S(1)}, u32[]{:S(2)}, u32[]{:S(2)}) collective-permute-start(bf16[768,768]{1,0:T(8,128)(2,1)} %bitcast.45), channel_id=1, source_target_pairs={{0,2},{1,3},{2,0},{3,1},{4,6},{5,7},{6,4},{7,5},{8,10},{9,11},{10,... | collective-permute-start | bytes 3538952 | tf_op jit(solution)/shard_map/ppermute | solution.py:256
  10.8 11.9 %collective-permute-start.2 = (f32[8,768]{1,0:T(8,128)S(1)}, f32[8,768]{1,0:T(8,128)S(1)}, u32[]{:S(2)}, u32[]{:S(2)}) collective-permute-start(f32[8,768]{1,0:T(8,128)S(1)} %maximum_maximum_fusion), channel_id=1, source_target_pairs={{0,1},{1,0},{2,3},{3,2},{4,5},{5,4},{6,7},{7,6},{8,9},{9,8},{10,11... | collective-permute-start | bytes 73736 | tf_op jit(solution)/shard_map/ppermute | solution.py:256
  12.9 23.7 %collective-permute-start.3 = (f32[8,768]{1,0:T(8,128)S(1)}, f32[8,768]{1,0:T(8,128)S(1)}, u32[]{:S(2)}, u32[]{:S(2)}) collective-permute-start(f32[8,768]{1,0:T(8,128)S(1)} %maximum_maximum_fusion), channel_id=1, source_target_pairs={{0,2},{1,3},{2,0},{3,1},{4,6},{5,7},{6,4},{7,5},{8,10},{9,11},{10,... | collective-permute-start | bytes 73736 | tf_op jit(solution)/shard_map/ppermute | solution.py:256
  15.1 21.6 %collective-permute-start.4 = (f32[8,768]{1,0:T(8,128)S(1)}, f32[8,768]{1,0:T(8,128)S(1)}, u32[]{:S(2)}, u32[]{:S(2)}) collective-permute-start(f32[8,768]{1,0:T(8,128)S(1)} %maximum_maximum_fusion), channel_id=1, source_target_pairs={{0,3},{1,2},{2,1},{3,0},{4,7},{5,6},{6,5},{7,4},{8,11},{9,10},{10,... | collective-permute-start | bytes 73736 | tf_op jit(solution)/shard_map/ppermute | solution.py:256
  20.3 1.3 copy-start.1
  36.7 4.7 %collective-permute-start.5 = (bf16[768,768]{1,0:T(8,128)(2,1)S(1)}, bf16[768,768]{1,0:T(8,128)(2,1)S(1)}, u32[]{:S(2)}, u32[]{:S(2)}) collective-permute-start(bf16[768,768]{1,0:T(8,128)(2,1)S(1)} %collective-permute-done.rest_0_), channel_id=1, source_target_pairs={{0,1},{1,0},{2,3},{3,2},{4,5},{5,4},{6,7},{7,6},{8,9},{9,8},{10,11... | collective-permute-start | bytes 3538952 | tf_op jit(solution)/shard_map/ppermute | solution.py:256
  44.7 5.6 %collective-permute-start.6 = (bf16[64,768]{1,0:T(8,128)(2,1)S(1)}, bf16[64,768]{1,0:T(8,128)(2,1)S(1)}, u32[]{:S(2)}, u32[]{:S(2)}) collective-permute-start(bf16[64,768]{1,0:T(8,128)(2,1)S(1)} %get-tuple-element.51), channel_id=1, source_target_pairs={{0,4},{1,5},{2,6},{16,20},{17,21},{18,22},{32,36},{33,37},{34,38},... | collective-permute-start | bytes 294920 | tf_op jit(solution)/shard_map/ppermute | solution.py:302
  50.2 6.6 %collective-permute-start.9 = (bf16[4,64,768]{2,1,0:T(8,128)(2,1)S(1)}, bf16[4,64,768]{2,1,0:T(8,128)(2,1)S(1)}, u32[]{:S(2)}, u32[]{:S(2)}) collective-permute-start(bf16[4,64,768]{2,1,0:T(8,128)(2,1)S(1)} %get-tuple-element.58), channel_id=1, source_target_pairs={{0,12},{1,13},{2,14},{16,28},{17,29},{18,30},{32,44},{33,45},{34,4... | collective-permute-start | bytes 1179656 | tf_op jit(solution)/shard_map/ppermute | solution.py:302
  52.2 0.7 collective-permute-start.7
  53.4 0.7 collective-permute-start.8
  57.5 0.7 collective-permute-start.10
  58.8 15.2 %collective-permute-start.14 = (bf16[64,768]{1,0:T(8,128)(2,1)S(1)}, bf16[64,768]{1,0:T(8,128)(2,1)S(1)}, u32[]{:S(2)}, u32[]{:S(2)}) collective-permute-start(bf16[64,768]{1,0:T(8,128)(2,1)S(1)} %get-tuple-element.70), channel_id=1, source_target_pairs={{8,4},{9,5},{10,6},{24,20},{25,21},{26,22},{40,36},{41,37},{42,38}... | collective-permute-start | bytes 294920 | tf_op jit(solution)/shard_map/ppermute | solution.py:302
  59.5 37.2 %collective-permute-start.16 = (bf16[4,64,768]{2,1,0:T(8,128)(2,1)S(1)}, bf16[4,64,768]{2,1,0:T(8,128)(2,1)S(1)}, u32[]{:S(2)}, u32[]{:S(2)}) collective-permute-start(bf16[4,64,768]{2,1,0:T(8,128)(2,1)S(1)} %get-tuple-element.81), channel_id=1, source_target_pairs={{12,0},{13,1},{14,2},{28,16},{29,17},{30,18},{44,32},{45,33},{46,3... | collective-permute-start | bytes 1179656 | tf_op jit(solution)/shard_map/ppermute | solution.py:302
  60.8 15.1 %collective-permute-start.11 = (bf16[64,768]{1,0:T(8,128)(2,1)S(1)}, bf16[64,768]{1,0:T(8,128)(2,1)S(1)}, u32[]{:S(2)}, u32[]{:S(2)}) collective-permute-start(bf16[64,768]{1,0:T(8,128)(2,1)S(1)} %get-tuple-element.90), channel_id=1, source_target_pairs={{0,1},{1,0},{2,3},{4,5},{5,4},{6,7},{8,9},{9,8},{10,11},{12,13},{1... | collective-permute-start | bytes 294920 | tf_op jit(solution)/shard_map/ppermute | solution.py:307
  62.2 13.8 %collective-permute-start.12 = (bf16[64,768]{1,0:T(8,128)(2,1)S(1)}, bf16[64,768]{1,0:T(8,128)(2,1)S(1)}, u32[]{:S(2)}, u32[]{:S(2)}) collective-permute-start(bf16[64,768]{1,0:T(8,128)(2,1)S(1)} %get-tuple-element.89), channel_id=1, source_target_pairs={{0,2},{1,3},{2,0},{4,6},{5,7},{6,4},{8,10},{9,11},{10,8},{12,14},{... | collective-permute-start | bytes 294920 | tf_op jit(solution)/shard_map/ppermute | solution.py:307
  72.1 5.9 %collective-permute-start.13 = (bf16[64,768]{1,0:T(8,128)(2,1)S(1)}, bf16[64,768]{1,0:T(8,128)(2,1)S(1)}, u32[]{:S(2)}, u32[]{:S(2)}) collective-permute-start(bf16[64,768]{1,0:T(8,128)(2,1)S(1)} %get-tuple-element.88), channel_id=1, source_target_pairs={{0,3},{1,2},{2,1},{4,7},{5,6},{6,5},{8,11},{9,10},{10,9},{12,15},{... | collective-permute-start | bytes 294920 | tf_op jit(solution)/shard_map/ppermute | solution.py:307
  74.7 22.0 %collective-permute-start.15 = (bf16[64,768]{1,0:T(8,128)(2,1)S(1)}, bf16[64,768]{1,0:T(8,128)(2,1)S(1)}, u32[]{:S(2)}, u32[]{:S(2)}) collective-permute-start(bf16[64,768]{1,0:T(8,128)(2,1)S(1)} %get-tuple-element.77), channel_id=1, source_target_pairs={{4,0},{5,1},{6,2},{20,16},{21,17},{22,18},{36,32},{37,33},{38,34},... | collective-permute-start | bytes 294920 | tf_op jit(solution)/shard_map/ppermute | solution.py:302
  99.2 5.3 %collective-permute-start.17 = (bf16[64,768]{1,0:T(8,128)(2,1)S(1)}, bf16[64,768]{1,0:T(8,128)(2,1)S(1)}, u32[]{:S(2)}, u32[]{:S(2)}) collective-permute-start(bf16[64,768]{1,0:T(8,128)(2,1)S(1)} %get-tuple-element.86), channel_id=1, source_target_pairs={{0,1},{1,0},{2,3},{4,5},{5,4},{6,7},{8,9},{9,8},{10,11},{12,13},{1... | collective-permute-start | bytes 294920 | tf_op jit(solution)/shard_map/ppermute | solution.py:307
  100.5 6.5 %collective-permute-start.18 = (bf16[64,768]{1,0:T(8,128)(2,1)S(1)}, bf16[64,768]{1,0:T(8,128)(2,1)S(1)}, u32[]{:S(2)}, u32[]{:S(2)}) collective-permute-start(bf16[64,768]{1,0:T(8,128)(2,1)S(1)} %get-tuple-element.85), channel_id=1, source_target_pairs={{0,2},{1,3},{2,0},{4,6},{5,7},{6,4},{8,10},{9,11},{10,8},{12,14},{... | collective-permute-start | bytes 294920 | tf_op jit(solution)/shard_map/ppermute | solution.py:307
  102.6 6.8 %collective-permute-start.19 = (bf16[64,768]{1,0:T(8,128)(2,1)S(1)}, bf16[64,768]{1,0:T(8,128)(2,1)S(1)}, u32[]{:S(2)}, u32[]{:S(2)}) collective-permute-start(bf16[64,768]{1,0:T(8,128)(2,1)S(1)} %get-tuple-element.84), channel_id=1, source_target_pairs={{0,3},{1,2},{2,1},{4,7},{5,6},{6,5},{8,11},{9,10},{10,9},{12,15},{... | collective-permute-start | bytes 294920 | tf_op jit(solution)/shard_map/ppermute | solution.py:307

commit v9 on v7

--- a/solution.py
+++ b/solution.py
@@ -154,12 +154,12 @@
         dx = g_ref[...]
         for j in reversed(range(GROUP)):
             d = jnp.bitwise_xor(member, j)
-            for cs in chunks_of(channels):
-                g = dx[:, cs].astype(jnp.float32)
-                if first:
-                    g = g + k_ref[j, :, cs].astype(jnp.float32)
-                gb[:, cs] = g
-            e = gb[...].astype(jnp.bfloat16)
+            if first:
+                gb[...] = dx.astype(jnp.float32) + k_ref[j].astype(jnp.float32)
+                e = gb[...].astype(jnp.bfloat16)
+            else:
+                gb[...] = dx.astype(jnp.float32)
+                e = dx
             eb[d] = e
             if first and j == 0:
                 continue

time: 175 us -> 175 us (level)
  no operation moved by 1% of the time
where the time goes in v9:
time: 175 us; the launch traced here: 174 us
  blocking collectives  63.7 us (36%)
  waiting for transfers between devices  47.5 us (27%)
  starting transfers between devices  42.9 us (25%)
  Pallas kernels  11.8 us (7%)
  local copies, waits for them, and re-layouts  3.15 us (2%)
  other arithmetic  2.63 us (2%)
    all_to_all x2, blocking collectives, summed_part(): parts = lax.all_to_all(block.reshape(count, -1, block.shape[1]), axis, 0, 0)  36.3 us
    ppermute x8, waiting for transfers between devices, shifted(): return lax.ppermute(block, PIPE, pairs)  30.4 us
    all_to_all x2, blocking collectives, all_parts(): lax.all_to_all(jnp.broadcast_to(block, (count,) + block.shape), axis, 0, 0)  27.4 us
    ppermute x6, starting transfers between devices, swapped(): return lax.ppermute(block, PIPE, pairs)  15.9 us
    ppermute x6, waiting for transfers between devices, swapped(): return lax.ppermute(block, PIPE, pairs)  15.9 us
    ppermute x6, starting transfers between devices, traded(): return lax.ppermute(block[distance], PIPE, pairs)  14.9 us
    ppermute x8, starting transfers between devices, shifted(): return lax.ppermute(block, PIPE, pairs)  12.1 us
    pallas_call x4, Pallas kernels, forward_stage(): pl.pallas_call(functools.partial(forward_kernel, stage, skip, towers), ou...  4.85 us
  transfers between devices with their start and end apart: 20, of which 8 were waited for; matrix products, arithmetic and copies ran while one was open for 2% of the time, Pallas kernels for 2%

profile of v9, /device:TPU:8, one launch (start us, length us, event | category | flops | bytes accessed | tf_op | source)
XLA Modules:
  0.0 173.9 jit_solution(4368088625132344524)
XLA Ops:
  0.0 2.0 %collective-permute-start.1 = (bf16[768,768]{1,0:T(8,128)(2,1)}, bf16[768,768]{1,0:T(8,128)(2,1)S(1)}, u32[]{:S(2)}, u32[]{:S(2)}) collective-permute-start(bf16[768,768]{1,0:T(8,128)(2,1)} %bitcast.44), channel_id=1, source_target_pairs={{0,1},{1,0},{2,3},{3,2},{4,5},{5,4},{6,7},{7,6},{8,9},{9,8},{10,11... | collective-permute-start | bytes 3538952 | tf_op jit(solution)/shard_map/ppermute | solution.py:224
  2.1 4.3 %collective-permute-start = (bf16[768,768]{1,0:T(8,128)(2,1)}, bf16[768,768]{1,0:T(8,128)(2,1)S(1)}, u32[]{:S(2)}, u32[]{:S(2)}) collective-permute-start(bf16[768,768]{1,0:T(8,128)(2,1)} %bitcast.45), channel_id=1, source_target_pairs={{0,2},{1,3},{2,0},{3,1},{4,6},{5,7},{6,4},{7,5},{8,10},{9,11},{10,... | collective-permute-start | bytes 3538952 | tf_op jit(solution)/shard_map/ppermute | solution.py:224
  8.1 2.1 %collective-permute-start.2 = (f32[8,768]{1,0:T(8,128)S(1)}, f32[8,768]{1,0:T(8,128)S(1)}, u32[]{:S(2)}, u32[]{:S(2)}) collective-permute-start(f32[8,768]{1,0:T(8,128)S(1)} %maximum_maximum_fusion), channel_id=1, source_target_pairs={{0,1},{1,0},{2,3},{3,2},{4,5},{5,4},{6,7},{7,6},{8,9},{9,8},{10,11... | collective-permute-start | bytes 73736 | tf_op jit(solution)/shard_map/ppermute | solution.py:224
  10.2 2.2 %collective-permute-start.3 = (f32[8,768]{1,0:T(8,128)S(1)}, f32[8,768]{1,0:T(8,128)S(1)}, u32[]{:S(2)}, u32[]{:S(2)}) collective-permute-start(f32[8,768]{1,0:T(8,128)S(1)} %maximum_maximum_fusion), channel_id=1, source_target_pairs={{0,2},{1,3},{2,0},{3,1},{4,6},{5,7},{6,4},{7,5},{8,10},{9,11},{10,... | collective-permute-start | bytes 73736 | tf_op jit(solution)/shard_map/ppermute | solution.py:224
  12.4 3.3 %collective-permute-start.4 = (f32[8,768]{1,0:T(8,128)S(1)}, f32[8,768]{1,0:T(8,128)S(1)}, u32[]{:S(2)}, u32[]{:S(2)}) collective-permute-start(f32[8,768]{1,0:T(8,128)S(1)} %maximum_maximum_fusion), channel_id=1, source_target_pairs={{0,3},{1,2},{2,1},{3,0},{4,7},{5,6},{6,5},{7,4},{8,11},{9,10},{10,... | collective-permute-start | bytes 73736 | tf_op jit(solution)/shard_map/ppermute | solution.py:224
  16.4 1.2 convolution_convert_fusion.1.x_ref
  17.7 1.3 copy-done.1
  19.0 1.1 packed.3.rest_1_
  20.0 13.8 %collective-permute-done.3 = f32[8,768]{1,0:T(8,128)S(1)} collective-permute-done((f32[8,768]{1,0:T(8,128)S(1)}, f32[8,768]{1,0:T(8,128)S(1)}, u32[]{:S(2)}, u32[]{:S(2)}) %collective-permute-start.3) | collective-permute-done | bytes 24608 | tf_op jit(solution)/shard_map/ppermute | solution.py:224
  34.0 2.0 %collective-permute-start.5 = (bf16[768,768]{1,0:T(8,128)(2,1)S(1)}, bf16[768,768]{1,0:T(8,128)(2,1)S(1)}, u32[]{:S(2)}, u32[]{:S(2)}) collective-permute-start(bf16[768,768]{1,0:T(8,128)(2,1)S(1)} %collective-permute-done.rest_0_), channel_id=1, source_target_pairs={{0,1},{1,0},{2,3},{3,2},{4,5},{5,4},{6,7},{7,6},{8,9},{9,8},{10,11... | collective-permute-start | bytes 3538952 | tf_op jit(solution)/shard_map/ppermute | solution.py:224
  36.9 1.9 %collective-permute-done.5.rest_0_ = bf16[768,768]{1,0:T(8,128)(2,1)S(1)} collective-permute-done((bf16[768,768]{1,0:T(8,128)(2,1)S(1)}, bf16[768,768]{1,0:T(8,128)(2,1)S(1)}, u32[]{:S(2)}, u32[]{:S(2)}) %collective-permute-start.5) | collective-permute-done | bytes 1179680 | tf_op jit(solution)/shard_map/ppermute | solution.py:224
  39.6 2.4 %ahead0.1 = (bf16[64,768]{1,0:T(8,128)(2,1)S(1)}, f32[4,64,768]{2,1,0:T(8,128)S(1)}, f32[4,64,768]{2,1,0:T(8,128)S(1)}, f32[4,64,128]{2,1,0:T(8,128)S(1)}, bf16[...) custom-call(s32[2]{0:T(128)S(1)} %pad_add_fusion.flags, ...), custom_call_target="tpu_custom_call", output_to_operand_aliasing={{4}: (4, {})} | custom-call | tf_op jit(solution)/shard_map/ahead0/pallas_call | solution.py:124
  42.0 4.3 %collective-permute-start.6 = (bf16[64,768]{1,0:T(8,128)(2,1)S(1)}, bf16[64,768]{1,0:T(8,128)(2,1)S(1)}, u32[]{:S(2)}, u32[]{:S(2)}) collective-permute-start(bf16[64,768]{1,0:T(8,128)(2,1)S(1)} %get-tuple-element.54), channel_id=1, source_target_pairs={{0,4},{1,5},{2,6},{16,20},{17,21},{18,22},{32,36},{33,37},{34,38},... | collective-permute-start | bytes 294920 | tf_op jit(solution)/shard_map/ppermute | solution.py:270
  46.3 2.3 %collective-permute-done.6.x_ref = bf16[64,768]{1,0:T(8,128)(2,1)S(1)} collective-permute-done((bf16[64,768]{1,0:T(8,128)(2,1)S(1)}, bf16[64,768]{1,0:T(8,128)(2,1)S(1)}, u32[]{:S(2)}, u32[]{:S(2)}) %collective-permute-start.6) | collective-permute-done | bytes 98336 | tf_op jit(solution)/shard_map/ppermute | solution.py:270
  48.6 2.5 %collective-permute-start.9 = (bf16[4,64,768]{2,1,0:T(8,128)(2,1)S(1)}, bf16[4,64,768]{2,1,0:T(8,128)(2,1)S(1)}, u32[]{:S(2)}, u32[]{:S(2)}) collective-permute-start(bf16[4,64,768]{2,1,0:T(8,128)(2,1)S(1)} %get-tuple-element.61), channel_id=1, source_target_pairs={{0,12},{1,13},{2,14},{16,28},{17,29},{18,30},{32,44},{33,45},{34,4... | collective-permute-start | bytes 1179656 | tf_op jit(solution)/shard_map/ppermute | solution.py:270
  53.8 10.2 %collective-permute-done.9.rest_0_ = bf16[4,64,768]{2,1,0:T(8,128)(2,1)S(1)} collective-permute-done((bf16[4,64,768]{2,1,0:T(8,128)(2,1)S(1)}, bf16[4,64,768]{2,1,0:T(8,128)(2,1)S(1)}, u32[]{:S(2)}, u32[]{:S(2)}) %collective-permute-start.9) | collective-permute-done | bytes 393248 | tf_op jit(solution)/shard_map/ppermute | solution.py:270
  64.0 1.2 ahead3.1
  67.9 1.3 collective-permute-start.16
  69.2 1.3 collective-permute-start.13
  70.5 3.5 %collective-permute-start.12 = (bf16[64,768]{1,0:T(8,128)(2,1)S(1)}, bf16[64,768]{1,0:T(8,128)(2,1)S(1)}, u32[]{:S(2)}, u32[]{:S(2)}) collective-permute-start(bf16[64,768]{1,0:T(8,128)(2,1)S(1)} %get-tuple-element.95), channel_id=1, source_target_pairs={{0,2},{1,3},{2,0},{4,6},{5,7},{6,4},{8,10},{9,11},{10,8},{12,14},{... | collective-permute-start | bytes 294920 | tf_op jit(solution)/shard_map/ppermute | solution.py:275
  74.0 1.9 %collective-permute-start.11 = (bf16[64,768]{1,0:T(8,128)(2,1)S(1)}, bf16[64,768]{1,0:T(8,128)(2,1)S(1)}, u32[]{:S(2)}, u32[]{:S(2)}) collective-permute-start(bf16[64,768]{1,0:T(8,128)(2,1)S(1)} %get-tuple-element.96), channel_id=1, source_target_pairs={{0,1},{1,0},{2,3},{4,5},{5,4},{6,7},{8,9},{9,8},{10,11},{12,13},{1... | collective-permute-start | bytes 294920 | tf_op jit(solution)/shard_map/ppermute | solution.py:275
  76.6 1.3 collective-permute-start.15
  77.9 17.8 %collective-permute-done.15.g_ref = bf16[64,768]{1,0:T(8,128)(2,1)S(1)} collective-permute-done((bf16[64,768]{1,0:T(8,128)(2,1)S(1)}, bf16[64,768]{1,0:T(8,128)(2,1)S(1)}, u32[]{:S(2)}, u32[]{:S(2)}) %collective-permute-start.15) | collective-permute-done | bytes 98336 | tf_op jit(solution)/shard_map/ppermute | solution.py:270
  95.7 2.5 %behind0.1 = bf16[4,64,768]{2,1,0:T(8,128)(2,1)S(1)} custom-call(s32[2]{0:T(128)S(1)} %pad_add_fusion.flags, bf16[64,768]{1,0:T(8,128)(2,1)S(1)} %collective-permute-done.15.g_ref, bf16[4,768,768]{2,1,0:T(8,128)(2,1)S(1)} %packed.5.w_ref, f32[4,8,768]{2,1,0:T(8,128)S(1)} %bitcast_dynamic-update-slice_fusion.par_ref, ...), custom_call_target="tpu_custom_call", output_to_operand_aliasing={{}: (8, {})} | custom-call | tf_op jit(solution)/shard_map/behind0/pallas_call | solution.py:204
  98.3 1.3 collective-permute-start.19
  99.6 5.1 %collective-permute-start.18 = (bf16[64,768]{1,0:T(8,128)(2,1)S(1)}, bf16[64,768]{1,0:T(8,128)(2,1)S(1)}, u32[]{:S(2)}, u32[]{:S(2)}) collective-permute-start(bf16[64,768]{1,0:T(8,128)(2,1)S(1)} %get-tuple-element.91), channel_id=1, source_target_pairs={{0,2},{1,3},{2,0},{4,6},{5,7},{6,4},{8,10},{9,11},{10,8},{12,14},{... | collective-permute-start | bytes 294920 | tf_op jit(solution)/shard_map/ppermute | solution.py:275
  104.6 1.9 %collective-permute-start.17 = (bf16[64,768]{1,0:T(8,128)(2,1)S(1)}, bf16[64,768]{1,0:T(8,128)(2,1)S(1)}, u32[]{:S(2)}, u32[]{:S(2)}) collective-permute-start(bf16[64,768]{1,0:T(8,128)(2,1)S(1)} %get-tuple-element.92), channel_id=1, source_target_pairs={{0,1},{1,0},{2,3},{4,5},{5,4},{6,7},{8,9},{9,8},{10,11},{12,13},{1... | collective-permute-start | bytes 294920 | tf_op jit(solution)/shard_map/ppermute | solution.py:275
  108.3 21.6 %all_to_all.23 = bf16[8,96,768]{2,1,0:T(8,128)(2,1)S(1)} all-to-all(bf16[8,96,768]{2,1,0:T(8,128)(2,1)S(1)} %bitcast.48), channel_id=1, replica_groups=mesh['yh'=4,'yl'=2,'x'=4,'g'=4,'q'=4] {'yl','x'}, dimensions={0} | all-to-all | bytes 2359296 | tf_op jit(solution)/shard_map/all_to_all | solution.py:284
  130.1 14.7 %all_to_all.20 = bf16[4,24,768]{2,1,0:T(8,128)(2,1)S(1)} all-to-all(bf16[4,24,768]{2,1,0:T(8,128)(2,1)S(1)} %bitcast.49), channel_id=1, replica_groups=mesh['yh'=4,'yl'=2,'x'=4,'g'=4,'q'=4] {'yh'}, dimensions={0} | all-to-all | bytes 294912 | tf_op jit(solution)/shard_map/all_to_all | solution.py:284
  144.9 11.0 %all_to_all.21 = bf16[4,24,768]{2,1,0:T(8,128)(2,1)S(1)} all-to-all(bf16[4,24,768]{2,1,0:T(8,128)(2,1)S(1)} %broadcast_in_dim.32), channel_id=1, replica_groups=mesh['yh'=4,'yl'=2,'x'=4,'g'=4,'q'=4] {'yh'}, dimensions={0} | all-to-all | bytes 294912 | tf_op jit(solution)/shard_map/all_to_all | solution.py:290
  156.0 16.3 %all_to_all.22 = bf16[8,96,768]{2,1,0:T(8,128)(2,1)S(1)} all-to-all(bf16[8,96,768]{2,1,0:T(8,128)(2,1)S(1)} %broadcast_in_dim.33), channel_id=1, replica_groups=mesh['yh'=4,'yl'=2,'x'=4,'g'=4,'q'=4] {'yl','x'}, dimensions={0} | all-to-all | bytes 2359296 | tf_op jit(solution)/shard_map/all_to_all | solution.py:290
  172.3 1.6 bitcast_convert_fusion
  (55 shorter events, 12.2 us)
Async XLA Ops:
  0.0 53.8 %copy-start = (bf16[1,3,64,768]{3,2,1,0:T(8,128)(2,1)S(1)}, bf16[1,3,64,768]{3,2,1,0:T(8,128)(2,1)}, u32[]{:S(2)}) copy-start(bf16[1,3,64,768]{3,2,1,0:T(8,128)(2,1)} %param.11) | copy-start | bytes 884740
  0.0 8.1 %collective-permute-start.1 = (bf16[768,768]{1,0:T(8,128)(2,1)}, bf16[768,768]{1,0:T(8,128)(2,1)S(1)}, u32[]{:S(2)}, u32[]{:S(2)}) collective-permute-start(bf16[768,768]{1,0:T(8,128)(2,1)} %bitcast.44), channel_id=1, source_target_pairs={{0,1},{1,0},{2,3},{3,2},{4,5},{5,4},{6,7},{7,6},{8,9},{9,8},{10,11... | collective-permute-start | bytes 3538952 | tf_op jit(solution)/shard_map/ppermute | solution.py:224
  2.1 32.0 %collective-permute-start = (bf16[768,768]{1,0:T(8,128)(2,1)}, bf16[768,768]{1,0:T(8,128)(2,1)S(1)}, u32[]{:S(2)}, u32[]{:S(2)}) collective-permute-start(bf16[768,768]{1,0:T(8,128)(2,1)} %bitcast.45), channel_id=1, source_target_pairs={{0,2},{1,3},{2,0},{3,1},{4,6},{5,7},{6,4},{7,5},{8,10},{9,11},{10,... | collective-permute-start | bytes 3538952 | tf_op jit(solution)/shard_map/ppermute | solution.py:224
  8.1 11.9 %collective-permute-start.2 = (f32[8,768]{1,0:T(8,128)S(1)}, f32[8,768]{1,0:T(8,128)S(1)}, u32[]{:S(2)}, u32[]{:S(2)}) collective-permute-start(f32[8,768]{1,0:T(8,128)S(1)} %maximum_maximum_fusion), channel_id=1, source_target_pairs={{0,1},{1,0},{2,3},{3,2},{4,5},{5,4},{6,7},{7,6},{8,9},{9,8},{10,11... | collective-permute-start | bytes 73736 | tf_op jit(solution)/shard_map/ppermute | solution.py:224
  10.2 23.7 %collective-permute-start.3 = (f32[8,768]{1,0:T(8,128)S(1)}, f32[8,768]{1,0:T(8,128)S(1)}, u32[]{:S(2)}, u32[]{:S(2)}) collective-permute-start(f32[8,768]{1,0:T(8,128)S(1)} %maximum_maximum_fusion), channel_id=1, source_target_pairs={{0,2},{1,3},{2,0},{3,1},{4,6},{5,7},{6,4},{7,5},{8,10},{9,11},{10,... | collective-permute-start | bytes 73736 | tf_op jit(solution)/shard_map/ppermute | solution.py:224
  12.4 21.6 %collective-permute-start.4 = (f32[8,768]{1,0:T(8,128)S(1)}, f32[8,768]{1,0:T(8,128)S(1)}, u32[]{:S(2)}, u32[]{:S(2)}) collective-permute-start(f32[8,768]{1,0:T(8,128)S(1)} %maximum_maximum_fusion), channel_id=1, source_target_pairs={{0,3},{1,2},{2,1},{3,0},{4,7},{5,6},{6,5},{7,4},{8,11},{9,10},{10,... | collective-permute-start | bytes 73736 | tf_op jit(solution)/shard_map/ppermute | solution.py:224
  17.7 1.3 copy-start.1
  34.0 4.7 %collective-permute-start.5 = (bf16[768,768]{1,0:T(8,128)(2,1)S(1)}, bf16[768,768]{1,0:T(8,128)(2,1)S(1)}, u32[]{:S(2)}, u32[]{:S(2)}) collective-permute-start(bf16[768,768]{1,0:T(8,128)(2,1)S(1)} %collective-permute-done.rest_0_), channel_id=1, source_target_pairs={{0,1},{1,0},{2,3},{3,2},{4,5},{5,4},{6,7},{7,6},{8,9},{9,8},{10,11... | collective-permute-start | bytes 3538952 | tf_op jit(solution)/shard_map/ppermute | solution.py:224
  42.0 6.6 %collective-permute-start.6 = (bf16[64,768]{1,0:T(8,128)(2,1)S(1)}, bf16[64,768]{1,0:T(8,128)(2,1)S(1)}, u32[]{:S(2)}, u32[]{:S(2)}) collective-permute-start(bf16[64,768]{1,0:T(8,128)(2,1)S(1)} %get-tuple-element.54), channel_id=1, source_target_pairs={{0,4},{1,5},{2,6},{16,20},{17,21},{18,22},{32,36},{33,37},{34,38},... | collective-permute-start | bytes 294920 | tf_op jit(solution)/shard_map/ppermute | solution.py:270
  48.6 15.4 %collective-permute-start.9 = (bf16[4,64,768]{2,1,0:T(8,128)(2,1)S(1)}, bf16[4,64,768]{2,1,0:T(8,128)(2,1)S(1)}, u32[]{:S(2)}, u32[]{:S(2)}) collective-permute-start(bf16[4,64,768]{2,1,0:T(8,128)(2,1)S(1)} %get-tuple-element.61), channel_id=1, source_target_pairs={{0,12},{1,13},{2,14},{16,28},{17,29},{18,30},{32,44},{33,45},{34,4... | collective-permute-start | bytes 1179656 | tf_op jit(solution)/shard_map/ppermute | solution.py:270
  51.8 0.7 collective-permute-start.7
  53.1 0.7 collective-permute-start.8
  65.9 0.7 collective-permute-start.10
  67.2 8.7 %collective-permute-start.14 = (bf16[64,768]{1,0:T(8,128)(2,1)S(1)}, bf16[64,768]{1,0:T(8,128)(2,1)S(1)}, u32[]{:S(2)}, u32[]{:S(2)}) collective-permute-start(bf16[64,768]{1,0:T(8,128)(2,1)S(1)} %get-tuple-element.76), channel_id=1, source_target_pairs={{8,4},{9,5},{10,6},{24,20},{25,21},{26,22},{40,36},{41,37},{42,38}... | collective-permute-start | bytes 294920 | tf_op jit(solution)/shard_map/ppermute | solution.py:270
  67.9 27.8 %collective-permute-start.16 = (bf16[4,64,768]{2,1,0:T(8,128)(2,1)S(1)}, bf16[4,64,768]{2,1,0:T(8,128)(2,1)S(1)}, u32[]{:S(2)}, u32[]{:S(2)}) collective-permute-start(bf16[4,64,768]{2,1,0:T(8,128)(2,1)S(1)} %get-tuple-element.87), channel_id=1, source_target_pairs={{12,0},{13,1},{14,2},{28,16},{29,17},{30,18},{44,32},{45,33},{46,3... | collective-permute-start | bytes 1179656 | tf_op jit(solution)/shard_map/ppermute | solution.py:270
  69.2 8.6 %collective-permute-start.13 = (bf16[64,768]{1,0:T(8,128)(2,1)S(1)}, bf16[64,768]{1,0:T(8,128)(2,1)S(1)}, u32[]{:S(2)}, u32[]{:S(2)}) collective-permute-start(bf16[64,768]{1,0:T(8,128)(2,1)S(1)} %get-tuple-element.94), channel_id=1, source_target_pairs={{0,3},{1,2},{2,1},{4,7},{5,6},{6,5},{8,11},{9,10},{10,9},{12,15},{... | collective-permute-start | bytes 294920 | tf_op jit(solution)/shard_map/ppermute | solution.py:275
  70.5 7.3 %collective-permute-start.12 = (bf16[64,768]{1,0:T(8,128)(2,1)S(1)}, bf16[64,768]{1,0:T(8,128)(2,1)S(1)}, u32[]{:S(2)}, u32[]{:S(2)}) collective-permute-start(bf16[64,768]{1,0:T(8,128)(2,1)S(1)} %get-tuple-element.95), channel_id=1, source_target_pairs={{0,2},{1,3},{2,0},{4,6},{5,7},{6,4},{8,10},{9,11},{10,8},{12,14},{... | collective-permute-start | bytes 294920 | tf_op jit(solution)/shard_map/ppermute | solution.py:275
  74.0 3.9 %collective-permute-start.11 = (bf16[64,768]{1,0:T(8,128)(2,1)S(1)}, bf16[64,768]{1,0:T(8,128)(2,1)S(1)}, u32[]{:S(2)}, u32[]{:S(2)}) collective-permute-start(bf16[64,768]{1,0:T(8,128)(2,1)S(1)} %get-tuple-element.96), channel_id=1, source_target_pairs={{0,1},{1,0},{2,3},{4,5},{5,4},{6,7},{8,9},{9,8},{10,11},{12,13},{1... | collective-permute-start | bytes 294920 | tf_op jit(solution)/shard_map/ppermute | solution.py:275
  76.6 19.2 %collective-permute-start.15 = (bf16[64,768]{1,0:T(8,128)(2,1)S(1)}, bf16[64,768]{1,0:T(8,128)(2,1)S(1)}, u32[]{:S(2)}, u32[]{:S(2)}) collective-permute-start(bf16[64,768]{1,0:T(8,128)(2,1)S(1)} %get-tuple-element.83), channel_id=1, source_target_pairs={{4,0},{5,1},{6,2},{20,16},{21,17},{22,18},{36,32},{37,33},{38,34},... | collective-permute-start | bytes 294920 | tf_op jit(solution)/shard_map/ppermute | solution.py:270
  98.3 8.3 %collective-permute-start.19 = (bf16[64,768]{1,0:T(8,128)(2,1)S(1)}, bf16[64,768]{1,0:T(8,128)(2,1)S(1)}, u32[]{:S(2)}, u32[]{:S(2)}) collective-permute-start(bf16[64,768]{1,0:T(8,128)(2,1)S(1)} %get-tuple-element.90), channel_id=1, source_target_pairs={{0,3},{1,2},{2,1},{4,7},{5,6},{6,5},{8,11},{9,10},{10,9},{12,15},{... | collective-permute-start | bytes 294920 | tf_op jit(solution)/shard_map/ppermute | solution.py:275
  99.6 7.6 %collective-permute-start.18 = (bf16[64,768]{1,0:T(8,128)(2,1)S(1)}, bf16[64,768]{1,0:T(8,128)(2,1)S(1)}, u32[]{:S(2)}, u32[]{:S(2)}) collective-permute-start(bf16[64,768]{1,0:T(8,128)(2,1)S(1)} %get-tuple-element.91), channel_id=1, source_target_pairs={{0,2},{1,3},{2,0},{4,6},{5,7},{6,4},{8,10},{9,11},{10,8},{12,14},{... | collective-permute-start | bytes 294920 | tf_op jit(solution)/shard_map/ppermute | solution.py:275
  104.6 3.2 %collective-permute-start.17 = (bf16[64,768]{1,0:T(8,128)(2,1)S(1)}, bf16[64,768]{1,0:T(8,128)(2,1)S(1)}, u32[]{:S(2)}, u32[]{:S(2)}) collective-permute-start(bf16[64,768]{1,0:T(8,128)(2,1)S(1)} %get-tuple-element.92), channel_id=1, source_target_pairs={{0,1},{1,0},{2,3},{4,5},{5,4},{6,7},{8,9},{9,8},{10,11},{12,13},{1... | collective-permute-start | bytes 294920 | tf_op jit(solution)/shard_map/ppermute | solution.py:275
